TPU v7x, 32 devices: a whole 2x2x4 slice. The times are simulated.
32 devices in a mesh: area: 4 (over x, core), local: 8 (over z, y).
Axes of the slice: x: 2, y: 2, z: 4, core: 2. Of those that a mesh axis runs over, the one named last changes fastest.
Arguments:
- rates_init: float32 [32, 16384], P(None, ('area', 'local')), may hold values from -1 to 1
- drive: float32 [32, 16384], P(None, ('area', 'local')), may hold values from -4 to 4
- within_w: bfloat16 [16384, 4096], P(('area', 'local')), may hold values from -0.125 to 0.125
- long_w: bfloat16 [128, 16, 128, 128], P(('area', 'local')), may hold values from -0.1875 to 0.1875
- columns: int32 [128, 16], P(('area', 'local')), may hold values from 0 to 127, as said below
- area_map: int32 [4], replicated, may hold values from 0 to 3, each once
- counts: int32 [4], replicated, may hold values from 9 to 32, as said below
Outputs:
- rates: float32 [32, 16384], P(None, ('area', 'local'))
Inputs may be any that keep to these rules, and one draw needn't show every extreme that they name: `columns`: each device's 4 * 16 entries name populations of any one logical area (entry // 32) at most 32 times, and exactly 32 times for some area. `counts`: some area has all 32 populations present, and some other area has exactly 9.
All inputs are finite; a program needn't handle non-finite values.
Results may differ from a plain program's by a relative error of at most 0.0031.
Values may be sent and summed in bfloat16 or wider, within the bound.
No kernel may reach another device: no remote copies, remote signals or barrier semaphores. Data moves between devices by JAX's collectives and lax.ppermute only.
A program may use at most 64 MiB of HBM per device.

v0:
```python
import jax
import jax.numpy as jnp
from jax import lax
from jax.sharding import PartitionSpec as P

STEPS = 2


def body(rates_init, drive, within_w, long_w, columns, area_map, counts):
    nareas = lax.axis_size("area")
    here_area = lax.axis_index("area")
    here_local = lax.axis_index("local")
    pop = long_w.shape[2]
    p_dev = long_w.shape[0]
    kblk = long_w.shape[1]
    cond = rates_init.shape[0]
    area_n = within_w.shape[1]
    p_area = area_n // pop
    many = p_dev * kblk
    area_ids = jnp.arange(nareas, dtype=jnp.int32)
    own_count = jnp.sum(jnp.where(area_ids == here_area, counts, 0))
    in_area = here_local * p_dev + jnp.arange(p_dev, dtype=jnp.int32)
    present = jnp.repeat((in_area < own_count).astype(jnp.float32), pop)[None, :]
    rates = rates_init * present
    flat_cols = columns.reshape(many)
    logical = flat_cols // p_area
    pop_idx = flat_cols % p_area
    target = jnp.sum(jnp.where(logical[:, None] == area_ids[None, :], area_map[None, :], 0), axis=1)
    global_pop = target * p_area + pop_idx
    for step in range(STEPS):
        rounded = rates.astype(jnp.bfloat16)
        whole_area = lax.all_gather(rounded, "local", axis=1, tiled=True)
        inner = lax.dot_general(
            whole_area, within_w, (((1,), (1,)), ((), ())), preferred_element_type=jnp.float32
        )
        piece = lax.all_gather(whole_area, "area", axis=1, tiled=True)
        width = piece.shape[1] // pop
        valid = (global_pop >= 0) & (global_pop < width)
        values = jnp.take(
            piece.reshape(cond, width, pop), jnp.clip(global_pop, 0, width - 1), axis=1
        )
        picked = jnp.where(valid[None, :, None], values, jnp.zeros_like(values))
        picked = picked.reshape(cond, p_dev, kblk, pop)
        outer = jnp.einsum("cpkj,pkij->cpi", picked, long_w, preferred_element_type=jnp.float32)
        outer = outer.reshape(cond, p_dev * pop)
        rates = jnp.tanh(inner + outer + drive) * present
    return rates


def solution(mesh):
    in_specs = (
        P(None, ("area", "local")),
        P(None, ("area", "local")),
        P(("area", "local"), None),
        P(("area", "local"), None, None, None),
        P(("area", "local"), None),
        P(),
        P(),
    )
    out_specs = P(None, ("area", "local"))
    return jax.shard_map(body, mesh=mesh, in_specs=in_specs, out_specs=out_specs, check_vma=False)
```

profile of v0, /device:TPU:0, one launch (start us, length us, event | category | flops | bytes accessed | tf_op | source)
XLA Modules:
  0.0 136.0 jit_solution(4989111884943554247)
XLA Ops:
  6.5 0.0 copy-start
  6.5 0.0 copy-start.3
  6.5 0.0 all-gather.3.cloned.1.call-start
  6.5 1.4 %fusion.8 = s32[]{:T(128)} fusion(s32[4]{0:T(128)} %param.15, s32[]{:T(128)S(6)} %axis_index.25), kind=kLoop, calls=%fused_computation.33 | loop fusion | flops 11 | bytes 24 | tf_op jit(solution)/shard_map/reduce_sum | solution.py:21
  8.0 0.6 compare_convert_fusion
  8.6 0.1 broadcast_bitcast_fusion
  8.7 0.8 multiply_convert_fusion
  9.6 34.5 %all_gather.12 = bf16[32,4096]{1,0:T(8,128)(2,1)} all-gather(bf16[32,512]{1,0:T(8,128)(2,1)S(1)} %multiply_convert_fusion), channel_id=1, replica_groups=mesh['area'=4,'local'=8] {'local'}, dimensions={1}, use_global_device_ids=true | all-gather | bytes 294912 | tf_op jit(solution)/shard_map/all_gather | solution.py:32
  44.1 0.0 copy-start.1
  44.1 0.0 all-gather.3.cloned.1.call-update
  44.1 0.0 all-gather.5.cloned.1.call-start
  44.2 0.8 reshape.84
  44.9 0.7 select_reduce_fusion
  45.7 16.2 %all-gather.3.cloned.1.call-done = bf16[32,16384]{1,0:T(8,128)(2,1)} async-done(((bf16[32,4096]{1,0:T(8,128)(2,1)}), bf16[32,16384]{1,0:T(8,128)(2,1)}) %all-gather.3.cloned.1.call-update) | async-done | bytes 1048592 | tf_op jit(solution)/shard_map/all_gather | solution.py:36
  61.9 1.4 %copy_bitcast_fusion.1 = bf16[32,128,128]{2,0,1:T(8,128)(2,1)S(1)} fusion(bf16[32,16384]{1,0:T(8,128)(2,1)} %all-gather.3.cloned.1.call-done), kind=kLoop, calls=%fused_computation.14 | loop fusion | bytes 2097152 | tf_op jit(solution)/shard_map/reshape | solution.py:40
  63.3 1.4 %gather_fusion = bf16[64,32,128]{2,1,0:T(8,128)(2,1)} fusion(bf16[32,128,128]{2,0,1:T(8,128)(2,1)S(1)} %copy_bitcast_fusion.1, s32[1024]{0:T(1024)S(1)} %pad_clamp_fusion), kind=kCustom, calls=%fused_computation.clone | custom fusion | bytes 1048832 | tf_op jit(solution)/shard_map/jit(_take)/gather | solution.py:39
  64.7 1.2 bitcast_select_fusion.1
  66.0 0.0 copy-done
  66.0 0.8 convolution_bitcast_fusion.1
  66.7 0.0 copy-done.3
  66.7 0.0 copy-done.1
  66.8 3.6 %fusion.6 = bf16[32,512]{1,0:T(8,128)(2,1)S(1)} fusion(f32[32,512]{1,0:T(8,128)S(1)} %copy-done.3, bf16[32,4096]{1,0:T(8,128)(2,1)S(1)} %copy-done.1, bf16[512,4096]{1,0:T(8,128)(2,1)} %param.11, f32[4,4,8,128]{3,2,1,0:T(8,128)S(1)} %convolution_bitcast_fusion.1, f32[512]{0:T(512)S(1)} %broadcast_bitcast_fusion), kind=kOutput, calls=%fused_computation.12 | convolution fusion | flops 134283264 | bytes 4622336 | tf_op jit(solution)/shard_map/dot_general | solution.py:33
  70.3 32.9 %all_gather.14 = bf16[32,4096]{1,0:T(8,128)(2,1)} all-gather(bf16[32,512]{1,0:T(8,128)(2,1)S(1)} %fusion.6), channel_id=1, replica_groups=mesh['area'=4,'local'=8] {'local'}, dimensions={1}, use_global_device_ids=true | all-gather | bytes 294912 | tf_op jit(solution)/shard_map/all_gather | solution.py:32
  103.2 0.0 copy-start.2
  103.2 0.0 all-gather.5.cloned.1.call-update
  103.2 16.9 %all-gather.5.cloned.1.call-done = bf16[32,16384]{1,0:T(8,128)(2,1)} async-done(((bf16[32,4096]{1,0:T(8,128)(2,1)}), bf16[32,16384]{1,0:T(8,128)(2,1)}) %all-gather.5.cloned.1.call-update) | async-done | bytes 1048592 | tf_op jit(solution)/shard_map/all_gather | solution.py:36
  120.1 1.4 %copy_bitcast_fusion = bf16[32,128,128]{2,0,1:T(8,128)(2,1)S(1)} fusion(bf16[32,16384]{1,0:T(8,128)(2,1)} %all-gather.5.cloned.1.call-done), kind=kLoop, calls=%fused_computation.13 | loop fusion | bytes 2097152 | tf_op jit(solution)/shard_map/reshape | solution.py:40
  121.5 1.4 %gather_fusion.1 = bf16[64,32,128]{2,1,0:T(8,128)(2,1)} fusion(bf16[32,128,128]{2,0,1:T(8,128)(2,1)S(1)} %copy_bitcast_fusion, s32[1024]{0:T(1024)S(1)} %pad_clamp_fusion), kind=kCustom, calls=%fused_computation.1.clone | custom fusion | bytes 1048832 | tf_op jit(solution)/shard_map/jit(_take)/gather | solution.py:39
  123.0 1.2 bitcast_select_fusion
  124.2 0.8 convolution_bitcast_fusion
  125.0 0.0 copy-done.2
  125.0 4.2 %fusion.5 = f32[32,512]{1,0:T(8,128)} fusion(f32[32,512]{1,0:T(8,128)S(1)} %copy-done.3, bf16[32,4096]{1,0:T(8,128)(2,1)S(1)} %copy-done.2, bf16[512,4096]{1,0:T(8,128)(2,1)} %param.11, f32[4,4,8,128]{3,2,1,0:T(8,128)S(1)} %convolution_bitcast_fusion, f32[512]{0:T(512)S(1)} %broadcast_bitcast_fusion), kind=kOutput, calls=%fused_computation.11 | convolution fusion | flops 134266880 | bytes 4655104 | tf_op jit(solution)/shard_map/dot_general | solution.py:33
  (4 shorter events, 0.0 us)
Async XLA Ops:
  6.5 59.4 %copy-start = (bf16[4,16,128,128]{3,2,1,0:T(8,128)(2,1)S(1)}, bf16[4,16,128,128]{3,2,1,0:T(8,128)(2,1)}, u32[]{:S(2)}) copy-start(bf16[4,16,128,128]{3,2,1,0:T(8,128)(2,1)} %param.12) | copy-start | bytes 6291460
  6.5 60.2 %copy-start.3 = (f32[32,512]{1,0:T(8,128)S(1)}, f32[32,512]{1,0:T(8,128)}, u32[]{:S(2)}) copy-start(f32[32,512]{1,0:T(8,128)} %param.10) | copy-start | bytes 196612
  6.5 55.3 %all-gather.3.cloned.1.call-start = ((), (), s32[]{:S(2)}) async-start(), calls=%async_computation | async-start | bytes 1310720 | tf_op jit(solution)/shard_map/all_gather | solution.py:36
  44.1 22.7 %copy-start.1 = (bf16[32,4096]{1,0:T(8,128)(2,1)S(1)}, bf16[32,4096]{1,0:T(8,128)(2,1)}, u32[]{:S(2)}) copy-start(bf16[32,4096]{1,0:T(8,128)(2,1)} %all_gather.12) | copy-start | bytes 786436
  44.1 76.0 %all-gather.5.cloned.1.call-start = ((), (), s32[]{:S(2)}) async-start(), calls=%async_computation.1 | async-start | bytes 1310720 | tf_op jit(solution)/shard_map/all_gather | solution.py:36
  103.2 21.8 %copy-start.2 = (bf16[32,4096]{1,0:T(8,128)(2,1)S(1)}, bf16[32,4096]{1,0:T(8,128)(2,1)}, u32[]{:S(2)}) copy-start(bf16[32,4096]{1,0:T(8,128)(2,1)} %all_gather.14) | copy-start | bytes 786436
Sparse Core Ops, SparseCore 0:
  44.2 17.6 all-gather.2
  103.3 16.7 all-gather.4
where the time goes:
time: 136 us
  blocking collectives  67.4 us (50%)
  waiting for transfers between devices  33.1 us (24%)
  between operations  13.5 us (10%)
  matrix products  9.3 us (7%)
  local copies, waits for them, and re-layouts  6.51 us (5%)
  other arithmetic  6.21 us (5%)
    all_gather x2, blocking collectives, body(): whole_area = lax.all_gather(rounded, 'local', axis=1, tiled=True)  67.4 us
    all_gather x2, waiting for transfers between devices, body(): piece = lax.all_gather(whole_area, 'area', axis=1, tiled=True)  33.1 us
    dot_general x2, matrix products, body(): lax.dot_general(whole_area, within_w, (((1,), (1,)), ((), ())), preferred...  7.78 us
    gather x2, local copies, waits for them, and re-layouts, body(): jnp.take(piece.reshape(cond, width, pop), jnp.clip(global_pop, 0, width -...  2.83 us
    reshape x2, local copies, waits for them, and re-layouts, body(): piece.reshape(cond, width, pop)  2.81 us
  transfers between devices with their start and end apart: 2, of which 2 were waited for; matrix products, arithmetic and copies ran while one was open for 1% of the time, Pallas kernels for 0%

commit v1 on v0

v1 whole, which is shorter than its diff:
```python
import functools

import jax
import jax.numpy as jnp
from jax import lax
from jax.experimental import pallas as pl
from jax.experimental.pallas import tpu as pltpu
from jax.sharding import PartitionSpec as P

STEPS = 2
CORES = 2
AXES = ("area", "local")
VMEM = pl.BlockSpec(memory_space=pltpu.VMEM)
SMEM = pl.BlockSpec(memory_space=pltpu.SMEM)


def call(kernel, out, operands, specs, flops, scratch=(), trans=0):
    moved = sum(x.size * x.dtype.itemsize for x in operands)
    return pl.pallas_call(
        kernel,
        out_shape=out,
        in_specs=specs,
        out_specs=VMEM,
        scratch_shapes=scratch,
        compiler_params=pltpu.CompilerParams(vmem_limit_bytes=40 * 2**20),
        cost_estimate=pl.CostEstimate(
            flops=flops, bytes_accessed=moved, transcendentals=trans
        ),
    )(*operands)


def present_of(s, p_dev, counts_ref):
    here = lax.axis_index("local") * p_dev + s
    return jnp.where(here < counts_ref[lax.axis_index("area")], 1.0, 0.0)


def first_kernel(p_dev, pop, counts_ref, x_ref, out_ref):
    for s in range(p_dev):
        at = slice(s * pop, (s + 1) * pop)
        out_ref[:, at] = (x_ref[:, at] * present_of(s, p_dev, counts_ref)).astype(
            out_ref.dtype
        )


def inner_kernel(lsub, other, cond, *refs):
    blocks_ref, w_ref = refs[0], refs[1]
    out_ref = refs[-1]
    here = lax.axis_index("local")
    width = blocks_ref.shape[1]
    total = refs[2][...] if len(refs) == 4 else None
    for d in range(blocks_ref.shape[0] // cond):
        l = here ^ (d * lsub + other)
        at = pl.ds(pl.multiple_of(l * width, width), width)
        part = lax.dot_general(
            blocks_ref[d * cond : (d + 1) * cond, :],
            w_ref[:, at],
            (((1,), (1,)), ((), ())),
            preferred_element_type=jnp.float32,
        )
        total = part if total is None else total + part
    out_ref[...] = total


def outer_kernel(shape, n_arrays, *refs):
    nx, l1, l2, p_dev, pop, kblk, cond = shape
    counts_ref, map_ref, columns_ref, w_ref, inner_ref, drive_ref = refs[:6]
    arrays = refs[6 : 6 + n_arrays]
    out_ref, table = refs[-2:]
    per = l1 * p_dev
    for n, a in enumerate(arrays):
        for d in range(l1):
            for s in range(p_dev):
                table[n * per + d * p_dev + s] = a[
                    d * cond : (d + 1) * cond, s * pop : (s + 1) * pop
                ]
    area = lax.axis_index("area")
    local = lax.axis_index("local")
    p_area = l1 * l2 * p_dev
    for p in range(p_dev):
        total = None
        for k in range(kblk):
            column = columns_ref[p, k]
            da = map_ref[column // p_area] ^ area
            inside = column % p_area
            dl = (inside // p_dev) ^ local
            n = ((da % CORES) * nx + da // CORES) * l2 + dl % l2
            at = n * per + (dl // l2) * p_dev + inside % p_dev
            part = lax.dot_general(
                table[at],
                w_ref[p, k],
                (((1,), (1,)), ((), ())),
                preferred_element_type=jnp.float32,
            )
            total = part if total is None else total + part
        here = slice(p * pop, (p + 1) * pop)
        rates = jnp.tanh(inner_ref[:, here] + total + drive_ref[:, here])
        out_ref[:, here] = (rates * present_of(p, p_dev, counts_ref)).astype(
            out_ref.dtype
        )


def body(rates_init, drive, within_w, long_w, columns, area_map, counts):
    areas, locs = lax.axis_size("area"), lax.axis_size("local")
    nx, l1 = areas // CORES, 4
    l2 = locs // l1
    p_dev, kblk, pop, _ = long_w.shape
    cond, width = rates_init.shape
    count = areas * locs

    def swap(x, dx=0, dc=0, d1=0, d2=0):
        by = (dx * CORES + dc) * locs + d1 * l2 + d2
        return lax.ppermute(x, AXES, [(i, i ^ by) for i in range(count)])

    mine = call(
        functools.partial(first_kernel, p_dev, pop),
        jax.ShapeDtypeStruct((cond, width), jnp.bfloat16),
        (counts, rates_init),
        [SMEM, VMEM],
        cond * width,
    )
    for step in range(STEPS):
        column = jnp.concatenate(
            [mine] + [swap(mine, d1=d) for d in range(1, l1)], axis=0
        )
        got = {
            (dx, d2): swap(column, dx=dx, d2=d2) if dx or d2 else column
            for dx in range(nx)
            for d2 in range(l2)
        }
        inner = None
        for d2 in range(l2):
            operands = [got[0, d2], within_w] + ([] if inner is None else [inner])
            inner = call(
                functools.partial(inner_kernel, l2, d2, cond),
                jax.ShapeDtypeStruct((cond, width), jnp.float32),
                operands,
                [VMEM] * len(operands),
                2 * cond * width * width * l1,
            )
        arrays = [got[dx, d2] for dx in range(nx) for d2 in range(l2)]
        arrays += [swap(x, dc=1) for x in arrays]
        last = step == STEPS - 1
        mine = call(
            functools.partial(
                outer_kernel, (nx, l1, l2, p_dev, pop, kblk, cond), len(arrays)
            ),
            jax.ShapeDtypeStruct((cond, width), jnp.float32 if last else jnp.bfloat16),
            [counts, area_map, columns, long_w, inner, drive] + arrays,
            [SMEM] * 3 + [VMEM] * (3 + len(arrays)),
            2 * cond * width * kblk * pop,
            scratch=[
                pltpu.VMEM((len(arrays) * l1 * p_dev, cond, pop), jnp.bfloat16)
            ],
            trans=cond * width,
        )
    return mine


def solution(mesh):
    in_specs = (
        P(None, AXES),
        P(None, AXES),
        P(AXES, None),
        P(AXES, None, None, None),
        P(AXES, None),
        P(),
        P(),
    )
    return jax.shard_map(
        body, mesh=mesh, in_specs=in_specs, out_specs=P(None, AXES), check_vma=False
    )
```

time: 136 us -> 48.7 us (0.36)
  blocking collectives: 67.4 us -> 0 us
  starting transfers between devices: 0.04 us -> 17.9 us
  waiting for transfers between devices: 33.1 us -> 16.4 us
  between operations: 13.5 us -> 0.15 us
  matrix products: 9.3 us -> 0 us
  Pallas kernels: 0 us -> 8.84 us
  other arithmetic: 6.21 us -> 0.02 us
    all_gather x2 -> x0, blocking collectives: 67.4 us -> none  [body(): whole_area = lax.all_gather(rounded, 'local', axis=1, tiled=True)]
    all_gather x2 -> x0, waiting for transfers between devices: 33.1 us -> none  [body(): piece = lax.all_gather(whole_area, 'area', axis=1, tiled=True)]
    ppermute x0 -> x20, starting transfers between devices: none -> 17.9 us  [swap(): return lax.ppermute(x, AXES, [(i, i ^ by) for i in range(count)])]
    ppermute x0 -> x20, waiting for transfers between devices: none -> 16.4 us  [swap(): return lax.ppermute(x, AXES, [(i, i ^ by) for i in range(count)])]
    dot_general x4 -> x0, matrix products: 9.3 us -> none  [the longest x2 7.78 us: body(): lax.dot_general(whole_area, within_w, (((1,), (1,)), ((), ())), preferred...]
    pallas_call x0 -> x7, Pallas kernels: none -> 8.84 us  [call(): pl.pallas_call(kernel, out_shape=out, in_specs=specs, out_specs=VMEM, scr...]
    unnamed x8 -> x16, local copies, waits for them, and re-layouts: 0.03 us -> 5.17 us
    reshape x3 -> x0, local copies, waits for them, and re-layouts: 3.57 us -> none  [the longest x2 2.81 us: body(): piece.reshape(cond, width, pop)]
  transfers between devices with their start and end apart: 2 -> 20, of which waited for: 2 -> 10; matrix products, arithmetic and copies ran while one was open for 1% -> 0% of each run, Pallas kernels for 0% -> 6%
where the time goes in v1:
time: 48.7 us; the launch traced here: 48.5 us
  starting transfers between devices  17.9 us (37%)
  waiting for transfers between devices  16.4 us (34%)
  Pallas kernels  8.84 us (18%)
  local copies, waits for them, and re-layouts  5.17 us (11%)
    ppermute x20, starting transfers between devices, swap(): return lax.ppermute(x, AXES, [(i, i ^ by) for i in range(count)])  17.9 us
    ppermute x20, waiting for transfers between devices, swap(): return lax.ppermute(x, AXES, [(i, i ^ by) for i in range(count)])  16.4 us
    pallas_call x7, Pallas kernels, call(): pl.pallas_call(kernel, out_shape=out, in_specs=specs, out_specs=VMEM, scr...  8.84 us
    unnamed x16, local copies, waits for them, and re-layouts  5.17 us
  transfers between devices with their start and end apart: 20, of which 10 were waited for; matrix products, arithmetic and copies ran while one was open for 0% of the time, Pallas kernels for 6%

profile of v1, /device:TPU:0, one launch (start us, length us, event | category | flops | bytes accessed | tf_op | source)
XLA Modules:
  0.0 48.5 jit_solution(15273219318020770762)
XLA Ops:
  0.0 0.0 copy-start.4
  0.0 0.8 %copy-done.4 = f32[32,512]{1,0:T(8,128)S(1)} copy-done((f32[32,512]{1,0:T(8,128)S(1)}, f32[32,512]{1,0:T(8,128)}, u32[]{:S(2)}) %copy-start.4) | copy-done | bytes 65560
  0.8 0.0 copy-start.6
  0.8 0.7 %copy-done.6 = s32[4]{0:T(128)S(1)} copy-done((s32[4]{0:T(128)S(1)}, s32[4]{0:T(128)}, u32[]{:S(2)}) %copy-start.6) | copy-done | bytes 40
  1.5 0.6 %shard_map.73 = bf16[32,512]{1,0:T(8,128)(2,1)S(1)} custom-call(s32[4]{0:T(128)S(1)} %copy-done.6, f32[32,512]{1,0:T(8,128)S(1)} %copy-done.4), custom_call_target="tpu_custom_call" | custom-call | flops 16384 | bytes 65552 | tf_op jit(solution)/shard_map/pallas_call | solution.py:19
  2.1 5.1 %collective-permute-start.2 = (bf16[32,512]{1,0:T(8,128)(2,1)S(1)}, bf16[32,512]{1,0:T(8,128)(2,1)S(1)}, u32[]{:S(2)}, u32[]{:S(2)}) collective-permute-start(bf16[32,512]{1,0:T(8,128)(2,1)S(1)} %shard_map.73), channel_id=1, source_target_pairs={{0,6},{1,7},{2,4},{3,5},{4,2},{5,3},{6,0},{7,1},{8,14},{9,15},{10,... | collective-permute-start | bytes 98312 | tf_op jit(solution)/shard_map/ppermute | solution.py:112
  7.2 0.0 collective-permute-start.1
  7.2 0.6 %collective-permute-start = (bf16[32,512]{1,0:T(8,128)(2,1)S(1)}, bf16[32,512]{1,0:T(8,128)(2,1)S(1)}, u32[]{:S(2)}, u32[]{:S(2)}) collective-permute-start(bf16[32,512]{1,0:T(8,128)(2,1)S(1)} %shard_map.73), channel_id=1, source_target_pairs={{0,2},{1,3},{2,0},{3,1},{4,6},{5,7},{6,4},{7,5},{8,10},{9,11},{10,... | collective-permute-start | bytes 98312 | tf_op jit(solution)/shard_map/ppermute | solution.py:112
  7.8 1.3 %collective-permute-done.2 = bf16[32,512]{1,0:T(8,128)(2,1)S(1)} collective-permute-done((bf16[32,512]{1,0:T(8,128)(2,1)S(1)}, bf16[32,512]{1,0:T(8,128)(2,1)S(1)}, u32[]{:S(2)}, u32[]{:S(2)}) %collective-permute-start.2) | collective-permute-done | bytes 32800 | tf_op jit(solution)/shard_map/ppermute | solution.py:112
  9.1 2.9 %collective-permute-done.1 = bf16[32,512]{1,0:T(8,128)(2,1)S(1)} collective-permute-done((bf16[32,512]{1,0:T(8,128)(2,1)S(1)}, bf16[32,512]{1,0:T(8,128)(2,1)S(1)}, u32[]{:S(2)}, u32[]{:S(2)}) %collective-permute-start.1) | collective-permute-done | bytes 32800 | tf_op jit(solution)/shard_map/ppermute | solution.py:112
  12.0 0.0 collective-permute-done
  12.0 0.0 copy-start.3
  12.0 0.0 copy-start.5
  12.0 0.0 copy-start.7
  12.0 2.5 %collective-permute-start.5 = (bf16[128,512]{1,0:T(8,128)(2,1)S(1)}, bf16[128,512]{1,0:T(8,128)(2,1)S(1)}, u32[]{:S(2)}, u32[]{:S(2)}) collective-permute-start(bf16[128,512]{1,0:T(8,128)(2,1)S(1)} %pad_maximum_fusion.refs_0_.refs_6_), channel_id=1, source_target_pairs={{0,17},{1,16},{2,19},{3,18},{4,21},{5,20},{6,23},{7,22},{8,25},{9,... | collective-permute-start | bytes 393224 | tf_op jit(solution)/shard_map/ppermute | solution.py:112
  14.5 0.5 %collective-permute-start.4 = (bf16[128,512]{1,0:T(8,128)(2,1)S(1)}, bf16[128,512]{1,0:T(8,128)(2,1)S(1)}, u32[]{:S(2)}, u32[]{:S(2)}) collective-permute-start(bf16[128,512]{1,0:T(8,128)(2,1)S(1)} %pad_maximum_fusion.refs_0_.refs_6_), channel_id=1, source_target_pairs={{0,16},{1,17},{2,18},{3,19},{4,20},{5,21},{6,22},{7,23},{8,24},{9,... | collective-permute-start | bytes 393224 | tf_op jit(solution)/shard_map/ppermute | solution.py:112
  15.1 0.5 %collective-permute-start.3 = (bf16[128,512]{1,0:T(8,128)(2,1)S(1)}, bf16[128,512]{1,0:T(8,128)(2,1)S(1)}, u32[]{:S(2)}, u32[]{:S(2)}) collective-permute-start(bf16[128,512]{1,0:T(8,128)(2,1)S(1)} %pad_maximum_fusion.refs_0_.refs_6_), channel_id=1, source_target_pairs={{0,1},{1,0},{2,3},{3,2},{4,5},{5,4},{6,7},{7,6},{8,9},{9,8},{10,11... | collective-permute-start | bytes 393224 | tf_op jit(solution)/shard_map/ppermute | solution.py:112
  15.6 0.0 collective-permute-start.6
  15.6 2.7 %collective-permute-done.5.refs_9_ = bf16[128,512]{1,0:T(8,128)(2,1)S(1)} collective-permute-done((bf16[128,512]{1,0:T(8,128)(2,1)S(1)}, bf16[128,512]{1,0:T(8,128)(2,1)S(1)}, u32[]{:S(2)}, u32[]{:S(2)}) %collective-permute-start.5) | collective-permute-done | bytes 131104 | tf_op jit(solution)/shard_map/ppermute | solution.py:112
  18.3 0.0 collective-permute-start.9
  18.3 1.3 %collective-permute-done.4.refs_8_ = bf16[128,512]{1,0:T(8,128)(2,1)S(1)} collective-permute-done((bf16[128,512]{1,0:T(8,128)(2,1)S(1)}, bf16[128,512]{1,0:T(8,128)(2,1)S(1)}, u32[]{:S(2)}, u32[]{:S(2)}) %collective-permute-start.4) | collective-permute-done | bytes 131104 | tf_op jit(solution)/shard_map/ppermute | solution.py:112
  19.7 0.0 collective-permute-start.8
  19.7 0.4 collective-permute-done.3.refs_0_.refs_7_
  20.0 0.1 collective-permute-start.7
  20.2 0.0 copy-start
  20.2 2.2 %copy-done = bf16[512,4096]{1,0:T(8,128)(2,1)S(1)} copy-done((bf16[512,4096]{1,0:T(8,128)(2,1)S(1)}, bf16[512,4096]{1,0:T(8,128)(2,1)}, u32[]{:S(2)}) %copy-start) | copy-done | bytes 4194328
  22.4 0.0 copy-start.1
  22.4 0.0 copy-start.2
  22.4 0.7 %shard_map.74.refs_2_ = f32[32,512]{1,0:T(8,128)S(1)} custom-call(bf16[128,512]{1,0:T(8,128)(2,1)S(1)} %pad_maximum_fusion.refs_0_.refs_6_, bf16[512,4096]{1,0:T(8,128)(2,1)S(1)} %copy-done), custom_call_target="tpu_custom_call" | custom-call | flops 67108864 | bytes 4325376 | tf_op jit(solution)/shard_map/pallas_call | solution.py:19
  23.1 1.5 %copy-done.1 = bf16[512,4096]{1,0:T(8,128)(2,1)S(1)} copy-done((bf16[512,4096]{1,0:T(8,128)(2,1)S(1)}, bf16[512,4096]{1,0:T(8,128)(2,1)}, u32[]{:S(2)}) %copy-start.1) | copy-done | bytes 4194328
  24.6 0.7 %shard_map.75.refs_4_ = f32[32,512]{1,0:T(8,128)S(1)} custom-call(bf16[128,512]{1,0:T(8,128)(2,1)S(1)} %collective-permute-done.3.refs_0_.refs_7_, bf16[512,4096]{1,0:T(8,128)(2,1)S(1)} %copy-done.1, f32[32,512]{1,0:T(8,128)S(1)} %shard_map.74.refs_2_), custom_call_target="tpu_custom_call" | custom-call | flops 67108864 | bytes 4390912 | tf_op jit(solution)/shard_map/pallas_call | solution.py:19
  25.3 0.0 collective-permute-done.6.refs_10_
  25.3 0.0 collective-permute-done.9.refs_13_
  25.3 0.0 collective-permute-done.8.refs_12_
  25.3 0.0 collective-permute-done.7.refs_11_
  25.3 0.0 copy-done.3
  25.3 0.0 copy-done.5
  25.4 0.0 copy-done.7
  25.4 0.0 copy-done.2
  25.4 2.4 %shard_map.76 = bf16[32,512]{1,0:T(8,128)(2,1)S(1)} custom-call(s32[4]{0:T(128)S(1)} %copy-done.6, s32[4]{0:T(128)S(1)} %copy-done.7, s32[4,16]{1,0:T(4,128)S(1)} %copy-done.5, bf16[4,16,128,128]{3,2,1,0:T(8,128)(2,1)S(1)} %copy-done.2, f32[32,512]{1,0:T(8,128)S(1)} %shard_map.75.refs_4_, f32[32,512]{1,0:T(8,128)S(1)} %copy-done.3, ...), custom_call_target="tpu_custom_call" | custom-call | flops 67108864 | bytes 3277088 | tf_op jit(solution)/shard_map/pallas_call | solution.py:19
  27.8 1.9 %collective-permute-start.12 = (bf16[32,512]{1,0:T(8,128)(2,1)S(1)}, bf16[32,512]{1,0:T(8,128)(2,1)S(1)}, u32[]{:S(2)}, u32[]{:S(2)}) collective-permute-start(bf16[32,512]{1,0:T(8,128)(2,1)S(1)} %shard_map.76), channel_id=1, source_target_pairs={{0,6},{1,7},{2,4},{3,5},{4,2},{5,3},{6,0},{7,1},{8,14},{9,15},{10,... | collective-permute-start | bytes 98312 | tf_op jit(solution)/shard_map/ppermute | solution.py:112
  29.7 0.3 collective-permute-start.11
  29.9 2.3 %collective-permute-start.10 = (bf16[32,512]{1,0:T(8,128)(2,1)S(1)}, bf16[32,512]{1,0:T(8,128)(2,1)S(1)}, u32[]{:S(2)}, u32[]{:S(2)}) collective-permute-start(bf16[32,512]{1,0:T(8,128)(2,1)S(1)} %shard_map.76), channel_id=1, source_target_pairs={{0,2},{1,3},{2,0},{3,1},{4,6},{5,7},{6,4},{7,5},{8,10},{9,11},{10,... | collective-permute-start | bytes 98312 | tf_op jit(solution)/shard_map/ppermute | solution.py:112
  32.2 1.5 %collective-permute-done.12 = bf16[32,512]{1,0:T(8,128)(2,1)S(1)} collective-permute-done((bf16[32,512]{1,0:T(8,128)(2,1)S(1)}, bf16[32,512]{1,0:T(8,128)(2,1)S(1)}, u32[]{:S(2)}, u32[]{:S(2)}) %collective-permute-start.12) | collective-permute-done | bytes 32800 | tf_op jit(solution)/shard_map/ppermute | solution.py:112
  33.7 1.1 %collective-permute-done.11 = bf16[32,512]{1,0:T(8,128)(2,1)S(1)} collective-permute-done((bf16[32,512]{1,0:T(8,128)(2,1)S(1)}, bf16[32,512]{1,0:T(8,128)(2,1)S(1)}, u32[]{:S(2)}, u32[]{:S(2)}) %collective-permute-start.11) | collective-permute-done | bytes 32800 | tf_op jit(solution)/shard_map/ppermute | solution.py:112
  34.8 0.0 collective-permute-done.10
  34.8 2.1 %collective-permute-start.15 = (bf16[128,512]{1,0:T(8,128)(2,1)S(1)}, bf16[128,512]{1,0:T(8,128)(2,1)S(1)}, u32[]{:S(2)}, u32[]{:S(2)}) collective-permute-start(bf16[128,512]{1,0:T(8,128)(2,1)S(1)} %pad_maximum_fusion.1.refs_0_.refs_6_), channel_id=1, source_target_pairs={{0,17},{1,16},{2,19},{3,18},{4,21},{5,20},{6,23},{7,22},{8,25},{9,... | collective-permute-start | bytes 393224 | tf_op jit(solution)/shard_map/ppermute | solution.py:112
  36.9 0.5 %collective-permute-start.14 = (bf16[128,512]{1,0:T(8,128)(2,1)S(1)}, bf16[128,512]{1,0:T(8,128)(2,1)S(1)}, u32[]{:S(2)}, u32[]{:S(2)}) collective-permute-start(bf16[128,512]{1,0:T(8,128)(2,1)S(1)} %pad_maximum_fusion.1.refs_0_.refs_6_), channel_id=1, source_target_pairs={{0,16},{1,17},{2,18},{3,19},{4,20},{5,21},{6,22},{7,23},{8,24},{9,... | collective-permute-start | bytes 393224 | tf_op jit(solution)/shard_map/ppermute | solution.py:112
  37.4 1.0 %collective-permute-start.13 = (bf16[128,512]{1,0:T(8,128)(2,1)S(1)}, bf16[128,512]{1,0:T(8,128)(2,1)S(1)}, u32[]{:S(2)}, u32[]{:S(2)}) collective-permute-start(bf16[128,512]{1,0:T(8,128)(2,1)S(1)} %pad_maximum_fusion.1.refs_0_.refs_6_), channel_id=1, source_target_pairs={{0,1},{1,0},{2,3},{3,2},{4,5},{5,4},{6,7},{7,6},{8,9},{9,8},{10,11... | collective-permute-start | bytes 393224 | tf_op jit(solution)/shard_map/ppermute | solution.py:112
  38.4 0.0 collective-permute-start.16
  38.4 3.7 %collective-permute-done.15.refs_9_ = bf16[128,512]{1,0:T(8,128)(2,1)S(1)} collective-permute-done((bf16[128,512]{1,0:T(8,128)(2,1)S(1)}, bf16[128,512]{1,0:T(8,128)(2,1)S(1)}, u32[]{:S(2)}, u32[]{:S(2)}) %collective-permute-start.15) | collective-permute-done | bytes 131104 | tf_op jit(solution)/shard_map/ppermute | solution.py:112
  42.1 0.0 collective-permute-start.19
  42.1 1.3 %collective-permute-done.14.refs_8_ = bf16[128,512]{1,0:T(8,128)(2,1)S(1)} collective-permute-done((bf16[128,512]{1,0:T(8,128)(2,1)S(1)}, bf16[128,512]{1,0:T(8,128)(2,1)S(1)}, u32[]{:S(2)}, u32[]{:S(2)}) %collective-permute-start.14) | collective-permute-done | bytes 131104 | tf_op jit(solution)/shard_map/ppermute | solution.py:112
  43.4 0.0 collective-permute-start.18
  43.4 0.1 collective-permute-done.13.refs_0_.refs_7_
  43.5 0.4 collective-permute-start.17
  43.9 0.7 %shard_map.77.refs_2_ = f32[32,512]{1,0:T(8,128)S(1)} custom-call(bf16[128,512]{1,0:T(8,128)(2,1)S(1)} %pad_maximum_fusion.1.refs_0_.refs_6_, bf16[512,4096]{1,0:T(8,128)(2,1)S(1)} %copy-done.1), custom_call_target="tpu_custom_call" | custom-call | flops 67108864 | bytes 4325376 | tf_op jit(solution)/shard_map/pallas_call | solution.py:19
  44.7 0.7 %shard_map.78.refs_4_ = f32[32,512]{1,0:T(8,128)S(1)} custom-call(bf16[128,512]{1,0:T(8,128)(2,1)S(1)} %collective-permute-done.13.refs_0_.refs_7_, bf16[512,4096]{1,0:T(8,128)(2,1)S(1)} %copy-done.1, f32[32,512]{1,0:T(8,128)S(1)} %shard_map.77.refs_2_), custom_call_target="tpu_custom_call" | custom-call | flops 67108864 | bytes 4390912 | tf_op jit(solution)/shard_map/pallas_call | solution.py:19
  45.4 0.0 collective-permute-done.16.refs_10_
  45.4 0.0 collective-permute-done.19.refs_13_
  45.4 0.0 collective-permute-done.18.refs_12_
  45.4 0.0 collective-permute-done.17.refs_11_
  45.5 3.0 %shard_map.79 = f32[32,512]{1,0:T(8,128)} custom-call(s32[4]{0:T(128)S(1)} %copy-done.6, s32[4]{0:T(128)S(1)} %copy-done.7, s32[4,16]{1,0:T(4,128)S(1)} %copy-done.5, bf16[4,16,128,128]{3,2,1,0:T(8,128)(2,1)S(1)} %copy-done.2, f32[32,512]{1,0:T(8,128)S(1)} %shard_map.78.refs_4_, f32[32,512]{1,0:T(8,128)S(1)} %copy-done.3, ...), custom_call_target="tpu_custom_call" | custom-call | flops 67108864 | bytes 3277088 | tf_op jit(solution)/shard_map/pallas_call | solution.py:19
  (2 shorter events, 0.0 us)
Async XLA Ops:
  0.0 0.8 %copy-start.4 = (f32[32,512]{1,0:T(8,128)S(1)}, f32[32,512]{1,0:T(8,128)}, u32[]{:S(2)}) copy-start(f32[32,512]{1,0:T(8,128)} %x_ref.1) | copy-start | bytes 196612
  0.8 0.7 %copy-start.6 = (s32[4]{0:T(128)S(1)}, s32[4]{0:T(128)}, u32[]{:S(2)}) copy-start(s32[4]{0:T(128)} %refs_0_.3) | copy-start | bytes 52
  2.1 7.0 %collective-permute-start.2 = (bf16[32,512]{1,0:T(8,128)(2,1)S(1)}, bf16[32,512]{1,0:T(8,128)(2,1)S(1)}, u32[]{:S(2)}, u32[]{:S(2)}) collective-permute-start(bf16[32,512]{1,0:T(8,128)(2,1)S(1)} %shard_map.73), channel_id=1, source_target_pairs={{0,6},{1,7},{2,4},{3,5},{4,2},{5,3},{6,0},{7,1},{8,14},{9,15},{10,... | collective-permute-start | bytes 98312 | tf_op jit(solution)/shard_map/ppermute | solution.py:112
  7.2 4.8 %collective-permute-start.1 = (bf16[32,512]{1,0:T(8,128)(2,1)S(1)}, bf16[32,512]{1,0:T(8,128)(2,1)S(1)}, u32[]{:S(2)}, u32[]{:S(2)}) collective-permute-start(bf16[32,512]{1,0:T(8,128)(2,1)S(1)} %shard_map.73), channel_id=1, source_target_pairs={{0,4},{1,5},{2,6},{3,7},{4,0},{5,1},{6,2},{7,3},{8,12},{9,13},{10,... | collective-permute-start | bytes 98312 | tf_op jit(solution)/shard_map/ppermute | solution.py:112
  7.2 4.8 %collective-permute-start = (bf16[32,512]{1,0:T(8,128)(2,1)S(1)}, bf16[32,512]{1,0:T(8,128)(2,1)S(1)}, u32[]{:S(2)}, u32[]{:S(2)}) collective-permute-start(bf16[32,512]{1,0:T(8,128)(2,1)S(1)} %shard_map.73), channel_id=1, source_target_pairs={{0,2},{1,3},{2,0},{3,1},{4,6},{5,7},{6,4},{7,5},{8,10},{9,11},{10,... | collective-permute-start | bytes 98312 | tf_op jit(solution)/shard_map/ppermute | solution.py:112
  12.0 13.3 %copy-start.3 = (f32[32,512]{1,0:T(8,128)S(1)}, f32[32,512]{1,0:T(8,128)}, u32[]{:S(2)}) copy-start(f32[32,512]{1,0:T(8,128)} %refs_5_.3) | copy-start | bytes 196612
  12.0 13.3 %copy-start.5 = (s32[4,16]{1,0:T(4,128)S(1)}, s32[4,16]{1,0:T(4,128)}, u32[]{:S(2)}) copy-start(s32[4,16]{1,0:T(4,128)} %refs_2_.3) | copy-start | bytes 772
  12.0 13.3 %copy-start.7 = (s32[4]{0:T(128)S(1)}, s32[4]{0:T(128)}, u32[]{:S(2)}) copy-start(s32[4]{0:T(128)} %refs_1_.11) | copy-start | bytes 52
  12.0 6.3 %collective-permute-start.5 = (bf16[128,512]{1,0:T(8,128)(2,1)S(1)}, bf16[128,512]{1,0:T(8,128)(2,1)S(1)}, u32[]{:S(2)}, u32[]{:S(2)}) collective-permute-start(bf16[128,512]{1,0:T(8,128)(2,1)S(1)} %pad_maximum_fusion.refs_0_.refs_6_), channel_id=1, source_target_pairs={{0,17},{1,16},{2,19},{3,18},{4,21},{5,20},{6,23},{7,22},{8,25},{9,... | collective-permute-start | bytes 393224 | tf_op jit(solution)/shard_map/ppermute | solution.py:112
  14.5 5.1 %collective-permute-start.4 = (bf16[128,512]{1,0:T(8,128)(2,1)S(1)}, bf16[128,512]{1,0:T(8,128)(2,1)S(1)}, u32[]{:S(2)}, u32[]{:S(2)}) collective-permute-start(bf16[128,512]{1,0:T(8,128)(2,1)S(1)} %pad_maximum_fusion.refs_0_.refs_6_), channel_id=1, source_target_pairs={{0,16},{1,17},{2,18},{3,19},{4,20},{5,21},{6,22},{7,23},{8,24},{9,... | collective-permute-start | bytes 393224 | tf_op jit(solution)/shard_map/ppermute | solution.py:112
  15.1 5.0 %collective-permute-start.3 = (bf16[128,512]{1,0:T(8,128)(2,1)S(1)}, bf16[128,512]{1,0:T(8,128)(2,1)S(1)}, u32[]{:S(2)}, u32[]{:S(2)}) collective-permute-start(bf16[128,512]{1,0:T(8,128)(2,1)S(1)} %pad_maximum_fusion.refs_0_.refs_6_), channel_id=1, source_target_pairs={{0,1},{1,0},{2,3},{3,2},{4,5},{5,4},{6,7},{7,6},{8,9},{9,8},{10,11... | collective-permute-start | bytes 393224 | tf_op jit(solution)/shard_map/ppermute | solution.py:112
  15.6 9.7 %collective-permute-start.6 = (bf16[128,512]{1,0:T(8,128)(2,1)S(1)}, bf16[128,512]{1,0:T(8,128)(2,1)S(1)}, u32[]{:S(2)}, u32[]{:S(2)}) collective-permute-start(bf16[128,512]{1,0:T(8,128)(2,1)S(1)} %pad_maximum_fusion.refs_0_.refs_6_), channel_id=1, source_target_pairs={{0,8},{1,9},{2,10},{3,11},{4,12},{5,13},{6,14},{7,15},{8,0},{9,1},... | collective-permute-start | bytes 393224 | tf_op jit(solution)/shard_map/ppermute | solution.py:112
  18.3 7.0 %collective-permute-start.9 = (bf16[128,512]{1,0:T(8,128)(2,1)S(1)}, bf16[128,512]{1,0:T(8,128)(2,1)S(1)}, u32[]{:S(2)}, u32[]{:S(2)}) collective-permute-start(bf16[128,512]{1,0:T(8,128)(2,1)S(1)} %collective-permute-done.5.refs_9_), channel_id=1, source_target_pairs={{0,8},{1,9},{2,10},{3,11},{4,12},{5,13},{6,14},{7,15},{8,0},{9,1},... | collective-permute-start | bytes 393224 | tf_op jit(solution)/shard_map/ppermute | solution.py:112
  19.7 5.6 %collective-permute-start.8 = (bf16[128,512]{1,0:T(8,128)(2,1)S(1)}, bf16[128,512]{1,0:T(8,128)(2,1)S(1)}, u32[]{:S(2)}, u32[]{:S(2)}) collective-permute-start(bf16[128,512]{1,0:T(8,128)(2,1)S(1)} %collective-permute-done.4.refs_8_), channel_id=1, source_target_pairs={{0,8},{1,9},{2,10},{3,11},{4,12},{5,13},{6,14},{7,15},{8,0},{9,1},... | collective-permute-start | bytes 393224 | tf_op jit(solution)/shard_map/ppermute | solution.py:112
  20.0 5.3 %collective-permute-start.7 = (bf16[128,512]{1,0:T(8,128)(2,1)S(1)}, bf16[128,512]{1,0:T(8,128)(2,1)S(1)}, u32[]{:S(2)}, u32[]{:S(2)}) collective-permute-start(bf16[128,512]{1,0:T(8,128)(2,1)S(1)} %collective-permute-done.3.refs_0_.refs_7_), channel_id=1, source_target_pairs={{0,8},{1,9},{2,10},{3,11},{4,12},{5,13},{6,14},{7,15},{8,0},{9,1},... | collective-permute-start | bytes 393224 | tf_op jit(solution)/shard_map/ppermute | solution.py:112
  20.2 2.2 %copy-start = (bf16[512,4096]{1,0:T(8,128)(2,1)S(1)}, bf16[512,4096]{1,0:T(8,128)(2,1)}, u32[]{:S(2)}) copy-start(bf16[512,4096]{1,0:T(8,128)(2,1)} %refs_1_.10) | copy-start | bytes 12582916
  22.4 2.2 %copy-start.1 = (bf16[512,4096]{1,0:T(8,128)(2,1)S(1)}, bf16[512,4096]{1,0:T(8,128)(2,1)}, u32[]{:S(2)}) copy-start(bf16[512,4096]{1,0:T(8,128)(2,1)} %refs_1_.10) | copy-start | bytes 12582916
  22.4 3.0 %copy-start.2 = (bf16[4,16,128,128]{3,2,1,0:T(8,128)(2,1)S(1)}, bf16[4,16,128,128]{3,2,1,0:T(8,128)(2,1)}, u32[]{:S(2)}) copy-start(bf16[4,16,128,128]{3,2,1,0:T(8,128)(2,1)} %refs_3_.3) | copy-start | bytes 6291460
  27.8 5.9 %collective-permute-start.12 = (bf16[32,512]{1,0:T(8,128)(2,1)S(1)}, bf16[32,512]{1,0:T(8,128)(2,1)S(1)}, u32[]{:S(2)}, u32[]{:S(2)}) collective-permute-start(bf16[32,512]{1,0:T(8,128)(2,1)S(1)} %shard_map.76), channel_id=1, source_target_pairs={{0,6},{1,7},{2,4},{3,5},{4,2},{5,3},{6,0},{7,1},{8,14},{9,15},{10,... | collective-permute-start | bytes 98312 | tf_op jit(solution)/shard_map/ppermute | solution.py:112
  29.7 5.2 %collective-permute-start.11 = (bf16[32,512]{1,0:T(8,128)(2,1)S(1)}, bf16[32,512]{1,0:T(8,128)(2,1)S(1)}, u32[]{:S(2)}, u32[]{:S(2)}) collective-permute-start(bf16[32,512]{1,0:T(8,128)(2,1)S(1)} %shard_map.76), channel_id=1, source_target_pairs={{0,4},{1,5},{2,6},{3,7},{4,0},{5,1},{6,2},{7,3},{8,12},{9,13},{10,... | collective-permute-start | bytes 98312 | tf_op jit(solution)/shard_map/ppermute | solution.py:112
  29.9 4.9 %collective-permute-start.10 = (bf16[32,512]{1,0:T(8,128)(2,1)S(1)}, bf16[32,512]{1,0:T(8,128)(2,1)S(1)}, u32[]{:S(2)}, u32[]{:S(2)}) collective-permute-start(bf16[32,512]{1,0:T(8,128)(2,1)S(1)} %shard_map.76), channel_id=1, source_target_pairs={{0,2},{1,3},{2,0},{3,1},{4,6},{5,7},{6,4},{7,5},{8,10},{9,11},{10,... | collective-permute-start | bytes 98312 | tf_op jit(solution)/shard_map/ppermute | solution.py:112
  34.8 7.3 %collective-permute-start.15 = (bf16[128,512]{1,0:T(8,128)(2,1)S(1)}, bf16[128,512]{1,0:T(8,128)(2,1)S(1)}, u32[]{:S(2)}, u32[]{:S(2)}) collective-permute-start(bf16[128,512]{1,0:T(8,128)(2,1)S(1)} %pad_maximum_fusion.1.refs_0_.refs_6_), channel_id=1, source_target_pairs={{0,17},{1,16},{2,19},{3,18},{4,21},{5,20},{6,23},{7,22},{8,25},{9,... | collective-permute-start | bytes 393224 | tf_op jit(solution)/shard_map/ppermute | solution.py:112
  36.9 6.5 %collective-permute-start.14 = (bf16[128,512]{1,0:T(8,128)(2,1)S(1)}, bf16[128,512]{1,0:T(8,128)(2,1)S(1)}, u32[]{:S(2)}, u32[]{:S(2)}) collective-permute-start(bf16[128,512]{1,0:T(8,128)(2,1)S(1)} %pad_maximum_fusion.1.refs_0_.refs_6_), channel_id=1, source_target_pairs={{0,16},{1,17},{2,18},{3,19},{4,20},{5,21},{6,22},{7,23},{8,24},{9,... | collective-permute-start | bytes 393224 | tf_op jit(solution)/shard_map/ppermute | solution.py:112
  37.4 6.1 %collective-permute-start.13 = (bf16[128,512]{1,0:T(8,128)(2,1)S(1)}, bf16[128,512]{1,0:T(8,128)(2,1)S(1)}, u32[]{:S(2)}, u32[]{:S(2)}) collective-permute-start(bf16[128,512]{1,0:T(8,128)(2,1)S(1)} %pad_maximum_fusion.1.refs_0_.refs_6_), channel_id=1, source_target_pairs={{0,1},{1,0},{2,3},{3,2},{4,5},{5,4},{6,7},{7,6},{8,9},{9,8},{10,11... | collective-permute-start | bytes 393224 | tf_op jit(solution)/shard_map/ppermute | solution.py:112
  38.4 7.0 %collective-permute-start.16 = (bf16[128,512]{1,0:T(8,128)(2,1)S(1)}, bf16[128,512]{1,0:T(8,128)(2,1)S(1)}, u32[]{:S(2)}, u32[]{:S(2)}) collective-permute-start(bf16[128,512]{1,0:T(8,128)(2,1)S(1)} %pad_maximum_fusion.1.refs_0_.refs_6_), channel_id=1, source_target_pairs={{0,8},{1,9},{2,10},{3,11},{4,12},{5,13},{6,14},{7,15},{8,0},{9,1},... | collective-permute-start | bytes 393224 | tf_op jit(solution)/shard_map/ppermute | solution.py:112
  42.1 3.3 %collective-permute-start.19 = (bf16[128,512]{1,0:T(8,128)(2,1)S(1)}, bf16[128,512]{1,0:T(8,128)(2,1)S(1)}, u32[]{:S(2)}, u32[]{:S(2)}) collective-permute-start(bf16[128,512]{1,0:T(8,128)(2,1)S(1)} %collective-permute-done.15.refs_9_), channel_id=1, source_target_pairs={{0,8},{1,9},{2,10},{3,11},{4,12},{5,13},{6,14},{7,15},{8,0},{9,1},... | collective-permute-start | bytes 393224 | tf_op jit(solution)/shard_map/ppermute | solution.py:112
  43.4 2.0 %collective-permute-start.18 = (bf16[128,512]{1,0:T(8,128)(2,1)S(1)}, bf16[128,512]{1,0:T(8,128)(2,1)S(1)}, u32[]{:S(2)}, u32[]{:S(2)}) collective-permute-start(bf16[128,512]{1,0:T(8,128)(2,1)S(1)} %collective-permute-done.14.refs_8_), channel_id=1, source_target_pairs={{0,8},{1,9},{2,10},{3,11},{4,12},{5,13},{6,14},{7,15},{8,0},{9,1},... | collective-permute-start | bytes 393224 | tf_op jit(solution)/shard_map/ppermute | solution.py:112
  43.5 1.9 %collective-permute-start.17 = (bf16[128,512]{1,0:T(8,128)(2,1)S(1)}, bf16[128,512]{1,0:T(8,128)(2,1)S(1)}, u32[]{:S(2)}, u32[]{:S(2)}) collective-permute-start(bf16[128,512]{1,0:T(8,128)(2,1)S(1)} %collective-permute-done.13.refs_0_.refs_7_), channel_id=1, source_target_pairs={{0,8},{1,9},{2,10},{3,11},{4,12},{5,13},{6,14},{7,15},{8,0},{9,1},... | collective-permute-start | bytes 393224 | tf_op jit(solution)/shard_map/ppermute | solution.py:112

commit v2 on v1

v2 whole, which is shorter than its diff:
```python
import functools

import jax
import jax.numpy as jnp
from jax import lax
from jax.experimental import pallas as pl
from jax.experimental.pallas import tpu as pltpu
from jax.sharding import PartitionSpec as P

STEPS = 2
CORES = 2
AXES = ("area", "local")
VMEM = pl.BlockSpec(memory_space=pltpu.VMEM)
HBM = pl.BlockSpec(memory_space=pltpu.HBM)
DIMS = (((1,), (1,)), ((), ()))


def call(kernel, out, operands, in_specs, flops, scratch=(), out_specs=VMEM, room=24):
    moved = sum(x.size * x.dtype.itemsize for x in operands)
    return pl.pallas_call(
        kernel,
        out_shape=out,
        in_specs=in_specs,
        out_specs=out_specs,
        scratch_shapes=scratch,
        compiler_params=pltpu.CompilerParams(vmem_limit_bytes=room * 2**20),
        cost_estimate=pl.CostEstimate(
            flops=flops, bytes_accessed=moved, transcendentals=0
        ),
    )(*operands)


def in_hbm(x):
    return pltpu.with_memory_space_constraint(x, pltpu.HBM)


def log2(n):
    bits = n.bit_length() - 1
    assert n == 1 << bits
    return bits


def fetch(sources, copies, sems):
    moves = []
    for a, b in zip(sources, copies):
        pieces = 4 if a.ndim > 1 and a.shape[0] >= 256 else 1
        rows = a.shape[0] // pieces
        for n in range(pieces):
            at = pl.ds(n * rows, rows)
            moves.append(
                pltpu.make_async_copy(a.at[at], b.at[at], sems.at[len(moves)])
            )
    for move in moves:
        move.start()
    return moves


def within_kernel(x_ref, w_ref, out_ref, again_ref, sems):
    moves = fetch([w_ref], [out_ref], sems)
    again_ref[...] = x_ref[...]
    for move in moves:
        move.wait()


def long_kernel(sizes, *refs):
    nx, l1, l2, p_dev = sizes
    x_ref, sources, copies = refs[0], refs[1:5], refs[5:7]
    slots_ref, again_ref, columns_ref, map_ref, sems = refs[7:]
    moves = fetch(sources, (columns_ref, map_ref, *copies), sems)
    again_ref[...] = x_ref[...]
    moves[0].wait()
    moves[1].wait()
    area, local = lax.axis_index("area"), lax.axis_index("local")
    inside_bits = log2(l1 * l2 * p_dev)
    columns = columns_ref[...]
    logical = columns >> inside_bits
    inside = columns & ((1 << inside_bits) - 1)
    target = jnp.zeros_like(columns)
    for a in range(nx * CORES):
        target = jnp.where(logical == a, map_ref[a], target)
    da = target ^ area
    dl = (inside >> log2(p_dev)) ^ local
    n = (da & (CORES - 1)) * nx + (da >> log2(CORES))
    n = n * l2 + (dl & (l2 - 1))
    n = n * l1 + (dl >> log2(l2))
    slots_ref[...] = n * p_dev + (inside & (p_dev - 1))
    for move in moves[2:]:
        move.wait()


def count_of(counts_ref):
    count = counts_ref[0]
    for a in range(1, counts_ref.shape[0]):
        count = jnp.where(lax.axis_index("area") == a, counts_ref[a], count)
    return count


def column_kernel(l2, p_dev, pop, counts_ref, *refs):
    out_ref = refs[-1]
    cond = refs[0].shape[0]
    count = count_of(counts_ref)
    for d, block in enumerate(refs[:-1]):
        first = (lax.axis_index("local") ^ (d * l2)) * p_dev
        for s in range(p_dev):
            at = slice(s * pop, (s + 1) * pop)
            x = block[:, at]
            out_ref[d * cond : (d + 1) * cond, at] = jnp.where(
                first + s < count, x, jnp.zeros_like(x)
            )


def inner_kernel(l2, other, cond, *refs):
    blocks_ref, w_ref = refs[:2]
    here = lax.axis_index("local")
    width = blocks_ref.shape[1]
    total = None
    if other:
        total, out_ref = refs[2][...], refs[3]
    else:
        out_ref, again_ref = refs[2:]
        again_ref[...] = blocks_ref[...]
    for d in range(blocks_ref.shape[0] // cond):
        l = here ^ (d * l2 + other)
        at = pl.ds(pl.multiple_of(l * width, width), width)
        part = lax.dot_general(
            blocks_ref[d * cond : (d + 1) * cond, :],
            w_ref[:, at],
            DIMS,
            preferred_element_type=jnp.float32,
        )
        total = part if total is None else total + part
    out_ref[...] = total


def outer_kernel(sizes, n_arrays, *refs):
    l1, p_dev, pop, kblk, cond = sizes
    counts_ref, slots_ref, w_ref, inner_ref, drive_ref = refs[:5]
    arrays = refs[5 : 5 + n_arrays]
    out_ref, table = refs[-2:]
    per = l1 * p_dev
    for n, a in enumerate(arrays):
        for d in range(l1):
            for s in range(p_dev):
                table[n * per + d * p_dev + s] = a[
                    d * cond : (d + 1) * cond, s * pop : (s + 1) * pop
                ]
    count = count_of(counts_ref)
    first = lax.axis_index("local") * p_dev
    for p in range(p_dev):
        picked = jnp.concatenate([table[slots_ref[p, k]] for k in range(kblk)], axis=1)
        weights = jnp.concatenate([w_ref[p, k] for k in range(kblk)], axis=1)
        outer = lax.dot_general(
            picked, weights, DIMS, preferred_element_type=jnp.float32
        )
        here = slice(p * pop, (p + 1) * pop)
        rates = jnp.tanh(inner_ref[:, here] + outer + drive_ref[:, here])
        present = jnp.where(first + p < count, 1.0, 0.0)
        out_ref[:, here] = (rates * present).astype(out_ref.dtype)


def body(rates_init, drive, within_w, long_w, columns, area_map, counts):
    areas, locs = lax.axis_size("area"), lax.axis_size("local")
    nx, l1 = areas // CORES, 4
    l2 = locs // l1
    p_dev, kblk, pop, _ = long_w.shape
    cond, width = rates_init.shape
    devices = areas * locs

    def swap(x, dx=0, dc=0, d1=0, d2=0):
        by = (dx * CORES + dc) * locs + d1 * l2 + d2
        return lax.ppermute(x, AXES, [(i, i ^ by) for i in range(devices)])

    mine = rates_init.astype(jnp.bfloat16)
    shape = jax.ShapeDtypeStruct
    within_w, kept = call(
        within_kernel,
        [pltpu.VMEM(x.shape, x.dtype) for x in (within_w, mine)],
        [mine, in_hbm(within_w)],
        [VMEM, HBM],
        0,
        scratch=[pltpu.SemaphoreType.DMA((4,))],
        out_specs=[VMEM] * 2,
    )
    for step in range(STEPS):
        blocks = [kept] + [swap(mine, d1=d) for d in range(1, l1)]
        column = call(
            functools.partial(column_kernel, l2, p_dev, pop),
            shape((l1 * cond, width), mine.dtype),
            [counts] + blocks,
            [VMEM] * (1 + l1),
            0,
        )
        got = {
            (dx, d2): swap(column, dx=dx, d2=d2) if dx or d2 else column
            for dx in range(nx)
            for d2 in range(l2)
        }
        if step == 0:
            long_w, drive, slots, got[0, 0] = call(
                functools.partial(long_kernel, (nx, l1, l2, p_dev)),
                [
                    pltpu.VMEM(x.shape, x.dtype)
                    for x in (long_w, drive, columns, column)
                ],
                [column] + [in_hbm(x) for x in (columns, area_map, long_w, drive)],
                [VMEM] + [HBM] * 4,
                0,
                scratch=[
                    pltpu.VMEM(columns.shape, columns.dtype),
                    pltpu.VMEM(area_map.shape, area_map.dtype),
                    pltpu.SemaphoreType.DMA((7,)),
                ],
                out_specs=[VMEM] * 4,
            )
        partial = shape((cond, width), jnp.float32)
        flops = 2 * cond * width * width * l1
        inner, got[0, 0] = call(
            functools.partial(inner_kernel, l2, 0, cond),
            [partial, shape(column.shape, column.dtype)],
            (got[0, 0], within_w),
            [VMEM] * 2,
            flops,
            out_specs=[VMEM] * 2,
        )
        for d2 in range(1, l2):
            inner = call(
                functools.partial(inner_kernel, l2, d2, cond),
                partial,
                (got[0, d2], within_w, inner),
                [VMEM] * 3,
                flops,
            )
        arrays = [got[dx, d2] for dx in range(nx) for d2 in range(l2)]
        arrays += [swap(x, dc=1) for x in arrays]
        last = step == STEPS - 1
        mine = kept = call(
            functools.partial(
                outer_kernel, (l1, p_dev, pop, kblk, cond), len(arrays)
            ),
            shape((cond, width), jnp.float32 if last else jnp.bfloat16),
            [counts, slots, long_w, inner, drive] + arrays,
            [VMEM] * (5 + len(arrays)),
            2 * cond * width * kblk * pop,
            scratch=[
                pltpu.VMEM((len(arrays) * l1 * p_dev, cond, pop), jnp.bfloat16)
            ],
        )
    return mine


def solution(mesh):
    in_specs = (
        P(None, AXES),
        P(None, AXES),
        P(AXES, None),
        P(AXES, None, None, None),
        P(AXES, None),
        P(),
        P(),
    )
    return jax.shard_map(
        body, mesh=mesh, in_specs=in_specs, out_specs=P(None, AXES), check_vma=False
    )
```

time: 48.7 us -> 40.1 us (0.82)
  local copies, waits for them, and re-layouts: 5.17 us -> 0.01 us
  waiting for transfers between devices: 16.4 us -> 11.5 us
  other arithmetic: 0.02 us -> 0.86 us
  Pallas kernels: 8.84 us -> 9.66 us
    unnamed x16 -> x2, local copies, waits for them, and re-layouts: 5.17 us -> 0.01 us
    ppermute x20, waiting for transfers between devices: 16.4 us -> 11.5 us  [swap(): return lax.ppermute(x, AXES, [(i, i ^ by) for i in range(devices)])]
    convert_element_type x0 -> x1, other arithmetic: none -> 0.86 us  [body(): mine = rates_init.astype(jnp.bfloat16)]
    pallas_call x7 -> x10, Pallas kernels: 8.84 us -> 9.66 us  [call(): pl.pallas_call(kernel, out_shape=out, in_specs=in_specs, out_specs=out_sp...]
  transfers between devices with their start and end apart: 20 -> 20, of which waited for: 10 -> 13; matrix products, arithmetic and copies ran while one was open for 0% -> 0% of each run, Pallas kernels for 6% -> 17%
where the time goes in v2:
time: 40.1 us; the launch traced here: 39.9 us
  starting transfers between devices  17.8 us (44%)
  waiting for transfers between devices  11.5 us (29%)
  Pallas kernels  9.66 us (24%)
  other arithmetic  0.86 us (2%)
    ppermute x20, starting transfers between devices, swap(): return lax.ppermute(x, AXES, [(i, i ^ by) for i in range(devices)])  17.8 us
    ppermute x20, waiting for transfers between devices, swap(): return lax.ppermute(x, AXES, [(i, i ^ by) for i in range(devices)])  11.5 us
    pallas_call x10, Pallas kernels, call(): pl.pallas_call(kernel, out_shape=out, in_specs=in_specs, out_specs=out_sp...  9.66 us
    convert_element_type x1, other arithmetic, body(): mine = rates_init.astype(jnp.bfloat16)  0.86 us
  transfers between devices with their start and end apart: 20, of which 13 were waited for; matrix products, arithmetic and copies ran while one was open for 0% of the time, Pallas kernels for 17%

profile of v2, /device:TPU:0, one launch (start us, length us, event | category | flops | bytes accessed | tf_op | source)
XLA Modules:
  0.0 39.9 jit_solution(1156429526809064471)
XLA Ops:
  0.0 0.0 copy-start
  0.0 0.9 %convert_element_type.3.x_ref = bf16[32,512]{1,0:T(8,128)(2,1)S(1)} convert(f32[32,512]{1,0:T(8,128)} %param.7) | non-fusion elementwise | flops 16384 | bytes 98304 | tf_op jit(solution)/shard_map/convert_element_type | solution.py:173
  0.9 5.0 %collective-permute-start.2 = (bf16[32,512]{1,0:T(8,128)(2,1)S(1)}, bf16[32,512]{1,0:T(8,128)(2,1)S(1)}, u32[]{:S(2)}, u32[]{:S(2)}) collective-permute-start(bf16[32,512]{1,0:T(8,128)(2,1)S(1)} %convert_element_type.3.x_ref), channel_id=1, source_target_pairs={{0,6},{1,7},{2,4},{3,5},{4,2},{5,3},{6,0},{7,1},{8,14},{9,15},{10,... | collective-permute-start | bytes 98312 | tf_op jit(solution)/shard_map/ppermute | solution.py:171
  5.9 0.0 collective-permute-start.1
  5.9 0.6 %collective-permute-start = (bf16[32,512]{1,0:T(8,128)(2,1)S(1)}, bf16[32,512]{1,0:T(8,128)(2,1)S(1)}, u32[]{:S(2)}, u32[]{:S(2)}) collective-permute-start(bf16[32,512]{1,0:T(8,128)(2,1)S(1)} %convert_element_type.3.x_ref), channel_id=1, source_target_pairs={{0,2},{1,3},{2,0},{3,1},{4,6},{5,7},{6,4},{7,5},{8,10},{9,11},{10,... | collective-permute-start | bytes 98312 | tf_op jit(solution)/shard_map/ppermute | solution.py:171
  6.5 2.2 %shard_map.73 = (bf16[512,4096]{1,0:T(8,128)(2,1)S(1)}, bf16[32,512]{1,0:T(8,128)(2,1)S(1)}) custom-call(bf16[32,512]{1,0:T(8,128)(2,1)S(1)} %convert_element_type.3.x_ref, bf16[512,4096]{1,0:T(8,128)(2,1)} %w_ref.1), custom_call_target="tpu_custom_call" | custom-call | bytes 4227072 | tf_op jit(solution)/shard_map/pallas_call | solution.py:20
  8.8 0.0 collective-permute-done.2.refs_3_
  8.8 2.0 %collective-permute-done.1.refs_2_ = bf16[32,512]{1,0:T(8,128)(2,1)S(1)} collective-permute-done((bf16[32,512]{1,0:T(8,128)(2,1)S(1)}, bf16[32,512]{1,0:T(8,128)(2,1)S(1)}, u32[]{:S(2)}, u32[]{:S(2)}) %collective-permute-start.1) | collective-permute-done | bytes 32800 | tf_op jit(solution)/shard_map/ppermute | solution.py:171
  10.7 0.0 collective-permute-done.refs_1_
  10.7 0.0 copy-done
  10.7 0.1 shard_map.74.refs_0_
  10.9 2.5 %collective-permute-start.5 = (bf16[128,512]{1,0:T(8,128)(2,1)S(1)}, bf16[128,512]{1,0:T(8,128)(2,1)S(1)}, u32[]{:S(2)}, u32[]{:S(2)}) collective-permute-start(bf16[128,512]{1,0:T(8,128)(2,1)S(1)} %shard_map.74.refs_0_), channel_id=1, source_target_pairs={{0,17},{1,16},{2,19},{3,18},{4,21},{5,20},{6,23},{7,22},{8,25},{9,... | collective-permute-start | bytes 393224 | tf_op jit(solution)/shard_map/ppermute | solution.py:171
  13.4 0.5 %collective-permute-start.4 = (bf16[128,512]{1,0:T(8,128)(2,1)S(1)}, bf16[128,512]{1,0:T(8,128)(2,1)S(1)}, u32[]{:S(2)}, u32[]{:S(2)}) collective-permute-start(bf16[128,512]{1,0:T(8,128)(2,1)S(1)} %shard_map.74.refs_0_), channel_id=1, source_target_pairs={{0,16},{1,17},{2,18},{3,19},{4,20},{5,21},{6,22},{7,23},{8,24},{9,... | collective-permute-start | bytes 393224 | tf_op jit(solution)/shard_map/ppermute | solution.py:171
  13.9 0.5 %collective-permute-start.3 = (bf16[128,512]{1,0:T(8,128)(2,1)S(1)}, bf16[128,512]{1,0:T(8,128)(2,1)S(1)}, u32[]{:S(2)}, u32[]{:S(2)}) collective-permute-start(bf16[128,512]{1,0:T(8,128)(2,1)S(1)} %shard_map.74.refs_0_), channel_id=1, source_target_pairs={{0,1},{1,0},{2,3},{3,2},{4,5},{5,4},{6,7},{7,6},{8,9},{9,8},{10,11... | collective-permute-start | bytes 393224 | tf_op jit(solution)/shard_map/ppermute | solution.py:171
  14.4 1.7 %shard_map.75 = (bf16[4,16,128,128]{3,2,1,0:T(8,128)(2,1)S(1)}, f32[32,512]{1,0:T(8,128)S(1)}, s32[4,16]{1,0:T(4,128)S(1)}, bf16[128,512]{1,0:T(8,128)(2,1)S(1)}) custom-call(bf16[128,512]{1,0:T(8,128)(2,1)S(1)} %shard_map.74.refs_0_, s32[4,16]{1,0:T(4,128)} %refs_1_.1, s32[4]{0:T(128)} %refs_2_.1, bf16[4,16,128,128]{3,2,1,0:T(8,128)(2,1)} %refs_3_.1, ...), custom_call_target="tpu_custom_call" | custom-call | bytes 2294032 | tf_op jit(solution)/shard_map/pallas_call | solution.py:20
  16.1 0.7 %shard_map.76 = (f32[32,512]{1,0:T(8,128)S(1)}, bf16[128,512]{1,0:T(8,128)(2,1)S(1)}) custom-call(bf16[128,512]{1,0:T(8,128)(2,1)S(1)} %get-tuple-element.19.refs_0_, bf16[512,4096]{1,0:T(8,128)(2,1)S(1)} %get-tuple-element.18.refs_1_), custom_call_target="tpu_custom_call" | custom-call | flops 67108864 | bytes 4325376 | tf_op jit(solution)/shard_map/pallas_call | solution.py:20
  16.8 0.0 collective-permute-start.6
  16.9 0.3 collective-permute-done.5.refs_8_
  17.2 0.2 collective-permute-start.9
  17.4 1.1 %collective-permute-done.4.refs_7_ = bf16[128,512]{1,0:T(8,128)(2,1)S(1)} collective-permute-done((bf16[128,512]{1,0:T(8,128)(2,1)S(1)}, bf16[128,512]{1,0:T(8,128)(2,1)S(1)}, u32[]{:S(2)}, u32[]{:S(2)}) %collective-permute-start.4) | collective-permute-done | bytes 131104 | tf_op jit(solution)/shard_map/ppermute | solution.py:171
  18.5 0.0 collective-permute-start.8
  18.5 0.4 collective-permute-done.3.refs_0_.refs_6_
  18.9 0.1 collective-permute-start.7
  19.0 0.7 %shard_map.77.refs_3_ = f32[32,512]{1,0:T(8,128)S(1)} custom-call(bf16[128,512]{1,0:T(8,128)(2,1)S(1)} %collective-permute-done.3.refs_0_.refs_6_, bf16[512,4096]{1,0:T(8,128)(2,1)S(1)} %get-tuple-element.18.refs_1_, f32[32,512]{1,0:T(8,128)S(1)} %get-tuple-element.20.refs_2_), custom_call_target="tpu_custom_call" | custom-call | flops 67108864 | bytes 4390912 | tf_op jit(solution)/shard_map/pallas_call | solution.py:20
  19.7 0.0 collective-permute-done.6.refs_9_
  19.8 0.0 collective-permute-done.9.refs_12_
  19.8 0.1 collective-permute-done.8.refs_11_
  19.9 0.4 collective-permute-done.7.refs_10_
  20.2 1.0 %shard_map.78.refs_0_ = bf16[32,512]{1,0:T(8,128)(2,1)S(1)} custom-call(s32[4]{0:T(128)S(1)} %copy-done, s32[4,16]{1,0:T(4,128)S(1)} %get-tuple-element.16.refs_1_, bf16[4,16,128,128]{3,2,1,0:T(8,128)(2,1)S(1)} %get-tuple-element.17.refs_2_, f32[32,512]{1,0:T(8,128)S(1)} %shard_map.77.refs_3_, f32[32,512]{1,0:T(8,128)S(1)} %get-tuple-element.21.refs_4_, ...), custom_call_target="tpu_custom_call" | custom-call | flops 67108864 | bytes 3277072 | tf_op jit(solution)/shard_map/pallas_call | solution.py:20
  21.2 2.3 %collective-permute-start.12 = (bf16[32,512]{1,0:T(8,128)(2,1)S(1)}, bf16[32,512]{1,0:T(8,128)(2,1)S(1)}, u32[]{:S(2)}, u32[]{:S(2)}) collective-permute-start(bf16[32,512]{1,0:T(8,128)(2,1)S(1)} %shard_map.78.refs_0_), channel_id=1, source_target_pairs={{0,6},{1,7},{2,4},{3,5},{4,2},{5,3},{6,0},{7,1},{8,14},{9,15},{10,... | collective-permute-start | bytes 98312 | tf_op jit(solution)/shard_map/ppermute | solution.py:171
  23.5 0.0 collective-permute-start.11
  23.5 2.2 %collective-permute-start.10 = (bf16[32,512]{1,0:T(8,128)(2,1)S(1)}, bf16[32,512]{1,0:T(8,128)(2,1)S(1)}, u32[]{:S(2)}, u32[]{:S(2)}) collective-permute-start(bf16[32,512]{1,0:T(8,128)(2,1)S(1)} %shard_map.78.refs_0_), channel_id=1, source_target_pairs={{0,2},{1,3},{2,0},{3,1},{4,6},{5,7},{6,4},{7,5},{8,10},{9,11},{10,... | collective-permute-start | bytes 98312 | tf_op jit(solution)/shard_map/ppermute | solution.py:171
  25.7 1.7 %collective-permute-done.12.refs_3_ = bf16[32,512]{1,0:T(8,128)(2,1)S(1)} collective-permute-done((bf16[32,512]{1,0:T(8,128)(2,1)S(1)}, bf16[32,512]{1,0:T(8,128)(2,1)S(1)}, u32[]{:S(2)}, u32[]{:S(2)}) %collective-permute-start.12) | collective-permute-done | bytes 32800 | tf_op jit(solution)/shard_map/ppermute | solution.py:171
  27.4 1.1 %collective-permute-done.11.refs_2_ = bf16[32,512]{1,0:T(8,128)(2,1)S(1)} collective-permute-done((bf16[32,512]{1,0:T(8,128)(2,1)S(1)}, bf16[32,512]{1,0:T(8,128)(2,1)S(1)}, u32[]{:S(2)}, u32[]{:S(2)}) %collective-permute-start.11) | collective-permute-done | bytes 32800 | tf_op jit(solution)/shard_map/ppermute | solution.py:171
  28.5 0.0 collective-permute-done.10.refs_1_
  28.5 0.1 shard_map.79.refs_0_
  28.6 2.1 %collective-permute-start.15 = (bf16[128,512]{1,0:T(8,128)(2,1)S(1)}, bf16[128,512]{1,0:T(8,128)(2,1)S(1)}, u32[]{:S(2)}, u32[]{:S(2)}) collective-permute-start(bf16[128,512]{1,0:T(8,128)(2,1)S(1)} %shard_map.79.refs_0_), channel_id=1, source_target_pairs={{0,17},{1,16},{2,19},{3,18},{4,21},{5,20},{6,23},{7,22},{8,25},{9,... | collective-permute-start | bytes 393224 | tf_op jit(solution)/shard_map/ppermute | solution.py:171
  30.8 0.5 %collective-permute-start.14 = (bf16[128,512]{1,0:T(8,128)(2,1)S(1)}, bf16[128,512]{1,0:T(8,128)(2,1)S(1)}, u32[]{:S(2)}, u32[]{:S(2)}) collective-permute-start(bf16[128,512]{1,0:T(8,128)(2,1)S(1)} %shard_map.79.refs_0_), channel_id=1, source_target_pairs={{0,16},{1,17},{2,18},{3,19},{4,20},{5,21},{6,22},{7,23},{8,24},{9,... | collective-permute-start | bytes 393224 | tf_op jit(solution)/shard_map/ppermute | solution.py:171
  31.3 0.9 %collective-permute-start.13 = (bf16[128,512]{1,0:T(8,128)(2,1)S(1)}, bf16[128,512]{1,0:T(8,128)(2,1)S(1)}, u32[]{:S(2)}, u32[]{:S(2)}) collective-permute-start(bf16[128,512]{1,0:T(8,128)(2,1)S(1)} %shard_map.79.refs_0_), channel_id=1, source_target_pairs={{0,1},{1,0},{2,3},{3,2},{4,5},{5,4},{6,7},{7,6},{8,9},{9,8},{10,11... | collective-permute-start | bytes 393224 | tf_op jit(solution)/shard_map/ppermute | solution.py:171
  32.2 0.7 %shard_map.80 = (f32[32,512]{1,0:T(8,128)S(1)}, bf16[128,512]{1,0:T(8,128)(2,1)S(1)}) custom-call(bf16[128,512]{1,0:T(8,128)(2,1)S(1)} %shard_map.79.refs_0_, bf16[512,4096]{1,0:T(8,128)(2,1)S(1)} %get-tuple-element.18.refs_1_), custom_call_target="tpu_custom_call" | custom-call | flops 67108864 | bytes 4325376 | tf_op jit(solution)/shard_map/pallas_call | solution.py:20
  32.9 0.0 collective-permute-start.16
  32.9 2.6 %collective-permute-done.15.refs_8_ = bf16[128,512]{1,0:T(8,128)(2,1)S(1)} collective-permute-done((bf16[128,512]{1,0:T(8,128)(2,1)S(1)}, bf16[128,512]{1,0:T(8,128)(2,1)S(1)}, u32[]{:S(2)}, u32[]{:S(2)}) %collective-permute-start.15) | collective-permute-done | bytes 131104 | tf_op jit(solution)/shard_map/ppermute | solution.py:171
  35.6 0.0 collective-permute-start.19
  35.6 1.0 %collective-permute-done.14.refs_7_ = bf16[128,512]{1,0:T(8,128)(2,1)S(1)} collective-permute-done((bf16[128,512]{1,0:T(8,128)(2,1)S(1)}, bf16[128,512]{1,0:T(8,128)(2,1)S(1)}, u32[]{:S(2)}, u32[]{:S(2)}) %collective-permute-start.14) | collective-permute-done | bytes 131104 | tf_op jit(solution)/shard_map/ppermute | solution.py:171
  36.6 0.0 collective-permute-start.18
  36.6 0.4 collective-permute-done.13.refs_0_.refs_6_
  36.9 0.1 collective-permute-start.17
  37.1 0.7 %shard_map.81.refs_3_ = f32[32,512]{1,0:T(8,128)S(1)} custom-call(bf16[128,512]{1,0:T(8,128)(2,1)S(1)} %collective-permute-done.13.refs_0_.refs_6_, bf16[512,4096]{1,0:T(8,128)(2,1)S(1)} %get-tuple-element.18.refs_1_, f32[32,512]{1,0:T(8,128)S(1)} %get-tuple-element.23.refs_2_), custom_call_target="tpu_custom_call" | custom-call | flops 67108864 | bytes 4390912 | tf_op jit(solution)/shard_map/pallas_call | solution.py:20
  37.8 0.0 collective-permute-done.16.refs_9_
  37.8 0.0 collective-permute-done.19.refs_12_
  37.8 0.1 collective-permute-done.18.refs_11_
  37.9 0.4 collective-permute-done.17.refs_10_
  38.3 1.6 %shard_map.82 = f32[32,512]{1,0:T(8,128)} custom-call(s32[4]{0:T(128)S(1)} %copy-done, s32[4,16]{1,0:T(4,128)S(1)} %get-tuple-element.16.refs_1_, bf16[4,16,128,128]{3,2,1,0:T(8,128)(2,1)S(1)} %get-tuple-element.17.refs_2_, f32[32,512]{1,0:T(8,128)S(1)} %shard_map.81.refs_3_, f32[32,512]{1,0:T(8,128)S(1)} %get-tuple-element.21.refs_4_, ...), custom_call_target="tpu_custom_call" | custom-call | flops 67108864 | bytes 3277072 | tf_op jit(solution)/shard_map/pallas_call | solution.py:20
Async XLA Ops:
  0.0 10.7 %copy-start = (s32[4]{0:T(128)S(1)}, s32[4]{0:T(128)}, u32[]{:S(2)}) copy-start(s32[4]{0:T(128)} %refs_0_.3) | copy-start | bytes 52
  0.9 7.9 %collective-permute-start.2 = (bf16[32,512]{1,0:T(8,128)(2,1)S(1)}, bf16[32,512]{1,0:T(8,128)(2,1)S(1)}, u32[]{:S(2)}, u32[]{:S(2)}) collective-permute-start(bf16[32,512]{1,0:T(8,128)(2,1)S(1)} %convert_element_type.3.x_ref), channel_id=1, source_target_pairs={{0,6},{1,7},{2,4},{3,5},{4,2},{5,3},{6,0},{7,1},{8,14},{9,15},{10,... | collective-permute-start | bytes 98312 | tf_op jit(solution)/shard_map/ppermute | solution.py:171
  5.9 4.8 %collective-permute-start.1 = (bf16[32,512]{1,0:T(8,128)(2,1)S(1)}, bf16[32,512]{1,0:T(8,128)(2,1)S(1)}, u32[]{:S(2)}, u32[]{:S(2)}) collective-permute-start(bf16[32,512]{1,0:T(8,128)(2,1)S(1)} %convert_element_type.3.x_ref), channel_id=1, source_target_pairs={{0,4},{1,5},{2,6},{3,7},{4,0},{5,1},{6,2},{7,3},{8,12},{9,13},{10,... | collective-permute-start | bytes 98312 | tf_op jit(solution)/shard_map/ppermute | solution.py:171
  5.9 4.8 %collective-permute-start = (bf16[32,512]{1,0:T(8,128)(2,1)S(1)}, bf16[32,512]{1,0:T(8,128)(2,1)S(1)}, u32[]{:S(2)}, u32[]{:S(2)}) collective-permute-start(bf16[32,512]{1,0:T(8,128)(2,1)S(1)} %convert_element_type.3.x_ref), channel_id=1, source_target_pairs={{0,2},{1,3},{2,0},{3,1},{4,6},{5,7},{6,4},{7,5},{8,10},{9,11},{10,... | collective-permute-start | bytes 98312 | tf_op jit(solution)/shard_map/ppermute | solution.py:171
  10.9 6.3 %collective-permute-start.5 = (bf16[128,512]{1,0:T(8,128)(2,1)S(1)}, bf16[128,512]{1,0:T(8,128)(2,1)S(1)}, u32[]{:S(2)}, u32[]{:S(2)}) collective-permute-start(bf16[128,512]{1,0:T(8,128)(2,1)S(1)} %shard_map.74.refs_0_), channel_id=1, source_target_pairs={{0,17},{1,16},{2,19},{3,18},{4,21},{5,20},{6,23},{7,22},{8,25},{9,... | collective-permute-start | bytes 393224 | tf_op jit(solution)/shard_map/ppermute | solution.py:171
  13.4 5.1 %collective-permute-start.4 = (bf16[128,512]{1,0:T(8,128)(2,1)S(1)}, bf16[128,512]{1,0:T(8,128)(2,1)S(1)}, u32[]{:S(2)}, u32[]{:S(2)}) collective-permute-start(bf16[128,512]{1,0:T(8,128)(2,1)S(1)} %shard_map.74.refs_0_), channel_id=1, source_target_pairs={{0,16},{1,17},{2,18},{3,19},{4,20},{5,21},{6,22},{7,23},{8,24},{9,... | collective-permute-start | bytes 393224 | tf_op jit(solution)/shard_map/ppermute | solution.py:171
  13.9 5.0 %collective-permute-start.3 = (bf16[128,512]{1,0:T(8,128)(2,1)S(1)}, bf16[128,512]{1,0:T(8,128)(2,1)S(1)}, u32[]{:S(2)}, u32[]{:S(2)}) collective-permute-start(bf16[128,512]{1,0:T(8,128)(2,1)S(1)} %shard_map.74.refs_0_), channel_id=1, source_target_pairs={{0,1},{1,0},{2,3},{3,2},{4,5},{5,4},{6,7},{7,6},{8,9},{9,8},{10,11... | collective-permute-start | bytes 393224 | tf_op jit(solution)/shard_map/ppermute | solution.py:171
  16.8 2.9 %collective-permute-start.6 = (bf16[128,512]{1,0:T(8,128)(2,1)S(1)}, bf16[128,512]{1,0:T(8,128)(2,1)S(1)}, u32[]{:S(2)}, u32[]{:S(2)}) collective-permute-start(bf16[128,512]{1,0:T(8,128)(2,1)S(1)} %get-tuple-element.22.refs_5_), channel_id=1, source_target_pairs={{0,8},{1,9},{2,10},{3,11},{4,12},{5,13},{6,14},{7,15},{8,0},{9,1},... | collective-permute-start | bytes 393224 | tf_op jit(solution)/shard_map/ppermute | solution.py:171
  17.2 2.6 %collective-permute-start.9 = (bf16[128,512]{1,0:T(8,128)(2,1)S(1)}, bf16[128,512]{1,0:T(8,128)(2,1)S(1)}, u32[]{:S(2)}, u32[]{:S(2)}) collective-permute-start(bf16[128,512]{1,0:T(8,128)(2,1)S(1)} %collective-permute-done.5.refs_8_), channel_id=1, source_target_pairs={{0,8},{1,9},{2,10},{3,11},{4,12},{5,13},{6,14},{7,15},{8,0},{9,1},... | collective-permute-start | bytes 393224 | tf_op jit(solution)/shard_map/ppermute | solution.py:171
  18.5 1.3 %collective-permute-start.8 = (bf16[128,512]{1,0:T(8,128)(2,1)S(1)}, bf16[128,512]{1,0:T(8,128)(2,1)S(1)}, u32[]{:S(2)}, u32[]{:S(2)}) collective-permute-start(bf16[128,512]{1,0:T(8,128)(2,1)S(1)} %collective-permute-done.4.refs_7_), channel_id=1, source_target_pairs={{0,8},{1,9},{2,10},{3,11},{4,12},{5,13},{6,14},{7,15},{8,0},{9,1},... | collective-permute-start | bytes 393224 | tf_op jit(solution)/shard_map/ppermute | solution.py:171
  18.9 1.3 %collective-permute-start.7 = (bf16[128,512]{1,0:T(8,128)(2,1)S(1)}, bf16[128,512]{1,0:T(8,128)(2,1)S(1)}, u32[]{:S(2)}, u32[]{:S(2)}) collective-permute-start(bf16[128,512]{1,0:T(8,128)(2,1)S(1)} %collective-permute-done.3.refs_0_.refs_6_), channel_id=1, source_target_pairs={{0,8},{1,9},{2,10},{3,11},{4,12},{5,13},{6,14},{7,15},{8,0},{9,1},... | collective-permute-start | bytes 393224 | tf_op jit(solution)/shard_map/ppermute | solution.py:171
  21.2 6.2 %collective-permute-start.12 = (bf16[32,512]{1,0:T(8,128)(2,1)S(1)}, bf16[32,512]{1,0:T(8,128)(2,1)S(1)}, u32[]{:S(2)}, u32[]{:S(2)}) collective-permute-start(bf16[32,512]{1,0:T(8,128)(2,1)S(1)} %shard_map.78.refs_0_), channel_id=1, source_target_pairs={{0,6},{1,7},{2,4},{3,5},{4,2},{5,3},{6,0},{7,1},{8,14},{9,15},{10,... | collective-permute-start | bytes 98312 | tf_op jit(solution)/shard_map/ppermute | solution.py:171
  23.5 5.0 %collective-permute-start.11 = (bf16[32,512]{1,0:T(8,128)(2,1)S(1)}, bf16[32,512]{1,0:T(8,128)(2,1)S(1)}, u32[]{:S(2)}, u32[]{:S(2)}) collective-permute-start(bf16[32,512]{1,0:T(8,128)(2,1)S(1)} %shard_map.78.refs_0_), channel_id=1, source_target_pairs={{0,4},{1,5},{2,6},{3,7},{4,0},{5,1},{6,2},{7,3},{8,12},{9,13},{10,... | collective-permute-start | bytes 98312 | tf_op jit(solution)/shard_map/ppermute | solution.py:171
  23.5 5.0 %collective-permute-start.10 = (bf16[32,512]{1,0:T(8,128)(2,1)S(1)}, bf16[32,512]{1,0:T(8,128)(2,1)S(1)}, u32[]{:S(2)}, u32[]{:S(2)}) collective-permute-start(bf16[32,512]{1,0:T(8,128)(2,1)S(1)} %shard_map.78.refs_0_), channel_id=1, source_target_pairs={{0,2},{1,3},{2,0},{3,1},{4,6},{5,7},{6,4},{7,5},{8,10},{9,11},{10,... | collective-permute-start | bytes 98312 | tf_op jit(solution)/shard_map/ppermute | solution.py:171
  28.6 6.9 %collective-permute-start.15 = (bf16[128,512]{1,0:T(8,128)(2,1)S(1)}, bf16[128,512]{1,0:T(8,128)(2,1)S(1)}, u32[]{:S(2)}, u32[]{:S(2)}) collective-permute-start(bf16[128,512]{1,0:T(8,128)(2,1)S(1)} %shard_map.79.refs_0_), channel_id=1, source_target_pairs={{0,17},{1,16},{2,19},{3,18},{4,21},{5,20},{6,23},{7,22},{8,25},{9,... | collective-permute-start | bytes 393224 | tf_op jit(solution)/shard_map/ppermute | solution.py:171
  30.8 5.8 %collective-permute-start.14 = (bf16[128,512]{1,0:T(8,128)(2,1)S(1)}, bf16[128,512]{1,0:T(8,128)(2,1)S(1)}, u32[]{:S(2)}, u32[]{:S(2)}) collective-permute-start(bf16[128,512]{1,0:T(8,128)(2,1)S(1)} %shard_map.79.refs_0_), channel_id=1, source_target_pairs={{0,16},{1,17},{2,18},{3,19},{4,20},{5,21},{6,22},{7,23},{8,24},{9,... | collective-permute-start | bytes 393224 | tf_op jit(solution)/shard_map/ppermute | solution.py:171
  31.3 5.6 %collective-permute-start.13 = (bf16[128,512]{1,0:T(8,128)(2,1)S(1)}, bf16[128,512]{1,0:T(8,128)(2,1)S(1)}, u32[]{:S(2)}, u32[]{:S(2)}) collective-permute-start(bf16[128,512]{1,0:T(8,128)(2,1)S(1)} %shard_map.79.refs_0_), channel_id=1, source_target_pairs={{0,1},{1,0},{2,3},{3,2},{4,5},{5,4},{6,7},{7,6},{8,9},{9,8},{10,11... | collective-permute-start | bytes 393224 | tf_op jit(solution)/shard_map/ppermute | solution.py:171
  32.9 4.9 %collective-permute-start.16 = (bf16[128,512]{1,0:T(8,128)(2,1)S(1)}, bf16[128,512]{1,0:T(8,128)(2,1)S(1)}, u32[]{:S(2)}, u32[]{:S(2)}) collective-permute-start(bf16[128,512]{1,0:T(8,128)(2,1)S(1)} %get-tuple-element.24.refs_5_), channel_id=1, source_target_pairs={{0,8},{1,9},{2,10},{3,11},{4,12},{5,13},{6,14},{7,15},{8,0},{9,1},... | collective-permute-start | bytes 393224 | tf_op jit(solution)/shard_map/ppermute | solution.py:171
  35.6 2.2 %collective-permute-start.19 = (bf16[128,512]{1,0:T(8,128)(2,1)S(1)}, bf16[128,512]{1,0:T(8,128)(2,1)S(1)}, u32[]{:S(2)}, u32[]{:S(2)}) collective-permute-start(bf16[128,512]{1,0:T(8,128)(2,1)S(1)} %collective-permute-done.15.refs_8_), channel_id=1, source_target_pairs={{0,8},{1,9},{2,10},{3,11},{4,12},{5,13},{6,14},{7,15},{8,0},{9,1},... | collective-permute-start | bytes 393224 | tf_op jit(solution)/shard_map/ppermute | solution.py:171
  36.6 1.3 %collective-permute-start.18 = (bf16[128,512]{1,0:T(8,128)(2,1)S(1)}, bf16[128,512]{1,0:T(8,128)(2,1)S(1)}, u32[]{:S(2)}, u32[]{:S(2)}) collective-permute-start(bf16[128,512]{1,0:T(8,128)(2,1)S(1)} %collective-permute-done.14.refs_7_), channel_id=1, source_target_pairs={{0,8},{1,9},{2,10},{3,11},{4,12},{5,13},{6,14},{7,15},{8,0},{9,1},... | collective-permute-start | bytes 393224 | tf_op jit(solution)/shard_map/ppermute | solution.py:171
  36.9 1.3 %collective-permute-start.17 = (bf16[128,512]{1,0:T(8,128)(2,1)S(1)}, bf16[128,512]{1,0:T(8,128)(2,1)S(1)}, u32[]{:S(2)}, u32[]{:S(2)}) collective-permute-start(bf16[128,512]{1,0:T(8,128)(2,1)S(1)} %collective-permute-done.13.refs_0_.refs_6_), channel_id=1, source_target_pairs={{0,8},{1,9},{2,10},{3,11},{4,12},{5,13},{6,14},{7,15},{8,0},{9,1},... | collective-permute-start | bytes 393224 | tf_op jit(solution)/shard_map/ppermute | solution.py:171

commit v3 on v2

--- a/solution.py
+++ b/solution.py
@@ -8,6 +8,7 @@
 from jax.sharding import PartitionSpec as P
 
 STEPS = 2
+PIECES = 4
 CORES = 2
 AXES = ("area", "local")
 VMEM = pl.BlockSpec(memory_space=pltpu.VMEM)
@@ -15,7 +16,7 @@
 DIMS = (((1,), (1,)), ((), ()))
 
 
-def call(kernel, out, operands, in_specs, flops, scratch=(), out_specs=VMEM, room=24):
+def call(kernel, out, operands, in_specs, flops, scratch=(), out_specs=VMEM, aliases={}):
     moved = sum(x.size * x.dtype.itemsize for x in operands)
     return pl.pallas_call(
         kernel,
@@ -23,7 +24,8 @@
         in_specs=in_specs,
         out_specs=out_specs,
         scratch_shapes=scratch,
-        compiler_params=pltpu.CompilerParams(vmem_limit_bytes=room * 2**20),
+        input_output_aliases=aliases,
+        compiler_params=pltpu.CompilerParams(vmem_limit_bytes=24 * 2**20),
         cost_estimate=pl.CostEstimate(
             flops=flops, bytes_accessed=moved, transcendentals=0
         ),
@@ -40,23 +42,20 @@
     return bits
 
 
-def fetch(sources, copies, sems):
-    moves = []
-    for a, b in zip(sources, copies):
-        pieces = 4 if a.ndim > 1 and a.shape[0] >= 256 else 1
-        rows = a.shape[0] // pieces
-        for n in range(pieces):
-            at = pl.ds(n * rows, rows)
-            moves.append(
-                pltpu.make_async_copy(a.at[at], b.at[at], sems.at[len(moves)])
-            )
+def pieces(a, b, n, sems):
+    rows = a.shape[0] // n
+    parts = [pl.ds(i * rows, rows) for i in range(n)]
+    moves = [
+        pltpu.make_async_copy(a.at[at], b.at[at], sems.at[i])
+        for i, at in enumerate(parts)
+    ]
     for move in moves:
         move.start()
     return moves
 
 
 def within_kernel(x_ref, w_ref, out_ref, again_ref, sems):
-    moves = fetch([w_ref], [out_ref], sems)
+    moves = pieces(w_ref, out_ref, PIECES, sems)
     again_ref[...] = x_ref[...]
     for move in moves:
         move.wait()
@@ -64,12 +63,21 @@
 
 def long_kernel(sizes, *refs):
     nx, l1, l2, p_dev = sizes
-    x_ref, sources, copies = refs[0], refs[1:5], refs[5:7]
-    slots_ref, again_ref, columns_ref, map_ref, sems = refs[7:]
-    moves = fetch(sources, (columns_ref, map_ref, *copies), sems)
+    x_ref, columns_hbm, map_hbm, w_hbm, drive_hbm = refs[:5]
+    w_ref, drive_ref, slots_ref, again_ref = refs[5:9]
+    columns_ref, map_ref, wide_ref, sems, w_sems = refs[9:]
+    moves = [
+        pltpu.make_async_copy(a, b, sems.at[n])
+        for n, (a, b) in enumerate(
+            ((columns_hbm, columns_ref), (map_hbm, map_ref), (drive_hbm, drive_ref))
+        )
+    ]
+    for move in moves:
+        move.start()
+    w_moves = pieces(w_hbm, wide_ref, p_dev, w_sems)
     again_ref[...] = x_ref[...]
-    moves[0].wait()
-    moves[1].wait()
+    for move in moves:
+        move.wait()
     area, local = lax.axis_index("area"), lax.axis_index("local")
     inside_bits = log2(l1 * l2 * p_dev)
     columns = columns_ref[...]
@@ -84,8 +92,10 @@
     n = n * l2 + (dl & (l2 - 1))
     n = n * l1 + (dl >> log2(l2))
     slots_ref[...] = n * p_dev + (inside & (p_dev - 1))
-    for move in moves[2:]:
+    for p, move in enumerate(w_moves):
         move.wait()
+        for k in range(w_ref.shape[1]):
+            w_ref[p, k] = wide_ref[p, k].T
 
 
 def count_of(counts_ref):
@@ -95,11 +105,11 @@
     return count
 
 
-def column_kernel(l2, p_dev, pop, counts_ref, *refs):
+def column_kernel(l2, p_dev, pop, order, counts_ref, *refs):
     out_ref = refs[-1]
     cond = refs[0].shape[0]
     count = count_of(counts_ref)
-    for d, block in enumerate(refs[:-1]):
+    for d, block in zip(order, refs[:-1]):
         first = (lax.axis_index("local") ^ (d * l2)) * p_dev
         for s in range(p_dev):
             at = slice(s * pop, (s + 1) * pop)
@@ -109,16 +119,29 @@
             )
 
 
+def lay(arrays, table, start, cond):
+    pop = table.shape[2]
+    at = start
+    for a in arrays:
+        for d in range(a.shape[0] // cond):
+            for s in range(a.shape[1] // pop):
+                table[at] = a[d * cond : (d + 1) * cond, s * pop : (s + 1) * pop]
+                at += 1
+
+
 def inner_kernel(l2, other, cond, *refs):
     blocks_ref, w_ref = refs[:2]
     here = lax.axis_index("local")
     width = blocks_ref.shape[1]
     total = None
-    if other:
+    if not other:
+        out_ref, again_ref = refs[2:]
+        again_ref[...] = blocks_ref[...]
+    elif len(refs) == 4:
         total, out_ref = refs[2][...], refs[3]
     else:
-        out_ref, again_ref = refs[2:]
-        again_ref[...] = blocks_ref[...]
+        total, arrays, out_ref, table = refs[2][...], refs[3:-2], refs[-2], refs[-1]
+        lay(arrays, table, 0, cond)
     for d in range(blocks_ref.shape[0] // cond):
         l = here ^ (d * l2 + other)
         at = pl.ds(pl.multiple_of(l * width, width), width)
@@ -132,26 +155,17 @@
     out_ref[...] = total
 
 
-def outer_kernel(sizes, n_arrays, *refs):
-    l1, p_dev, pop, kblk, cond = sizes
+def outer_kernel(start, *refs):
     counts_ref, slots_ref, w_ref, inner_ref, drive_ref = refs[:5]
-    arrays = refs[5 : 5 + n_arrays]
-    out_ref, table = refs[-2:]
-    per = l1 * p_dev
-    for n, a in enumerate(arrays):
-        for d in range(l1):
-            for s in range(p_dev):
-                table[n * per + d * p_dev + s] = a[
-                    d * cond : (d + 1) * cond, s * pop : (s + 1) * pop
-                ]
+    arrays, out_ref, table = refs[5:-3], refs[-2], refs[-1]
+    p_dev, kblk, pop, _ = w_ref.shape
+    lay(arrays, table, start, out_ref.shape[0])
     count = count_of(counts_ref)
     first = lax.axis_index("local") * p_dev
     for p in range(p_dev):
         picked = jnp.concatenate([table[slots_ref[p, k]] for k in range(kblk)], axis=1)
-        weights = jnp.concatenate([w_ref[p, k] for k in range(kblk)], axis=1)
-        outer = lax.dot_general(
-            picked, weights, DIMS, preferred_element_type=jnp.float32
-        )
+        weights = w_ref[p].reshape(kblk * pop, pop)
+        outer = jnp.dot(picked, weights, preferred_element_type=jnp.float32)
         here = slice(p * pop, (p + 1) * pop)
         rates = jnp.tanh(inner_ref[:, here] + outer + drive_ref[:, here])
         present = jnp.where(first + p < count, 1.0, 0.0)
@@ -178,15 +192,15 @@
         [mine, in_hbm(within_w)],
         [VMEM, HBM],
         0,
-        scratch=[pltpu.SemaphoreType.DMA((4,))],
+        scratch=[pltpu.SemaphoreType.DMA((PIECES,))],
         out_specs=[VMEM] * 2,
     )
     for step in range(STEPS):
-        blocks = [kept] + [swap(mine, d1=d) for d in range(1, l1)]
+        order = (1, 3, 2)
         column = call(
-            functools.partial(column_kernel, l2, p_dev, pop),
+            functools.partial(column_kernel, l2, p_dev, pop, (0,) + order),
             shape((l1 * cond, width), mine.dtype),
-            [counts] + blocks,
+            [counts, kept] + [swap(mine, d1=d) for d in order],
             [VMEM] * (1 + l1),
             0,
         )
@@ -208,7 +222,9 @@
                 scratch=[
                     pltpu.VMEM(columns.shape, columns.dtype),
                     pltpu.VMEM(area_map.shape, area_map.dtype),
-                    pltpu.SemaphoreType.DMA((7,)),
+                    pltpu.VMEM(long_w.shape, long_w.dtype),
+                    pltpu.SemaphoreType.DMA((3,)),
+                    pltpu.SemaphoreType.DMA((p_dev,)),
                 ],
                 out_specs=[VMEM] * 4,
             )
@@ -222,7 +238,7 @@
             flops,
             out_specs=[VMEM] * 2,
         )
-        for d2 in range(1, l2):
+        for d2 in range(1, l2 - 1):
             inner = call(
                 functools.partial(inner_kernel, l2, d2, cond),
                 partial,
@@ -232,19 +248,29 @@
             )
         arrays = [got[dx, d2] for dx in range(nx) for d2 in range(l2)]
         arrays += [swap(x, dc=1) for x in arrays]
+        early = len(arrays) // 2 + 1
+        per = l1 * p_dev
+        table = pltpu.VMEM((len(arrays) * per, cond, pop), mine.dtype)
+        inner, picks = call(
+            functools.partial(inner_kernel, l2, l2 - 1, cond),
+            [partial, table],
+            [got[0, l2 - 1], within_w, inner] + arrays[:early],
+            [VMEM] * (3 + early),
+            flops,
+            out_specs=[VMEM] * 2,
+        )
+        operands = [counts, slots, long_w, inner, drive] + arrays[early:] + [picks]
         last = step == STEPS - 1
-        mine = kept = call(
-            functools.partial(
-                outer_kernel, (l1, p_dev, pop, kblk, cond), len(arrays)
-            ),
-            shape((cond, width), jnp.float32 if last else jnp.bfloat16),
-            [counts, slots, long_w, inner, drive] + arrays,
-            [VMEM] * (5 + len(arrays)),
+        mine, _ = call(
+            functools.partial(outer_kernel, early * per),
+            [shape((cond, width), jnp.float32 if last else jnp.bfloat16), table],
+            operands,
+            [VMEM] * len(operands),
             2 * cond * width * kblk * pop,
-            scratch=[
-                pltpu.VMEM((len(arrays) * l1 * p_dev, cond, pop), jnp.bfloat16)
-            ],
-        )
+            out_specs=[VMEM] * 2,
+            aliases={len(operands) - 1: 1},
+        )
+        kept = mine
     return mine
 
 

time: 40.1 us -> 38.7 us (0.965)
  starting transfers between devices: 17.8 us -> 17.1 us
  waiting for transfers between devices: 11.5 us -> 10.9 us
    ppermute x20, starting transfers between devices: 17.8 us -> 17.1 us  [swap(): return lax.ppermute(x, AXES, [(i, i ^ by) for i in range(devices)])]
    ppermute x20, waiting for transfers between devices: 11.5 us -> 10.9 us  [swap(): return lax.ppermute(x, AXES, [(i, i ^ by) for i in range(devices)])]
  transfers between devices with their start and end apart: 20 -> 20, of which waited for: 13 -> 10; matrix products, arithmetic and copies ran while one was open for 0% -> 0% of each run, Pallas kernels for 17% -> 20%
where the time goes in v3:
time: 38.7 us; the launch traced here: 38.5 us
  starting transfers between devices  17.1 us (44%)
  waiting for transfers between devices  10.9 us (28%)
  Pallas kernels  9.54 us (25%)
  other arithmetic  0.86 us (2%)
    ppermute x20, starting transfers between devices, swap(): return lax.ppermute(x, AXES, [(i, i ^ by) for i in range(devices)])  17.1 us
    ppermute x20, waiting for transfers between devices, swap(): return lax.ppermute(x, AXES, [(i, i ^ by) for i in range(devices)])  10.9 us
    pallas_call x10, Pallas kernels, call(): pl.pallas_call(kernel, out_shape=out, in_specs=in_specs, out_specs=out_sp...  9.54 us
    convert_element_type x1, other arithmetic, body(): mine = rates_init.astype(jnp.bfloat16)  0.86 us
  transfers between devices with their start and end apart: 20, of which 10 were waited for; matrix products, arithmetic and copies ran while one was open for 0% of the time, Pallas kernels for 20%

profile of v3, /device:TPU:0, one launch (start us, length us, event | category | flops | bytes accessed | tf_op | source)
XLA Modules:
  0.0 38.5 jit_solution(5996066453616040206)
XLA Ops:
  0.0 0.0 copy-start
  0.0 0.9 %convert_element_type.3.x_ref = bf16[32,512]{1,0:T(8,128)(2,1)S(1)} convert(f32[32,512]{1,0:T(8,128)} %param.7) | non-fusion elementwise | flops 16384 | bytes 98304 | tf_op jit(solution)/shard_map/convert_element_type | solution.py:187
  0.9 4.0 %collective-permute-start.2 = (bf16[32,512]{1,0:T(8,128)(2,1)S(1)}, bf16[32,512]{1,0:T(8,128)(2,1)S(1)}, u32[]{:S(2)}, u32[]{:S(2)}) collective-permute-start(bf16[32,512]{1,0:T(8,128)(2,1)S(1)} %convert_element_type.3.x_ref), channel_id=1, source_target_pairs={{0,4},{1,5},{2,6},{3,7},{4,0},{5,1},{6,2},{7,3},{8,12},{9,13},{10,... | collective-permute-start | bytes 98312 | tf_op jit(solution)/shard_map/ppermute | solution.py:185
  4.9 1.3 %collective-permute-start.1 = (bf16[32,512]{1,0:T(8,128)(2,1)S(1)}, bf16[32,512]{1,0:T(8,128)(2,1)S(1)}, u32[]{:S(2)}, u32[]{:S(2)}) collective-permute-start(bf16[32,512]{1,0:T(8,128)(2,1)S(1)} %convert_element_type.3.x_ref), channel_id=1, source_target_pairs={{0,6},{1,7},{2,4},{3,5},{4,2},{5,3},{6,0},{7,1},{8,14},{9,15},{10,... | collective-permute-start | bytes 98312 | tf_op jit(solution)/shard_map/ppermute | solution.py:185
  6.2 0.2 collective-permute-start
  6.5 2.2 %shard_map.73 = (bf16[512,4096]{1,0:T(8,128)(2,1)S(1)}, bf16[32,512]{1,0:T(8,128)(2,1)S(1)}) custom-call(bf16[32,512]{1,0:T(8,128)(2,1)S(1)} %convert_element_type.3.x_ref, bf16[512,4096]{1,0:T(8,128)(2,1)} %w_ref.1), custom_call_target="tpu_custom_call" | custom-call | bytes 4227072 | tf_op jit(solution)/shard_map/pallas_call | solution.py:21
  8.7 0.0 collective-permute-done.2.refs_3_
  8.7 1.9 %collective-permute-done.1.refs_2_ = bf16[32,512]{1,0:T(8,128)(2,1)S(1)} collective-permute-done((bf16[32,512]{1,0:T(8,128)(2,1)S(1)}, bf16[32,512]{1,0:T(8,128)(2,1)S(1)}, u32[]{:S(2)}, u32[]{:S(2)}) %collective-permute-start.1) | collective-permute-done | bytes 32800 | tf_op jit(solution)/shard_map/ppermute | solution.py:185
  10.6 0.0 collective-permute-done.refs_1_
  10.6 0.0 copy-done
  10.6 0.1 shard_map.74.refs_0_
  10.8 2.5 %collective-permute-start.5 = (bf16[128,512]{1,0:T(8,128)(2,1)S(1)}, bf16[128,512]{1,0:T(8,128)(2,1)S(1)}, u32[]{:S(2)}, u32[]{:S(2)}) collective-permute-start(bf16[128,512]{1,0:T(8,128)(2,1)S(1)} %shard_map.74.refs_0_), channel_id=1, source_target_pairs={{0,17},{1,16},{2,19},{3,18},{4,21},{5,20},{6,23},{7,22},{8,25},{9,... | collective-permute-start | bytes 393224 | tf_op jit(solution)/shard_map/ppermute | solution.py:185
  13.3 0.5 %collective-permute-start.4 = (bf16[128,512]{1,0:T(8,128)(2,1)S(1)}, bf16[128,512]{1,0:T(8,128)(2,1)S(1)}, u32[]{:S(2)}, u32[]{:S(2)}) collective-permute-start(bf16[128,512]{1,0:T(8,128)(2,1)S(1)} %shard_map.74.refs_0_), channel_id=1, source_target_pairs={{0,16},{1,17},{2,18},{3,19},{4,20},{5,21},{6,22},{7,23},{8,24},{9,... | collective-permute-start | bytes 393224 | tf_op jit(solution)/shard_map/ppermute | solution.py:185
  13.8 0.5 %collective-permute-start.3 = (bf16[128,512]{1,0:T(8,128)(2,1)S(1)}, bf16[128,512]{1,0:T(8,128)(2,1)S(1)}, u32[]{:S(2)}, u32[]{:S(2)}) collective-permute-start(bf16[128,512]{1,0:T(8,128)(2,1)S(1)} %shard_map.74.refs_0_), channel_id=1, source_target_pairs={{0,1},{1,0},{2,3},{3,2},{4,5},{5,4},{6,7},{7,6},{8,9},{9,8},{10,11... | collective-permute-start | bytes 393224 | tf_op jit(solution)/shard_map/ppermute | solution.py:185
  14.3 2.3 %shard_map.75 = (bf16[4,16,128,128]{3,2,1,0:T(8,128)(2,1)S(1)}, f32[32,512]{1,0:T(8,128)S(1)}, s32[4,16]{1,0:T(4,128)S(1)}, bf16[128,512]{1,0:T(8,128)(2,1)S(1)}) custom-call(bf16[128,512]{1,0:T(8,128)(2,1)S(1)} %shard_map.74.refs_0_, s32[4,16]{1,0:T(4,128)} %refs_1_.1, s32[4]{0:T(128)} %refs_2_.1, bf16[4,16,128,128]{3,2,1,0:T(8,128)(2,1)} %refs_3_.1, ...), custom_call_target="tpu_custom_call" | custom-call | bytes 2294032 | tf_op jit(solution)/shard_map/pallas_call | solution.py:21
  16.6 0.7 %shard_map.76 = (f32[32,512]{1,0:T(8,128)S(1)}, bf16[128,512]{1,0:T(8,128)(2,1)S(1)}) custom-call(bf16[128,512]{1,0:T(8,128)(2,1)S(1)} %get-tuple-element.25.refs_0_, bf16[512,4096]{1,0:T(8,128)(2,1)S(1)} %get-tuple-element.24.refs_1_), custom_call_target="tpu_custom_call" | custom-call | flops 67108864 | bytes 4325376 | tf_op jit(solution)/shard_map/pallas_call | solution.py:21
  17.3 0.0 collective-permute-start.6
  17.4 0.0 collective-permute-done.5.refs_6_
  17.4 0.5 %collective-permute-start.9 = (bf16[128,512]{1,0:T(8,128)(2,1)S(1)}, bf16[128,512]{1,0:T(8,128)(2,1)S(1)}, u32[]{:S(2)}, u32[]{:S(2)}) collective-permute-start(bf16[128,512]{1,0:T(8,128)(2,1)S(1)} %collective-permute-done.5.refs_6_), channel_id=1, source_target_pairs={{0,8},{1,9},{2,10},{3,11},{4,12},{5,13},{6,14},{7,15},{8,0},{9,1},... | collective-permute-start | bytes 393224 | tf_op jit(solution)/shard_map/ppermute | solution.py:185
  17.9 0.5 %collective-permute-done.4.refs_5_ = bf16[128,512]{1,0:T(8,128)(2,1)S(1)} collective-permute-done((bf16[128,512]{1,0:T(8,128)(2,1)S(1)}, bf16[128,512]{1,0:T(8,128)(2,1)S(1)}, u32[]{:S(2)}, u32[]{:S(2)}) %collective-permute-start.4) | collective-permute-done | bytes 131104 | tf_op jit(solution)/shard_map/ppermute | solution.py:185
  18.4 0.0 collective-permute-start.8
  18.4 0.4 collective-permute-done.3.refs_0_.refs_4_
  18.8 0.1 collective-permute-start.7
  18.9 0.0 collective-permute-done.6.refs_7_
  18.9 0.8 %shard_map.77 = (f32[32,512]{1,0:T(8,128)S(1)}, bf16[128,32,128]{2,1,0:T(8,128)(2,1)S(1)}) custom-call(bf16[128,512]{1,0:T(8,128)(2,1)S(1)} %collective-permute-done.3.refs_0_.refs_4_, bf16[512,4096]{1,0:T(8,128)(2,1)S(1)} %get-tuple-element.24.refs_1_, f32[32,512]{1,0:T(8,128)S(1)} %get-tuple-element.26.refs_2_, ...), custom_call_target="tpu_custom_call" | custom-call | flops 67108864 | bytes 5046272 | tf_op jit(solution)/shard_map/pallas_call | solution.py:21
  19.7 0.0 collective-permute-done.9.refs_7_
  19.8 0.0 collective-permute-done.8.refs_6_
  19.8 0.4 collective-permute-done.7.refs_5_
  20.1 0.5 %shard_map.78 = (bf16[32,512]{1,0:T(8,128)(2,1)S(1)}, bf16[128,32,128]{2,1,0:T(8,128)(2,1)S(1)}) custom-call(s32[4]{0:T(128)S(1)} %copy-done, s32[4,16]{1,0:T(4,128)S(1)} %get-tuple-element.22.refs_1_, bf16[4,16,128,128]{3,2,1,0:T(8,128)(2,1)S(1)} %get-tuple-element.23.refs_2_, ...), custom_call_target="tpu_custom_call", output_to_operand_aliasing={{1}: (8, {})} | custom-call | flops 67108864 | bytes 3670288 | tf_op jit(solution)/shard_map/pallas_call | solution.py:21
  20.7 1.4 %collective-permute-start.12 = (bf16[32,512]{1,0:T(8,128)(2,1)S(1)}, bf16[32,512]{1,0:T(8,128)(2,1)S(1)}, u32[]{:S(2)}, u32[]{:S(2)}) collective-permute-start(bf16[32,512]{1,0:T(8,128)(2,1)S(1)} %get-tuple-element.31.refs_0_), channel_id=1, source_target_pairs={{0,4},{1,5},{2,6},{3,7},{4,0},{5,1},{6,2},{7,3},{8,12},{9,13},{10,... | collective-permute-start | bytes 98312 | tf_op jit(solution)/shard_map/ppermute | solution.py:185
  22.1 1.4 %collective-permute-start.11 = (bf16[32,512]{1,0:T(8,128)(2,1)S(1)}, bf16[32,512]{1,0:T(8,128)(2,1)S(1)}, u32[]{:S(2)}, u32[]{:S(2)}) collective-permute-start(bf16[32,512]{1,0:T(8,128)(2,1)S(1)} %get-tuple-element.31.refs_0_), channel_id=1, source_target_pairs={{0,6},{1,7},{2,4},{3,5},{4,2},{5,3},{6,0},{7,1},{8,14},{9,15},{10,... | collective-permute-start | bytes 98312 | tf_op jit(solution)/shard_map/ppermute | solution.py:185
  23.4 0.8 %collective-permute-start.10 = (bf16[32,512]{1,0:T(8,128)(2,1)S(1)}, bf16[32,512]{1,0:T(8,128)(2,1)S(1)}, u32[]{:S(2)}, u32[]{:S(2)}) collective-permute-start(bf16[32,512]{1,0:T(8,128)(2,1)S(1)} %get-tuple-element.31.refs_0_), channel_id=1, source_target_pairs={{0,2},{1,3},{2,0},{3,1},{4,6},{5,7},{6,4},{7,5},{8,10},{9,11},{10,... | collective-permute-start | bytes 98312 | tf_op jit(solution)/shard_map/ppermute | solution.py:185
  24.2 1.5 %collective-permute-done.12.refs_3_ = bf16[32,512]{1,0:T(8,128)(2,1)S(1)} collective-permute-done((bf16[32,512]{1,0:T(8,128)(2,1)S(1)}, bf16[32,512]{1,0:T(8,128)(2,1)S(1)}, u32[]{:S(2)}, u32[]{:S(2)}) %collective-permute-start.12) | collective-permute-done | bytes 32800 | tf_op jit(solution)/shard_map/ppermute | solution.py:185
  25.7 2.0 %collective-permute-done.11.refs_2_ = bf16[32,512]{1,0:T(8,128)(2,1)S(1)} collective-permute-done((bf16[32,512]{1,0:T(8,128)(2,1)S(1)}, bf16[32,512]{1,0:T(8,128)(2,1)S(1)}, u32[]{:S(2)}, u32[]{:S(2)}) %collective-permute-start.11) | collective-permute-done | bytes 32800 | tf_op jit(solution)/shard_map/ppermute | solution.py:185
  27.8 0.0 collective-permute-done.10.refs_1_
  27.8 0.1 shard_map.79.refs_0_
  27.9 2.3 %collective-permute-start.15 = (bf16[128,512]{1,0:T(8,128)(2,1)S(1)}, bf16[128,512]{1,0:T(8,128)(2,1)S(1)}, u32[]{:S(2)}, u32[]{:S(2)}) collective-permute-start(bf16[128,512]{1,0:T(8,128)(2,1)S(1)} %shard_map.79.refs_0_), channel_id=1, source_target_pairs={{0,17},{1,16},{2,19},{3,18},{4,21},{5,20},{6,23},{7,22},{8,25},{9,... | collective-permute-start | bytes 393224 | tf_op jit(solution)/shard_map/ppermute | solution.py:185
  30.2 0.5 %collective-permute-start.14 = (bf16[128,512]{1,0:T(8,128)(2,1)S(1)}, bf16[128,512]{1,0:T(8,128)(2,1)S(1)}, u32[]{:S(2)}, u32[]{:S(2)}) collective-permute-start(bf16[128,512]{1,0:T(8,128)(2,1)S(1)} %shard_map.79.refs_0_), channel_id=1, source_target_pairs={{0,16},{1,17},{2,18},{3,19},{4,20},{5,21},{6,22},{7,23},{8,24},{9,... | collective-permute-start | bytes 393224 | tf_op jit(solution)/shard_map/ppermute | solution.py:185
  30.7 0.8 %collective-permute-start.13 = (bf16[128,512]{1,0:T(8,128)(2,1)S(1)}, bf16[128,512]{1,0:T(8,128)(2,1)S(1)}, u32[]{:S(2)}, u32[]{:S(2)}) collective-permute-start(bf16[128,512]{1,0:T(8,128)(2,1)S(1)} %shard_map.79.refs_0_), channel_id=1, source_target_pairs={{0,1},{1,0},{2,3},{3,2},{4,5},{5,4},{6,7},{7,6},{8,9},{9,8},{10,11... | collective-permute-start | bytes 393224 | tf_op jit(solution)/shard_map/ppermute | solution.py:185
  31.5 0.7 %shard_map.80 = (f32[32,512]{1,0:T(8,128)S(1)}, bf16[128,512]{1,0:T(8,128)(2,1)S(1)}) custom-call(bf16[128,512]{1,0:T(8,128)(2,1)S(1)} %shard_map.79.refs_0_, bf16[512,4096]{1,0:T(8,128)(2,1)S(1)} %get-tuple-element.24.refs_1_), custom_call_target="tpu_custom_call" | custom-call | flops 67108864 | bytes 4325376 | tf_op jit(solution)/shard_map/pallas_call | solution.py:21
  32.2 0.0 collective-permute-start.16
  32.2 2.4 %collective-permute-done.15.refs_6_ = bf16[128,512]{1,0:T(8,128)(2,1)S(1)} collective-permute-done((bf16[128,512]{1,0:T(8,128)(2,1)S(1)}, bf16[128,512]{1,0:T(8,128)(2,1)S(1)}, u32[]{:S(2)}, u32[]{:S(2)}) %collective-permute-start.15) | collective-permute-done | bytes 131104 | tf_op jit(solution)/shard_map/ppermute | solution.py:185
  34.6 0.0 collective-permute-start.19
  34.6 1.0 %collective-permute-done.14.refs_5_ = bf16[128,512]{1,0:T(8,128)(2,1)S(1)} collective-permute-done((bf16[128,512]{1,0:T(8,128)(2,1)S(1)}, bf16[128,512]{1,0:T(8,128)(2,1)S(1)}, u32[]{:S(2)}, u32[]{:S(2)}) %collective-permute-start.14) | collective-permute-done | bytes 131104 | tf_op jit(solution)/shard_map/ppermute | solution.py:185
  35.6 0.0 collective-permute-start.18
  35.6 0.4 collective-permute-done.13.refs_0_.refs_4_
  36.0 0.1 collective-permute-start.17
  36.1 0.0 collective-permute-done.16.refs_7_
  36.1 0.8 %shard_map.81 = (f32[32,512]{1,0:T(8,128)S(1)}, bf16[128,32,128]{2,1,0:T(8,128)(2,1)S(1)}) custom-call(bf16[128,512]{1,0:T(8,128)(2,1)S(1)} %collective-permute-done.13.refs_0_.refs_4_, bf16[512,4096]{1,0:T(8,128)(2,1)S(1)} %get-tuple-element.24.refs_1_, f32[32,512]{1,0:T(8,128)S(1)} %get-tuple-element.32.refs_2_, ...), custom_call_target="tpu_custom_call" | custom-call | flops 67108864 | bytes 5046272 | tf_op jit(solution)/shard_map/pallas_call | solution.py:21
  37.0 0.0 collective-permute-done.19.refs_7_
  37.0 0.0 collective-permute-done.18.refs_6_
  37.0 0.4 collective-permute-done.17.refs_5_
  37.4 1.2 %shard_map.82 = (f32[32,512]{1,0:T(8,128)}, bf16[128,32,128]{2,1,0:T(8,128)(2,1)S(1)}) custom-call(s32[4]{0:T(128)S(1)} %copy-done, s32[4,16]{1,0:T(4,128)S(1)} %get-tuple-element.22.refs_1_, bf16[4,16,128,128]{3,2,1,0:T(8,128)(2,1)S(1)} %get-tuple-element.23.refs_2_, f32[32,512]{1,0:T(8,128)S(1)} %get-tuple-element.34.refs_3_, ...), custom_call_target="tpu_custom_call", output_to_operand_aliasing={{1}: (8, {})} | custom-call | flops 67108864 | bytes 3670288 | tf_op jit(solution)/shard_map/pallas_call | solution.py:21
Async XLA Ops:
  0.0 10.6 %copy-start = (s32[4]{0:T(128)S(1)}, s32[4]{0:T(128)}, u32[]{:S(2)}) copy-start(s32[4]{0:T(128)} %refs_0_.3) | copy-start | bytes 52
  0.9 7.8 %collective-permute-start.2 = (bf16[32,512]{1,0:T(8,128)(2,1)S(1)}, bf16[32,512]{1,0:T(8,128)(2,1)S(1)}, u32[]{:S(2)}, u32[]{:S(2)}) collective-permute-start(bf16[32,512]{1,0:T(8,128)(2,1)S(1)} %convert_element_type.3.x_ref), channel_id=1, source_target_pairs={{0,4},{1,5},{2,6},{3,7},{4,0},{5,1},{6,2},{7,3},{8,12},{9,13},{10,... | collective-permute-start | bytes 98312 | tf_op jit(solution)/shard_map/ppermute | solution.py:185
  4.9 5.7 %collective-permute-start.1 = (bf16[32,512]{1,0:T(8,128)(2,1)S(1)}, bf16[32,512]{1,0:T(8,128)(2,1)S(1)}, u32[]{:S(2)}, u32[]{:S(2)}) collective-permute-start(bf16[32,512]{1,0:T(8,128)(2,1)S(1)} %convert_element_type.3.x_ref), channel_id=1, source_target_pairs={{0,6},{1,7},{2,4},{3,5},{4,2},{5,3},{6,0},{7,1},{8,14},{9,15},{10,... | collective-permute-start | bytes 98312 | tf_op jit(solution)/shard_map/ppermute | solution.py:185
  6.2 4.4 %collective-permute-start = (bf16[32,512]{1,0:T(8,128)(2,1)S(1)}, bf16[32,512]{1,0:T(8,128)(2,1)S(1)}, u32[]{:S(2)}, u32[]{:S(2)}) collective-permute-start(bf16[32,512]{1,0:T(8,128)(2,1)S(1)} %convert_element_type.3.x_ref), channel_id=1, source_target_pairs={{0,2},{1,3},{2,0},{3,1},{4,6},{5,7},{6,4},{7,5},{8,10},{9,11},{10,... | collective-permute-start | bytes 98312 | tf_op jit(solution)/shard_map/ppermute | solution.py:185
  10.8 6.6 %collective-permute-start.5 = (bf16[128,512]{1,0:T(8,128)(2,1)S(1)}, bf16[128,512]{1,0:T(8,128)(2,1)S(1)}, u32[]{:S(2)}, u32[]{:S(2)}) collective-permute-start(bf16[128,512]{1,0:T(8,128)(2,1)S(1)} %shard_map.74.refs_0_), channel_id=1, source_target_pairs={{0,17},{1,16},{2,19},{3,18},{4,21},{5,20},{6,23},{7,22},{8,25},{9,... | collective-permute-start | bytes 393224 | tf_op jit(solution)/shard_map/ppermute | solution.py:185
  13.3 5.1 %collective-permute-start.4 = (bf16[128,512]{1,0:T(8,128)(2,1)S(1)}, bf16[128,512]{1,0:T(8,128)(2,1)S(1)}, u32[]{:S(2)}, u32[]{:S(2)}) collective-permute-start(bf16[128,512]{1,0:T(8,128)(2,1)S(1)} %shard_map.74.refs_0_), channel_id=1, source_target_pairs={{0,16},{1,17},{2,18},{3,19},{4,20},{5,21},{6,22},{7,23},{8,24},{9,... | collective-permute-start | bytes 393224 | tf_op jit(solution)/shard_map/ppermute | solution.py:185
  13.8 5.0 %collective-permute-start.3 = (bf16[128,512]{1,0:T(8,128)(2,1)S(1)}, bf16[128,512]{1,0:T(8,128)(2,1)S(1)}, u32[]{:S(2)}, u32[]{:S(2)}) collective-permute-start(bf16[128,512]{1,0:T(8,128)(2,1)S(1)} %shard_map.74.refs_0_), channel_id=1, source_target_pairs={{0,1},{1,0},{2,3},{3,2},{4,5},{5,4},{6,7},{7,6},{8,9},{9,8},{10,11... | collective-permute-start | bytes 393224 | tf_op jit(solution)/shard_map/ppermute | solution.py:185
  17.3 1.6 %collective-permute-start.6 = (bf16[128,512]{1,0:T(8,128)(2,1)S(1)}, bf16[128,512]{1,0:T(8,128)(2,1)S(1)}, u32[]{:S(2)}, u32[]{:S(2)}) collective-permute-start(bf16[128,512]{1,0:T(8,128)(2,1)S(1)} %get-tuple-element.27.refs_3_), channel_id=1, source_target_pairs={{0,8},{1,9},{2,10},{3,11},{4,12},{5,13},{6,14},{7,15},{8,0},{9,1},... | collective-permute-start | bytes 393224 | tf_op jit(solution)/shard_map/ppermute | solution.py:185
  17.4 2.4 %collective-permute-start.9 = (bf16[128,512]{1,0:T(8,128)(2,1)S(1)}, bf16[128,512]{1,0:T(8,128)(2,1)S(1)}, u32[]{:S(2)}, u32[]{:S(2)}) collective-permute-start(bf16[128,512]{1,0:T(8,128)(2,1)S(1)} %collective-permute-done.5.refs_6_), channel_id=1, source_target_pairs={{0,8},{1,9},{2,10},{3,11},{4,12},{5,13},{6,14},{7,15},{8,0},{9,1},... | collective-permute-start | bytes 393224 | tf_op jit(solution)/shard_map/ppermute | solution.py:185
  18.4 1.4 %collective-permute-start.8 = (bf16[128,512]{1,0:T(8,128)(2,1)S(1)}, bf16[128,512]{1,0:T(8,128)(2,1)S(1)}, u32[]{:S(2)}, u32[]{:S(2)}) collective-permute-start(bf16[128,512]{1,0:T(8,128)(2,1)S(1)} %collective-permute-done.4.refs_5_), channel_id=1, source_target_pairs={{0,8},{1,9},{2,10},{3,11},{4,12},{5,13},{6,14},{7,15},{8,0},{9,1},... | collective-permute-start | bytes 393224 | tf_op jit(solution)/shard_map/ppermute | solution.py:185
  18.8 1.3 %collective-permute-start.7 = (bf16[128,512]{1,0:T(8,128)(2,1)S(1)}, bf16[128,512]{1,0:T(8,128)(2,1)S(1)}, u32[]{:S(2)}, u32[]{:S(2)}) collective-permute-start(bf16[128,512]{1,0:T(8,128)(2,1)S(1)} %collective-permute-done.3.refs_0_.refs_4_), channel_id=1, source_target_pairs={{0,8},{1,9},{2,10},{3,11},{4,12},{5,13},{6,14},{7,15},{8,0},{9,1},... | collective-permute-start | bytes 393224 | tf_op jit(solution)/shard_map/ppermute | solution.py:185
  20.7 5.1 %collective-permute-start.12 = (bf16[32,512]{1,0:T(8,128)(2,1)S(1)}, bf16[32,512]{1,0:T(8,128)(2,1)S(1)}, u32[]{:S(2)}, u32[]{:S(2)}) collective-permute-start(bf16[32,512]{1,0:T(8,128)(2,1)S(1)} %get-tuple-element.31.refs_0_), channel_id=1, source_target_pairs={{0,4},{1,5},{2,6},{3,7},{4,0},{5,1},{6,2},{7,3},{8,12},{9,13},{10,... | collective-permute-start | bytes 98312 | tf_op jit(solution)/shard_map/ppermute | solution.py:185
  22.1 5.7 %collective-permute-start.11 = (bf16[32,512]{1,0:T(8,128)(2,1)S(1)}, bf16[32,512]{1,0:T(8,128)(2,1)S(1)}, u32[]{:S(2)}, u32[]{:S(2)}) collective-permute-start(bf16[32,512]{1,0:T(8,128)(2,1)S(1)} %get-tuple-element.31.refs_0_), channel_id=1, source_target_pairs={{0,6},{1,7},{2,4},{3,5},{4,2},{5,3},{6,0},{7,1},{8,14},{9,15},{10,... | collective-permute-start | bytes 98312 | tf_op jit(solution)/shard_map/ppermute | solution.py:185
  23.4 4.3 %collective-permute-start.10 = (bf16[32,512]{1,0:T(8,128)(2,1)S(1)}, bf16[32,512]{1,0:T(8,128)(2,1)S(1)}, u32[]{:S(2)}, u32[]{:S(2)}) collective-permute-start(bf16[32,512]{1,0:T(8,128)(2,1)S(1)} %get-tuple-element.31.refs_0_), channel_id=1, source_target_pairs={{0,2},{1,3},{2,0},{3,1},{4,6},{5,7},{6,4},{7,5},{8,10},{9,11},{10,... | collective-permute-start | bytes 98312 | tf_op jit(solution)/shard_map/ppermute | solution.py:185
  27.9 6.7 %collective-permute-start.15 = (bf16[128,512]{1,0:T(8,128)(2,1)S(1)}, bf16[128,512]{1,0:T(8,128)(2,1)S(1)}, u32[]{:S(2)}, u32[]{:S(2)}) collective-permute-start(bf16[128,512]{1,0:T(8,128)(2,1)S(1)} %shard_map.79.refs_0_), channel_id=1, source_target_pairs={{0,17},{1,16},{2,19},{3,18},{4,21},{5,20},{6,23},{7,22},{8,25},{9,... | collective-permute-start | bytes 393224 | tf_op jit(solution)/shard_map/ppermute | solution.py:185
  30.2 5.4 %collective-permute-start.14 = (bf16[128,512]{1,0:T(8,128)(2,1)S(1)}, bf16[128,512]{1,0:T(8,128)(2,1)S(1)}, u32[]{:S(2)}, u32[]{:S(2)}) collective-permute-start(bf16[128,512]{1,0:T(8,128)(2,1)S(1)} %shard_map.79.refs_0_), channel_id=1, source_target_pairs={{0,16},{1,17},{2,18},{3,19},{4,20},{5,21},{6,22},{7,23},{8,24},{9,... | collective-permute-start | bytes 393224 | tf_op jit(solution)/shard_map/ppermute | solution.py:185
  30.7 5.3 %collective-permute-start.13 = (bf16[128,512]{1,0:T(8,128)(2,1)S(1)}, bf16[128,512]{1,0:T(8,128)(2,1)S(1)}, u32[]{:S(2)}, u32[]{:S(2)}) collective-permute-start(bf16[128,512]{1,0:T(8,128)(2,1)S(1)} %shard_map.79.refs_0_), channel_id=1, source_target_pairs={{0,1},{1,0},{2,3},{3,2},{4,5},{5,4},{6,7},{7,6},{8,9},{9,8},{10,11... | collective-permute-start | bytes 393224 | tf_op jit(solution)/shard_map/ppermute | solution.py:185
  32.2 3.9 %collective-permute-start.16 = (bf16[128,512]{1,0:T(8,128)(2,1)S(1)}, bf16[128,512]{1,0:T(8,128)(2,1)S(1)}, u32[]{:S(2)}, u32[]{:S(2)}) collective-permute-start(bf16[128,512]{1,0:T(8,128)(2,1)S(1)} %get-tuple-element.33.refs_3_), channel_id=1, source_target_pairs={{0,8},{1,9},{2,10},{3,11},{4,12},{5,13},{6,14},{7,15},{8,0},{9,1},... | collective-permute-start | bytes 393224 | tf_op jit(solution)/shard_map/ppermute | solution.py:185
  34.6 2.3 %collective-permute-start.19 = (bf16[128,512]{1,0:T(8,128)(2,1)S(1)}, bf16[128,512]{1,0:T(8,128)(2,1)S(1)}, u32[]{:S(2)}, u32[]{:S(2)}) collective-permute-start(bf16[128,512]{1,0:T(8,128)(2,1)S(1)} %collective-permute-done.15.refs_6_), channel_id=1, source_target_pairs={{0,8},{1,9},{2,10},{3,11},{4,12},{5,13},{6,14},{7,15},{8,0},{9,1},... | collective-permute-start | bytes 393224 | tf_op jit(solution)/shard_map/ppermute | solution.py:185
  35.6 1.4 %collective-permute-start.18 = (bf16[128,512]{1,0:T(8,128)(2,1)S(1)}, bf16[128,512]{1,0:T(8,128)(2,1)S(1)}, u32[]{:S(2)}, u32[]{:S(2)}) collective-permute-start(bf16[128,512]{1,0:T(8,128)(2,1)S(1)} %collective-permute-done.14.refs_5_), channel_id=1, source_target_pairs={{0,8},{1,9},{2,10},{3,11},{4,12},{5,13},{6,14},{7,15},{8,0},{9,1},... | collective-permute-start | bytes 393224 | tf_op jit(solution)/shard_map/ppermute | solution.py:185
  36.0 1.3 %collective-permute-start.17 = (bf16[128,512]{1,0:T(8,128)(2,1)S(1)}, bf16[128,512]{1,0:T(8,128)(2,1)S(1)}, u32[]{:S(2)}, u32[]{:S(2)}) collective-permute-start(bf16[128,512]{1,0:T(8,128)(2,1)S(1)} %collective-permute-done.13.refs_0_.refs_4_), channel_id=1, source_target_pairs={{0,8},{1,9},{2,10},{3,11},{4,12},{5,13},{6,14},{7,15},{8,0},{9,1},... | collective-permute-start | bytes 393224 | tf_op jit(solution)/shard_map/ppermute | solution.py:185

commit v4 on v3

--- a/solution.py
+++ b/solution.py
@@ -105,11 +105,14 @@
     return count
 
 
-def column_kernel(l2, p_dev, pop, order, counts_ref, *refs):
+def column_kernel(l2, p_dev, pop, order, masked, counts_ref, *refs):
     out_ref = refs[-1]
     cond = refs[0].shape[0]
     count = count_of(counts_ref)
     for d, block in zip(order, refs[:-1]):
+        if not masked:
+            out_ref[d * cond : (d + 1) * cond, :] = block[...]
+            continue
         first = (lax.axis_index("local") ^ (d * l2)) * p_dev
         for s in range(p_dev):
             at = slice(s * pop, (s + 1) * pop)
@@ -198,7 +201,7 @@
     for step in range(STEPS):
         order = (1, 3, 2)
         column = call(
-            functools.partial(column_kernel, l2, p_dev, pop, (0,) + order),
+            functools.partial(column_kernel, l2, p_dev, pop, (0,) + order, step == 0),
             shape((l1 * cond, width), mine.dtype),
             [counts, kept] + [swap(mine, d1=d) for d in order],
             [VMEM] * (1 + l1),

time: 38.7 us -> 38.6 us (level)
  no operation moved by 1% of the time
where the time goes in v4:
time: 38.6 us; the launch traced here: 38.4 us
  starting transfers between devices  17.1 us (44%)
  waiting for transfers between devices  10.9 us (28%)
  Pallas kernels  9.41 us (24%)
  other arithmetic  0.86 us (2%)
    ppermute x20, starting transfers between devices, swap(): return lax.ppermute(x, AXES, [(i, i ^ by) for i in range(devices)])  17.1 us
    ppermute x20, waiting for transfers between devices, swap(): return lax.ppermute(x, AXES, [(i, i ^ by) for i in range(devices)])  10.9 us
    pallas_call x10, Pallas kernels, call(): pl.pallas_call(kernel, out_shape=out, in_specs=in_specs, out_specs=out_sp...  9.41 us
    convert_element_type x1, other arithmetic, body(): mine = rates_init.astype(jnp.bfloat16)  0.86 us
  transfers between devices with their start and end apart: 20, of which 10 were waited for; matrix products, arithmetic and copies ran while one was open for 0% of the time, Pallas kernels for 20%

profile of v4, /device:TPU:0, one launch (start us, length us, event | category | flops | bytes accessed | tf_op | source)
XLA Modules:
  0.0 38.4 jit_solution(14815998775053164384)
XLA Ops:
  0.0 0.0 copy-start
  0.0 0.9 %convert_element_type.3.x_ref = bf16[32,512]{1,0:T(8,128)(2,1)S(1)} convert(f32[32,512]{1,0:T(8,128)} %param.7) | non-fusion elementwise | flops 16384 | bytes 98304 | tf_op jit(solution)/shard_map/convert_element_type | solution.py:190
  0.9 4.0 %collective-permute-start.2 = (bf16[32,512]{1,0:T(8,128)(2,1)S(1)}, bf16[32,512]{1,0:T(8,128)(2,1)S(1)}, u32[]{:S(2)}, u32[]{:S(2)}) collective-permute-start(bf16[32,512]{1,0:T(8,128)(2,1)S(1)} %convert_element_type.3.x_ref), channel_id=1, source_target_pairs={{0,4},{1,5},{2,6},{3,7},{4,0},{5,1},{6,2},{7,3},{8,12},{9,13},{10,... | collective-permute-start | bytes 98312 | tf_op jit(solution)/shard_map/ppermute | solution.py:188
  4.9 1.3 %collective-permute-start.1 = (bf16[32,512]{1,0:T(8,128)(2,1)S(1)}, bf16[32,512]{1,0:T(8,128)(2,1)S(1)}, u32[]{:S(2)}, u32[]{:S(2)}) collective-permute-start(bf16[32,512]{1,0:T(8,128)(2,1)S(1)} %convert_element_type.3.x_ref), channel_id=1, source_target_pairs={{0,6},{1,7},{2,4},{3,5},{4,2},{5,3},{6,0},{7,1},{8,14},{9,15},{10,... | collective-permute-start | bytes 98312 | tf_op jit(solution)/shard_map/ppermute | solution.py:188
  6.2 0.2 collective-permute-start
  6.5 2.2 %shard_map.73 = (bf16[512,4096]{1,0:T(8,128)(2,1)S(1)}, bf16[32,512]{1,0:T(8,128)(2,1)S(1)}) custom-call(bf16[32,512]{1,0:T(8,128)(2,1)S(1)} %convert_element_type.3.x_ref, bf16[512,4096]{1,0:T(8,128)(2,1)} %w_ref.1), custom_call_target="tpu_custom_call" | custom-call | bytes 4227072 | tf_op jit(solution)/shard_map/pallas_call | solution.py:21
  8.7 0.0 collective-permute-done.2.refs_3_
  8.7 1.9 %collective-permute-done.1.refs_2_ = bf16[32,512]{1,0:T(8,128)(2,1)S(1)} collective-permute-done((bf16[32,512]{1,0:T(8,128)(2,1)S(1)}, bf16[32,512]{1,0:T(8,128)(2,1)S(1)}, u32[]{:S(2)}, u32[]{:S(2)}) %collective-permute-start.1) | collective-permute-done | bytes 32800 | tf_op jit(solution)/shard_map/ppermute | solution.py:188
  10.6 0.0 collective-permute-done.refs_1_
  10.6 0.0 copy-done
  10.6 0.1 shard_map.74.refs_0_
  10.8 2.5 %collective-permute-start.5 = (bf16[128,512]{1,0:T(8,128)(2,1)S(1)}, bf16[128,512]{1,0:T(8,128)(2,1)S(1)}, u32[]{:S(2)}, u32[]{:S(2)}) collective-permute-start(bf16[128,512]{1,0:T(8,128)(2,1)S(1)} %shard_map.74.refs_0_), channel_id=1, source_target_pairs={{0,17},{1,16},{2,19},{3,18},{4,21},{5,20},{6,23},{7,22},{8,25},{9,... | collective-permute-start | bytes 393224 | tf_op jit(solution)/shard_map/ppermute | solution.py:188
  13.3 0.5 %collective-permute-start.4 = (bf16[128,512]{1,0:T(8,128)(2,1)S(1)}, bf16[128,512]{1,0:T(8,128)(2,1)S(1)}, u32[]{:S(2)}, u32[]{:S(2)}) collective-permute-start(bf16[128,512]{1,0:T(8,128)(2,1)S(1)} %shard_map.74.refs_0_), channel_id=1, source_target_pairs={{0,16},{1,17},{2,18},{3,19},{4,20},{5,21},{6,22},{7,23},{8,24},{9,... | collective-permute-start | bytes 393224 | tf_op jit(solution)/shard_map/ppermute | solution.py:188
  13.8 0.5 %collective-permute-start.3 = (bf16[128,512]{1,0:T(8,128)(2,1)S(1)}, bf16[128,512]{1,0:T(8,128)(2,1)S(1)}, u32[]{:S(2)}, u32[]{:S(2)}) collective-permute-start(bf16[128,512]{1,0:T(8,128)(2,1)S(1)} %shard_map.74.refs_0_), channel_id=1, source_target_pairs={{0,1},{1,0},{2,3},{3,2},{4,5},{5,4},{6,7},{7,6},{8,9},{9,8},{10,11... | collective-permute-start | bytes 393224 | tf_op jit(solution)/shard_map/ppermute | solution.py:188
  14.3 2.3 %shard_map.75 = (bf16[4,16,128,128]{3,2,1,0:T(8,128)(2,1)S(1)}, f32[32,512]{1,0:T(8,128)S(1)}, s32[4,16]{1,0:T(4,128)S(1)}, bf16[128,512]{1,0:T(8,128)(2,1)S(1)}) custom-call(bf16[128,512]{1,0:T(8,128)(2,1)S(1)} %shard_map.74.refs_0_, s32[4,16]{1,0:T(4,128)} %refs_1_.1, s32[4]{0:T(128)} %refs_2_.1, bf16[4,16,128,128]{3,2,1,0:T(8,128)(2,1)} %refs_3_.1, ...), custom_call_target="tpu_custom_call" | custom-call | bytes 2294032 | tf_op jit(solution)/shard_map/pallas_call | solution.py:21
  16.6 0.7 %shard_map.76 = (f32[32,512]{1,0:T(8,128)S(1)}, bf16[128,512]{1,0:T(8,128)(2,1)S(1)}) custom-call(bf16[128,512]{1,0:T(8,128)(2,1)S(1)} %get-tuple-element.25.refs_0_, bf16[512,4096]{1,0:T(8,128)(2,1)S(1)} %get-tuple-element.24.refs_1_), custom_call_target="tpu_custom_call" | custom-call | flops 67108864 | bytes 4325376 | tf_op jit(solution)/shard_map/pallas_call | solution.py:21
  17.3 0.0 collective-permute-start.6
  17.4 0.0 collective-permute-done.5.refs_6_
  17.4 0.5 %collective-permute-start.9 = (bf16[128,512]{1,0:T(8,128)(2,1)S(1)}, bf16[128,512]{1,0:T(8,128)(2,1)S(1)}, u32[]{:S(2)}, u32[]{:S(2)}) collective-permute-start(bf16[128,512]{1,0:T(8,128)(2,1)S(1)} %collective-permute-done.5.refs_6_), channel_id=1, source_target_pairs={{0,8},{1,9},{2,10},{3,11},{4,12},{5,13},{6,14},{7,15},{8,0},{9,1},... | collective-permute-start | bytes 393224 | tf_op jit(solution)/shard_map/ppermute | solution.py:188
  17.9 0.5 %collective-permute-done.4.refs_5_ = bf16[128,512]{1,0:T(8,128)(2,1)S(1)} collective-permute-done((bf16[128,512]{1,0:T(8,128)(2,1)S(1)}, bf16[128,512]{1,0:T(8,128)(2,1)S(1)}, u32[]{:S(2)}, u32[]{:S(2)}) %collective-permute-start.4) | collective-permute-done | bytes 131104 | tf_op jit(solution)/shard_map/ppermute | solution.py:188
  18.4 0.0 collective-permute-start.8
  18.4 0.4 collective-permute-done.3.refs_0_.refs_4_
  18.8 0.1 collective-permute-start.7
  18.9 0.0 collective-permute-done.6.refs_7_
  18.9 0.8 %shard_map.77 = (f32[32,512]{1,0:T(8,128)S(1)}, bf16[128,32,128]{2,1,0:T(8,128)(2,1)S(1)}) custom-call(bf16[128,512]{1,0:T(8,128)(2,1)S(1)} %collective-permute-done.3.refs_0_.refs_4_, bf16[512,4096]{1,0:T(8,128)(2,1)S(1)} %get-tuple-element.24.refs_1_, f32[32,512]{1,0:T(8,128)S(1)} %get-tuple-element.26.refs_2_, ...), custom_call_target="tpu_custom_call" | custom-call | flops 67108864 | bytes 5046272 | tf_op jit(solution)/shard_map/pallas_call | solution.py:21
  19.7 0.0 collective-permute-done.9.refs_7_
  19.8 0.0 collective-permute-done.8.refs_6_
  19.8 0.4 collective-permute-done.7.refs_5_
  20.1 0.5 %shard_map.78 = (bf16[32,512]{1,0:T(8,128)(2,1)S(1)}, bf16[128,32,128]{2,1,0:T(8,128)(2,1)S(1)}) custom-call(s32[4]{0:T(128)S(1)} %copy-done, s32[4,16]{1,0:T(4,128)S(1)} %get-tuple-element.22.refs_1_, bf16[4,16,128,128]{3,2,1,0:T(8,128)(2,1)S(1)} %get-tuple-element.23.refs_2_, ...), custom_call_target="tpu_custom_call", output_to_operand_aliasing={{1}: (8, {})} | custom-call | flops 67108864 | bytes 3670288 | tf_op jit(solution)/shard_map/pallas_call | solution.py:21
  20.7 1.4 %collective-permute-start.12 = (bf16[32,512]{1,0:T(8,128)(2,1)S(1)}, bf16[32,512]{1,0:T(8,128)(2,1)S(1)}, u32[]{:S(2)}, u32[]{:S(2)}) collective-permute-start(bf16[32,512]{1,0:T(8,128)(2,1)S(1)} %get-tuple-element.31.refs_0_), channel_id=1, source_target_pairs={{0,4},{1,5},{2,6},{3,7},{4,0},{5,1},{6,2},{7,3},{8,12},{9,13},{10,... | collective-permute-start | bytes 98312 | tf_op jit(solution)/shard_map/ppermute | solution.py:188
  22.1 1.4 %collective-permute-start.11 = (bf16[32,512]{1,0:T(8,128)(2,1)S(1)}, bf16[32,512]{1,0:T(8,128)(2,1)S(1)}, u32[]{:S(2)}, u32[]{:S(2)}) collective-permute-start(bf16[32,512]{1,0:T(8,128)(2,1)S(1)} %get-tuple-element.31.refs_0_), channel_id=1, source_target_pairs={{0,6},{1,7},{2,4},{3,5},{4,2},{5,3},{6,0},{7,1},{8,14},{9,15},{10,... | collective-permute-start | bytes 98312 | tf_op jit(solution)/shard_map/ppermute | solution.py:188
  23.4 0.8 %collective-permute-start.10 = (bf16[32,512]{1,0:T(8,128)(2,1)S(1)}, bf16[32,512]{1,0:T(8,128)(2,1)S(1)}, u32[]{:S(2)}, u32[]{:S(2)}) collective-permute-start(bf16[32,512]{1,0:T(8,128)(2,1)S(1)} %get-tuple-element.31.refs_0_), channel_id=1, source_target_pairs={{0,2},{1,3},{2,0},{3,1},{4,6},{5,7},{6,4},{7,5},{8,10},{9,11},{10,... | collective-permute-start | bytes 98312 | tf_op jit(solution)/shard_map/ppermute | solution.py:188
  24.2 1.5 %collective-permute-done.12.refs_3_ = bf16[32,512]{1,0:T(8,128)(2,1)S(1)} collective-permute-done((bf16[32,512]{1,0:T(8,128)(2,1)S(1)}, bf16[32,512]{1,0:T(8,128)(2,1)S(1)}, u32[]{:S(2)}, u32[]{:S(2)}) %collective-permute-start.12) | collective-permute-done | bytes 32800 | tf_op jit(solution)/shard_map/ppermute | solution.py:188
  25.7 2.0 %collective-permute-done.11.refs_2_ = bf16[32,512]{1,0:T(8,128)(2,1)S(1)} collective-permute-done((bf16[32,512]{1,0:T(8,128)(2,1)S(1)}, bf16[32,512]{1,0:T(8,128)(2,1)S(1)}, u32[]{:S(2)}, u32[]{:S(2)}) %collective-permute-start.11) | collective-permute-done | bytes 32800 | tf_op jit(solution)/shard_map/ppermute | solution.py:188
  27.8 0.0 collective-permute-done.10.refs_1_
  27.8 2.3 %collective-permute-start.15 = (bf16[128,512]{1,0:T(8,128)(2,1)S(1)}, bf16[128,512]{1,0:T(8,128)(2,1)S(1)}, u32[]{:S(2)}, u32[]{:S(2)}) collective-permute-start(bf16[128,512]{1,0:T(8,128)(2,1)S(1)} %shard_map.79.refs_0_), channel_id=1, source_target_pairs={{0,17},{1,16},{2,19},{3,18},{4,21},{5,20},{6,23},{7,22},{8,25},{9,... | collective-permute-start | bytes 393224 | tf_op jit(solution)/shard_map/ppermute | solution.py:188
  30.1 0.5 %collective-permute-start.14 = (bf16[128,512]{1,0:T(8,128)(2,1)S(1)}, bf16[128,512]{1,0:T(8,128)(2,1)S(1)}, u32[]{:S(2)}, u32[]{:S(2)}) collective-permute-start(bf16[128,512]{1,0:T(8,128)(2,1)S(1)} %shard_map.79.refs_0_), channel_id=1, source_target_pairs={{0,16},{1,17},{2,18},{3,19},{4,20},{5,21},{6,22},{7,23},{8,24},{9,... | collective-permute-start | bytes 393224 | tf_op jit(solution)/shard_map/ppermute | solution.py:188
  30.6 0.8 %collective-permute-start.13 = (bf16[128,512]{1,0:T(8,128)(2,1)S(1)}, bf16[128,512]{1,0:T(8,128)(2,1)S(1)}, u32[]{:S(2)}, u32[]{:S(2)}) collective-permute-start(bf16[128,512]{1,0:T(8,128)(2,1)S(1)} %shard_map.79.refs_0_), channel_id=1, source_target_pairs={{0,1},{1,0},{2,3},{3,2},{4,5},{5,4},{6,7},{7,6},{8,9},{9,8},{10,11... | collective-permute-start | bytes 393224 | tf_op jit(solution)/shard_map/ppermute | solution.py:188
  31.3 0.7 %shard_map.80 = (f32[32,512]{1,0:T(8,128)S(1)}, bf16[128,512]{1,0:T(8,128)(2,1)S(1)}) custom-call(bf16[128,512]{1,0:T(8,128)(2,1)S(1)} %shard_map.79.refs_0_, bf16[512,4096]{1,0:T(8,128)(2,1)S(1)} %get-tuple-element.24.refs_1_), custom_call_target="tpu_custom_call" | custom-call | flops 67108864 | bytes 4325376 | tf_op jit(solution)/shard_map/pallas_call | solution.py:21
  32.1 0.0 collective-permute-start.16
  32.1 2.4 %collective-permute-done.15.refs_6_ = bf16[128,512]{1,0:T(8,128)(2,1)S(1)} collective-permute-done((bf16[128,512]{1,0:T(8,128)(2,1)S(1)}, bf16[128,512]{1,0:T(8,128)(2,1)S(1)}, u32[]{:S(2)}, u32[]{:S(2)}) %collective-permute-start.15) | collective-permute-done | bytes 131104 | tf_op jit(solution)/shard_map/ppermute | solution.py:188
  34.5 0.0 collective-permute-start.19
  34.5 1.0 %collective-permute-done.14.refs_5_ = bf16[128,512]{1,0:T(8,128)(2,1)S(1)} collective-permute-done((bf16[128,512]{1,0:T(8,128)(2,1)S(1)}, bf16[128,512]{1,0:T(8,128)(2,1)S(1)}, u32[]{:S(2)}, u32[]{:S(2)}) %collective-permute-start.14) | collective-permute-done | bytes 131104 | tf_op jit(solution)/shard_map/ppermute | solution.py:188
  35.5 0.0 collective-permute-start.18
  35.5 0.4 %collective-permute-done.13.refs_0_.refs_4_ = bf16[128,512]{1,0:T(8,128)(2,1)S(1)} collective-permute-done((bf16[128,512]{1,0:T(8,128)(2,1)S(1)}, bf16[128,512]{1,0:T(8,128)(2,1)S(1)}, u32[]{:S(2)}, u32[]{:S(2)}) %collective-permute-start.13) | collective-permute-done | bytes 131104 | tf_op jit(solution)/shard_map/ppermute | solution.py:188
  35.9 0.1 collective-permute-start.17
  36.0 0.0 collective-permute-done.16.refs_7_
  36.0 0.8 %shard_map.81 = (f32[32,512]{1,0:T(8,128)S(1)}, bf16[128,32,128]{2,1,0:T(8,128)(2,1)S(1)}) custom-call(bf16[128,512]{1,0:T(8,128)(2,1)S(1)} %collective-permute-done.13.refs_0_.refs_4_, bf16[512,4096]{1,0:T(8,128)(2,1)S(1)} %get-tuple-element.24.refs_1_, f32[32,512]{1,0:T(8,128)S(1)} %get-tuple-element.32.refs_2_, ...), custom_call_target="tpu_custom_call" | custom-call | flops 67108864 | bytes 5046272 | tf_op jit(solution)/shard_map/pallas_call | solution.py:21
  36.8 0.0 collective-permute-done.19.refs_7_
  36.9 0.0 collective-permute-done.18.refs_6_
  36.9 0.4 collective-permute-done.17.refs_5_
  37.2 1.2 %shard_map.82 = (f32[32,512]{1,0:T(8,128)}, bf16[128,32,128]{2,1,0:T(8,128)(2,1)S(1)}) custom-call(s32[4]{0:T(128)S(1)} %copy-done, s32[4,16]{1,0:T(4,128)S(1)} %get-tuple-element.22.refs_1_, bf16[4,16,128,128]{3,2,1,0:T(8,128)(2,1)S(1)} %get-tuple-element.23.refs_2_, f32[32,512]{1,0:T(8,128)S(1)} %get-tuple-element.34.refs_3_, ...), custom_call_target="tpu_custom_call", output_to_operand_aliasing={{1}: (8, {})} | custom-call | flops 67108864 | bytes 3670288 | tf_op jit(solution)/shard_map/pallas_call | solution.py:21
  (1 shorter events, 0.0 us)
Async XLA Ops:
  0.0 10.6 %copy-start = (s32[4]{0:T(128)S(1)}, s32[4]{0:T(128)}, u32[]{:S(2)}) copy-start(s32[4]{0:T(128)} %refs_0_.3) | copy-start | bytes 52
  0.9 7.8 %collective-permute-start.2 = (bf16[32,512]{1,0:T(8,128)(2,1)S(1)}, bf16[32,512]{1,0:T(8,128)(2,1)S(1)}, u32[]{:S(2)}, u32[]{:S(2)}) collective-permute-start(bf16[32,512]{1,0:T(8,128)(2,1)S(1)} %convert_element_type.3.x_ref), channel_id=1, source_target_pairs={{0,4},{1,5},{2,6},{3,7},{4,0},{5,1},{6,2},{7,3},{8,12},{9,13},{10,... | collective-permute-start | bytes 98312 | tf_op jit(solution)/shard_map/ppermute | solution.py:188
  4.9 5.7 %collective-permute-start.1 = (bf16[32,512]{1,0:T(8,128)(2,1)S(1)}, bf16[32,512]{1,0:T(8,128)(2,1)S(1)}, u32[]{:S(2)}, u32[]{:S(2)}) collective-permute-start(bf16[32,512]{1,0:T(8,128)(2,1)S(1)} %convert_element_type.3.x_ref), channel_id=1, source_target_pairs={{0,6},{1,7},{2,4},{3,5},{4,2},{5,3},{6,0},{7,1},{8,14},{9,15},{10,... | collective-permute-start | bytes 98312 | tf_op jit(solution)/shard_map/ppermute | solution.py:188
  6.2 4.4 %collective-permute-start = (bf16[32,512]{1,0:T(8,128)(2,1)S(1)}, bf16[32,512]{1,0:T(8,128)(2,1)S(1)}, u32[]{:S(2)}, u32[]{:S(2)}) collective-permute-start(bf16[32,512]{1,0:T(8,128)(2,1)S(1)} %convert_element_type.3.x_ref), channel_id=1, source_target_pairs={{0,2},{1,3},{2,0},{3,1},{4,6},{5,7},{6,4},{7,5},{8,10},{9,11},{10,... | collective-permute-start | bytes 98312 | tf_op jit(solution)/shard_map/ppermute | solution.py:188
  10.8 6.6 %collective-permute-start.5 = (bf16[128,512]{1,0:T(8,128)(2,1)S(1)}, bf16[128,512]{1,0:T(8,128)(2,1)S(1)}, u32[]{:S(2)}, u32[]{:S(2)}) collective-permute-start(bf16[128,512]{1,0:T(8,128)(2,1)S(1)} %shard_map.74.refs_0_), channel_id=1, source_target_pairs={{0,17},{1,16},{2,19},{3,18},{4,21},{5,20},{6,23},{7,22},{8,25},{9,... | collective-permute-start | bytes 393224 | tf_op jit(solution)/shard_map/ppermute | solution.py:188
  13.3 5.1 %collective-permute-start.4 = (bf16[128,512]{1,0:T(8,128)(2,1)S(1)}, bf16[128,512]{1,0:T(8,128)(2,1)S(1)}, u32[]{:S(2)}, u32[]{:S(2)}) collective-permute-start(bf16[128,512]{1,0:T(8,128)(2,1)S(1)} %shard_map.74.refs_0_), channel_id=1, source_target_pairs={{0,16},{1,17},{2,18},{3,19},{4,20},{5,21},{6,22},{7,23},{8,24},{9,... | collective-permute-start | bytes 393224 | tf_op jit(solution)/shard_map/ppermute | solution.py:188
  13.8 5.0 %collective-permute-start.3 = (bf16[128,512]{1,0:T(8,128)(2,1)S(1)}, bf16[128,512]{1,0:T(8,128)(2,1)S(1)}, u32[]{:S(2)}, u32[]{:S(2)}) collective-permute-start(bf16[128,512]{1,0:T(8,128)(2,1)S(1)} %shard_map.74.refs_0_), channel_id=1, source_target_pairs={{0,1},{1,0},{2,3},{3,2},{4,5},{5,4},{6,7},{7,6},{8,9},{9,8},{10,11... | collective-permute-start | bytes 393224 | tf_op jit(solution)/shard_map/ppermute | solution.py:188
  17.3 1.6 %collective-permute-start.6 = (bf16[128,512]{1,0:T(8,128)(2,1)S(1)}, bf16[128,512]{1,0:T(8,128)(2,1)S(1)}, u32[]{:S(2)}, u32[]{:S(2)}) collective-permute-start(bf16[128,512]{1,0:T(8,128)(2,1)S(1)} %get-tuple-element.27.refs_3_), channel_id=1, source_target_pairs={{0,8},{1,9},{2,10},{3,11},{4,12},{5,13},{6,14},{7,15},{8,0},{9,1},... | collective-permute-start | bytes 393224 | tf_op jit(solution)/shard_map/ppermute | solution.py:188
  17.4 2.4 %collective-permute-start.9 = (bf16[128,512]{1,0:T(8,128)(2,1)S(1)}, bf16[128,512]{1,0:T(8,128)(2,1)S(1)}, u32[]{:S(2)}, u32[]{:S(2)}) collective-permute-start(bf16[128,512]{1,0:T(8,128)(2,1)S(1)} %collective-permute-done.5.refs_6_), channel_id=1, source_target_pairs={{0,8},{1,9},{2,10},{3,11},{4,12},{5,13},{6,14},{7,15},{8,0},{9,1},... | collective-permute-start | bytes 393224 | tf_op jit(solution)/shard_map/ppermute | solution.py:188
  18.4 1.4 %collective-permute-start.8 = (bf16[128,512]{1,0:T(8,128)(2,1)S(1)}, bf16[128,512]{1,0:T(8,128)(2,1)S(1)}, u32[]{:S(2)}, u32[]{:S(2)}) collective-permute-start(bf16[128,512]{1,0:T(8,128)(2,1)S(1)} %collective-permute-done.4.refs_5_), channel_id=1, source_target_pairs={{0,8},{1,9},{2,10},{3,11},{4,12},{5,13},{6,14},{7,15},{8,0},{9,1},... | collective-permute-start | bytes 393224 | tf_op jit(solution)/shard_map/ppermute | solution.py:188
  18.8 1.3 %collective-permute-start.7 = (bf16[128,512]{1,0:T(8,128)(2,1)S(1)}, bf16[128,512]{1,0:T(8,128)(2,1)S(1)}, u32[]{:S(2)}, u32[]{:S(2)}) collective-permute-start(bf16[128,512]{1,0:T(8,128)(2,1)S(1)} %collective-permute-done.3.refs_0_.refs_4_), channel_id=1, source_target_pairs={{0,8},{1,9},{2,10},{3,11},{4,12},{5,13},{6,14},{7,15},{8,0},{9,1},... | collective-permute-start | bytes 393224 | tf_op jit(solution)/shard_map/ppermute | solution.py:188
  20.7 5.1 %collective-permute-start.12 = (bf16[32,512]{1,0:T(8,128)(2,1)S(1)}, bf16[32,512]{1,0:T(8,128)(2,1)S(1)}, u32[]{:S(2)}, u32[]{:S(2)}) collective-permute-start(bf16[32,512]{1,0:T(8,128)(2,1)S(1)} %get-tuple-element.31.refs_0_), channel_id=1, source_target_pairs={{0,4},{1,5},{2,6},{3,7},{4,0},{5,1},{6,2},{7,3},{8,12},{9,13},{10,... | collective-permute-start | bytes 98312 | tf_op jit(solution)/shard_map/ppermute | solution.py:188
  22.1 5.7 %collective-permute-start.11 = (bf16[32,512]{1,0:T(8,128)(2,1)S(1)}, bf16[32,512]{1,0:T(8,128)(2,1)S(1)}, u32[]{:S(2)}, u32[]{:S(2)}) collective-permute-start(bf16[32,512]{1,0:T(8,128)(2,1)S(1)} %get-tuple-element.31.refs_0_), channel_id=1, source_target_pairs={{0,6},{1,7},{2,4},{3,5},{4,2},{5,3},{6,0},{7,1},{8,14},{9,15},{10,... | collective-permute-start | bytes 98312 | tf_op jit(solution)/shard_map/ppermute | solution.py:188
  23.4 4.4 %collective-permute-start.10 = (bf16[32,512]{1,0:T(8,128)(2,1)S(1)}, bf16[32,512]{1,0:T(8,128)(2,1)S(1)}, u32[]{:S(2)}, u32[]{:S(2)}) collective-permute-start(bf16[32,512]{1,0:T(8,128)(2,1)S(1)} %get-tuple-element.31.refs_0_), channel_id=1, source_target_pairs={{0,2},{1,3},{2,0},{3,1},{4,6},{5,7},{6,4},{7,5},{8,10},{9,11},{10,... | collective-permute-start | bytes 98312 | tf_op jit(solution)/shard_map/ppermute | solution.py:188
  27.8 6.7 %collective-permute-start.15 = (bf16[128,512]{1,0:T(8,128)(2,1)S(1)}, bf16[128,512]{1,0:T(8,128)(2,1)S(1)}, u32[]{:S(2)}, u32[]{:S(2)}) collective-permute-start(bf16[128,512]{1,0:T(8,128)(2,1)S(1)} %shard_map.79.refs_0_), channel_id=1, source_target_pairs={{0,17},{1,16},{2,19},{3,18},{4,21},{5,20},{6,23},{7,22},{8,25},{9,... | collective-permute-start | bytes 393224 | tf_op jit(solution)/shard_map/ppermute | solution.py:188
  30.1 5.4 %collective-permute-start.14 = (bf16[128,512]{1,0:T(8,128)(2,1)S(1)}, bf16[128,512]{1,0:T(8,128)(2,1)S(1)}, u32[]{:S(2)}, u32[]{:S(2)}) collective-permute-start(bf16[128,512]{1,0:T(8,128)(2,1)S(1)} %shard_map.79.refs_0_), channel_id=1, source_target_pairs={{0,16},{1,17},{2,18},{3,19},{4,20},{5,21},{6,22},{7,23},{8,24},{9,... | collective-permute-start | bytes 393224 | tf_op jit(solution)/shard_map/ppermute | solution.py:188
  30.6 5.3 %collective-permute-start.13 = (bf16[128,512]{1,0:T(8,128)(2,1)S(1)}, bf16[128,512]{1,0:T(8,128)(2,1)S(1)}, u32[]{:S(2)}, u32[]{:S(2)}) collective-permute-start(bf16[128,512]{1,0:T(8,128)(2,1)S(1)} %shard_map.79.refs_0_), channel_id=1, source_target_pairs={{0,1},{1,0},{2,3},{3,2},{4,5},{5,4},{6,7},{7,6},{8,9},{9,8},{10,11... | collective-permute-start | bytes 393224 | tf_op jit(solution)/shard_map/ppermute | solution.py:188
  32.1 3.9 %collective-permute-start.16 = (bf16[128,512]{1,0:T(8,128)(2,1)S(1)}, bf16[128,512]{1,0:T(8,128)(2,1)S(1)}, u32[]{:S(2)}, u32[]{:S(2)}) collective-permute-start(bf16[128,512]{1,0:T(8,128)(2,1)S(1)} %get-tuple-element.33.refs_3_), channel_id=1, source_target_pairs={{0,8},{1,9},{2,10},{3,11},{4,12},{5,13},{6,14},{7,15},{8,0},{9,1},... | collective-permute-start | bytes 393224 | tf_op jit(solution)/shard_map/ppermute | solution.py:188
  34.5 2.3 %collective-permute-start.19 = (bf16[128,512]{1,0:T(8,128)(2,1)S(1)}, bf16[128,512]{1,0:T(8,128)(2,1)S(1)}, u32[]{:S(2)}, u32[]{:S(2)}) collective-permute-start(bf16[128,512]{1,0:T(8,128)(2,1)S(1)} %collective-permute-done.15.refs_6_), channel_id=1, source_target_pairs={{0,8},{1,9},{2,10},{3,11},{4,12},{5,13},{6,14},{7,15},{8,0},{9,1},... | collective-permute-start | bytes 393224 | tf_op jit(solution)/shard_map/ppermute | solution.py:188
  35.5 1.4 %collective-permute-start.18 = (bf16[128,512]{1,0:T(8,128)(2,1)S(1)}, bf16[128,512]{1,0:T(8,128)(2,1)S(1)}, u32[]{:S(2)}, u32[]{:S(2)}) collective-permute-start(bf16[128,512]{1,0:T(8,128)(2,1)S(1)} %collective-permute-done.14.refs_5_), channel_id=1, source_target_pairs={{0,8},{1,9},{2,10},{3,11},{4,12},{5,13},{6,14},{7,15},{8,0},{9,1},... | collective-permute-start | bytes 393224 | tf_op jit(solution)/shard_map/ppermute | solution.py:188
  35.9 1.3 %collective-permute-start.17 = (bf16[128,512]{1,0:T(8,128)(2,1)S(1)}, bf16[128,512]{1,0:T(8,128)(2,1)S(1)}, u32[]{:S(2)}, u32[]{:S(2)}) collective-permute-start(bf16[128,512]{1,0:T(8,128)(2,1)S(1)} %collective-permute-done.13.refs_0_.refs_4_), channel_id=1, source_target_pairs={{0,8},{1,9},{2,10},{3,11},{4,12},{5,13},{6,14},{7,15},{8,0},{9,1},... | collective-permute-start | bytes 393224 | tf_op jit(solution)/shard_map/ppermute | solution.py:188

commit v5 on v4

--- a/solution.py
+++ b/solution.py
@@ -9,6 +9,8 @@
 
 STEPS = 2
 PIECES = 4
+FIRST = ((0, 0), (1, 1), (3, 2), (2, 3))
+SECOND = ((0, 0), (1, 1), (2, 3), (3, 2))
 CORES = 2
 AXES = ("area", "local")
 VMEM = pl.BlockSpec(memory_space=pltpu.VMEM)
@@ -61,11 +63,11 @@
         move.wait()
 
 
-def long_kernel(sizes, *refs):
-    nx, l1, l2, p_dev = sizes
+def long_kernel(p_area, places, *refs):
     x_ref, columns_hbm, map_hbm, w_hbm, drive_hbm = refs[:5]
     w_ref, drive_ref, slots_ref, again_ref = refs[5:9]
     columns_ref, map_ref, wide_ref, sems, w_sems = refs[9:]
+    p_dev = w_ref.shape[0]
     moves = [
         pltpu.make_async_copy(a, b, sems.at[n])
         for n, (a, b) in enumerate(
@@ -79,41 +81,49 @@
     for move in moves:
         move.wait()
     area, local = lax.axis_index("area"), lax.axis_index("local")
-    inside_bits = log2(l1 * l2 * p_dev)
+    inside_bits = log2(p_area)
     columns = columns_ref[...]
     logical = columns >> inside_bits
     inside = columns & ((1 << inside_bits) - 1)
     target = jnp.zeros_like(columns)
-    for a in range(nx * CORES):
+    for a in range(map_ref.shape[0]):
         target = jnp.where(logical == a, map_ref[a], target)
     da = target ^ area
     dl = (inside >> log2(p_dev)) ^ local
-    n = (da & (CORES - 1)) * nx + (da >> log2(CORES))
-    n = n * l2 + (dl & (l2 - 1))
-    n = n * l1 + (dl >> log2(l2))
-    slots_ref[...] = n * p_dev + (inside & (p_dev - 1))
+    dc = da & (CORES - 1)
+    away = (da >> log2(CORES)) * (p_area // p_dev) + dl
+    place = jnp.zeros_like(columns)
+    for core in range(CORES):
+        held = ((target & (CORES - 1)) == core).astype(jnp.int32)
+        for by, at in places[core].items():
+            place = jnp.where((away == by) & (held == 1), at, place)
+    place = dc * len(places[0]) + place
+    slots_ref[...] = place * p_dev + (inside & (p_dev - 1))
     for p, move in enumerate(w_moves):
         move.wait()
         for k in range(w_ref.shape[1]):
             w_ref[p, k] = wide_ref[p, k].T
 
 
-def count_of(counts_ref):
+def count_of(counts_ref, area):
     count = counts_ref[0]
     for a in range(1, counts_ref.shape[0]):
-        count = jnp.where(lax.axis_index("area") == a, counts_ref[a], count)
+        count = jnp.where(area == a, counts_ref[a], count)
     return count
 
 
-def column_kernel(l2, p_dev, pop, order, masked, counts_ref, *refs):
+def column_kernel(parts, p_dev, pop, counts_ref, *refs):
     out_ref = refs[-1]
     cond = refs[0].shape[0]
-    count = count_of(counts_ref)
-    for d, block in zip(order, refs[:-1]):
-        if not masked:
+    area, local = lax.axis_index("area"), lax.axis_index("local")
+    for (d, far), block in zip(parts, refs[:-1]):
+        if far is None:
             out_ref[d * cond : (d + 1) * cond, :] = block[...]
             continue
-        first = (lax.axis_index("local") ^ (d * l2)) * p_dev
+        (x0, l0), (x1, l1) = far
+        odd = area & 1
+        count = count_of(counts_ref, area ^ (jnp.where(odd == 1, x1, x0) * CORES))
+        first = (local ^ jnp.where(odd == 1, l1, l0)) * p_dev
         for s in range(p_dev):
             at = slice(s * pop, (s + 1) * pop)
             x = block[:, at]
@@ -132,30 +142,40 @@
                 at += 1
 
 
-def inner_kernel(l2, other, cond, *refs):
-    blocks_ref, w_ref = refs[:2]
+def add_inner(lists, cond, arrays, w_ref, start_ref, out_ref):
     here = lax.axis_index("local")
-    width = blocks_ref.shape[1]
-    total = None
-    if not other:
-        out_ref, again_ref = refs[2:]
-        again_ref[...] = blocks_ref[...]
-    elif len(refs) == 4:
-        total, out_ref = refs[2][...], refs[3]
-    else:
-        total, arrays, out_ref, table = refs[2][...], refs[3:-2], refs[-2], refs[-1]
-        lay(arrays, table, 0, cond)
-    for d in range(blocks_ref.shape[0] // cond):
-        l = here ^ (d * l2 + other)
-        at = pl.ds(pl.multiple_of(l * width, width), width)
-        part = lax.dot_general(
-            blocks_ref[d * cond : (d + 1) * cond, :],
-            w_ref[:, at],
-            DIMS,
-            preferred_element_type=jnp.float32,
-        )
-        total = part if total is None else total + part
-    out_ref[...] = total
+    width = out_ref.shape[1]
+
+    def add(blocks):
+        total = None if start_ref is None else start_ref[...]
+        for n, d, far in blocks:
+            at = pl.ds(pl.multiple_of((here ^ far) * width, width), width)
+            part = lax.dot_general(
+                arrays[n][d * cond : (d + 1) * cond, :],
+                w_ref[:, at],
+                DIMS,
+                preferred_element_type=jnp.float32,
+            )
+            total = part if total is None else total + part
+        out_ref[...] = total
+
+    if lists[0] == lists[1]:
+        add(lists[0])
+        return
+    odd = lax.axis_index("area") & 1
+    for core in range(CORES):
+        pl.when(odd == core)(functools.partial(add, lists[core]))
+
+
+def inner_kernel(lists, cond, blocks_ref, w_ref, out_ref, again_ref):
+    again_ref[...] = blocks_ref[...]
+    add_inner(lists, cond, [blocks_ref], w_ref, None, out_ref)
+
+
+def rest_kernel(lists, cond, w_ref, start_ref, *refs):
+    arrays, out_ref, table = refs[:-2], refs[-2], refs[-1]
+    lay(arrays, table, 0, cond)
+    add_inner(lists, cond, arrays, w_ref, start_ref, out_ref)
 
 
 def outer_kernel(start, *refs):
@@ -163,7 +183,7 @@
     arrays, out_ref, table = refs[5:-3], refs[-2], refs[-1]
     p_dev, kblk, pop, _ = w_ref.shape
     lay(arrays, table, start, out_ref.shape[0])
-    count = count_of(counts_ref)
+    count = count_of(counts_ref, lax.axis_index("area"))
     first = lax.axis_index("local") * p_dev
     for p in range(p_dev):
         picked = jnp.concatenate([table[slots_ref[p, k]] for k in range(kblk)], axis=1)
@@ -175,6 +195,16 @@
         out_ref[:, here] = (rates * present).astype(out_ref.dtype)
 
 
+def plan(nx, l1, l2):
+    line = [(0, d * l2) for d in range(l1)]
+    plane = [(dx, d2) for dx in range(nx) for d2 in range(l2)]
+    if len(line) != len(plane):
+        return [(a, a) for a in line], [(a, a) for a in plane]
+    first = [(line[a], plane[b]) for a, b in FIRST]
+    second = [(plane[a], line[b]) for a, b in SECOND]
+    return first, second
+
+
 def body(rates_init, drive, within_w, long_w, columns, area_map, counts):
     areas, locs = lax.axis_size("area"), lax.axis_size("local")
     nx, l1 = areas // CORES, 4
@@ -182,10 +212,26 @@
     p_dev, kblk, pop, _ = long_w.shape
     cond, width = rates_init.shape
     devices = areas * locs
-
-    def swap(x, dx=0, dc=0, d1=0, d2=0):
-        by = (dx * CORES + dc) * locs + d1 * l2 + d2
-        return lax.ppermute(x, AXES, [(i, i ^ by) for i in range(devices)])
+    first, second = plan(nx, l1, l2)
+    places = [{}, {}]
+    lists = [([], []), ([], [])]
+    for core in range(CORES):
+        for n, by_n in enumerate(second):
+            for d, by_d in enumerate(first):
+                dx = by_n[core][0] ^ by_d[core][0]
+                dl = by_n[core][1] ^ by_d[core][1]
+                places[core][dx * locs + dl] = n * len(first) + d
+                if dx == 0:
+                    lists[n > 0][core].append((n, d, dl))
+
+    def swap(x, by):
+        far = [dx * CORES * locs + dl for dx, dl in by]
+        return lax.ppermute(
+            x, AXES, [(i, i ^ far[(i // locs) % CORES]) for i in range(devices)]
+        )
+
+    def across(x):
+        return lax.ppermute(x, AXES, [(i, i ^ locs) for i in range(devices)])
 
     mine = rates_init.astype(jnp.bfloat16)
     shape = jax.ShapeDtypeStruct
@@ -199,22 +245,22 @@
         out_specs=[VMEM] * 2,
     )
     for step in range(STEPS):
-        order = (1, 3, 2)
         column = call(
-            functools.partial(column_kernel, l2, p_dev, pop, (0,) + order, step == 0),
-            shape((l1 * cond, width), mine.dtype),
-            [counts, kept] + [swap(mine, d1=d) for d in order],
-            [VMEM] * (1 + l1),
+            functools.partial(
+                column_kernel,
+                [(d, None if step else by) for d, by in enumerate(first)],
+                p_dev,
+                pop,
+            ),
+            shape((len(first) * cond, width), mine.dtype),
+            [counts, kept] + [swap(mine, by) for by in first[1:]],
+            [VMEM] * (1 + len(first)),
             0,
         )
-        got = {
-            (dx, d2): swap(column, dx=dx, d2=d2) if dx or d2 else column
-            for dx in range(nx)
-            for d2 in range(l2)
-        }
+        whole = column
         if step == 0:
-            long_w, drive, slots, got[0, 0] = call(
-                functools.partial(long_kernel, (nx, l1, l2, p_dev)),
+            long_w, drive, slots, whole = call(
+                functools.partial(long_kernel, locs * p_dev, places),
                 [
                     pltpu.VMEM(x.shape, x.dtype)
                     for x in (long_w, drive, columns, column)
@@ -233,32 +279,24 @@
             )
         partial = shape((cond, width), jnp.float32)
         flops = 2 * cond * width * width * l1
-        inner, got[0, 0] = call(
-            functools.partial(inner_kernel, l2, 0, cond),
+        inner, whole = call(
+            functools.partial(inner_kernel, lists[0], cond),
             [partial, shape(column.shape, column.dtype)],
-            (got[0, 0], within_w),
+            (whole, within_w),
             [VMEM] * 2,
             flops,
             out_specs=[VMEM] * 2,
         )
-        for d2 in range(1, l2 - 1):
-            inner = call(
-                functools.partial(inner_kernel, l2, d2, cond),
-                partial,
-                (got[0, d2], within_w, inner),
-                [VMEM] * 3,
-                flops,
-            )
-        arrays = [got[dx, d2] for dx in range(nx) for d2 in range(l2)]
-        arrays += [swap(x, dc=1) for x in arrays]
-        early = len(arrays) // 2 + 1
-        per = l1 * p_dev
+        arrays = [whole] + [swap(column, by) for by in second[1:]]
+        arrays += [across(x) for x in arrays]
+        early = len(second) + 1
+        per = len(first) * p_dev
         table = pltpu.VMEM((len(arrays) * per, cond, pop), mine.dtype)
         inner, picks = call(
-            functools.partial(inner_kernel, l2, l2 - 1, cond),
+            functools.partial(rest_kernel, lists[1], cond),
             [partial, table],
-            [got[0, l2 - 1], within_w, inner] + arrays[:early],
-            [VMEM] * (3 + early),
+            [within_w, inner] + arrays[:early],
+            [VMEM] * (2 + early),
             flops,
             out_specs=[VMEM] * 2,
         )

time: 38.6 us -> 37.9 us (0.982)
  waiting for transfers between devices: 10.9 us -> 10.4 us
    ppermute x20, waiting for transfers between devices: 10.9 us -> 10.4 us  [the longest x12 9.44 us: swap(): lax.ppermute(x, AXES, [(i, i ^ far[i // locs % CORES]) for i in range(dev...]
where the time goes in v5:
time: 37.9 us; the launch traced here: 37.7 us
  starting transfers between devices  16.8 us (44%)
  waiting for transfers between devices  10.4 us (27%)
  Pallas kernels  9.46 us (25%)
  other arithmetic  0.86 us (2%)
    ppermute x12, starting transfers between devices, swap(): lax.ppermute(x, AXES, [(i, i ^ far[i // locs % CORES]) for i in range(dev...  16.3 us
    pallas_call x10, Pallas kernels, call(): pl.pallas_call(kernel, out_shape=out, in_specs=in_specs, out_specs=out_sp...  9.46 us
    ppermute x12, waiting for transfers between devices, swap(): lax.ppermute(x, AXES, [(i, i ^ far[i // locs % CORES]) for i in range(dev...  9.44 us
    ppermute x8, waiting for transfers between devices, across(): return lax.ppermute(x, AXES, [(i, i ^ locs) for i in range(devices)])  1.01 us
    convert_element_type x1, other arithmetic, body(): mine = rates_init.astype(jnp.bfloat16)  0.86 us
  transfers between devices with their start and end apart: 20, of which 10 were waited for; matrix products, arithmetic and copies ran while one was open for 0% of the time, Pallas kernels for 20%

profile of v5, /device:TPU:0, one launch (start us, length us, event | category | flops | bytes accessed | tf_op | source)
XLA Modules:
  0.0 37.7 jit_solution(3330845966599699681)
XLA Ops:
  0.0 0.0 copy-start
  0.0 0.9 %convert_element_type.3.x_ref = bf16[32,512]{1,0:T(8,128)(2,1)S(1)} convert(f32[32,512]{1,0:T(8,128)} %param.7) | non-fusion elementwise | flops 16384 | bytes 98304 | tf_op jit(solution)/shard_map/convert_element_type | solution.py:236
  0.9 4.0 %collective-permute-start.2 = (bf16[32,512]{1,0:T(8,128)(2,1)S(1)}, bf16[32,512]{1,0:T(8,128)(2,1)S(1)}, u32[]{:S(2)}, u32[]{:S(2)}) collective-permute-start(bf16[32,512]{1,0:T(8,128)(2,1)S(1)} %convert_element_type.3.x_ref), channel_id=1, source_target_pairs={{0,4},{1,5},{2,6},{3,7},{4,0},{5,1},{6,2},{7,3},{8,25},{9,24},{10,... | collective-permute-start | bytes 98312 | tf_op jit(solution)/shard_map/ppermute | solution.py:229
  4.9 1.3 %collective-permute-start.1 = (bf16[32,512]{1,0:T(8,128)(2,1)S(1)}, bf16[32,512]{1,0:T(8,128)(2,1)S(1)}, u32[]{:S(2)}, u32[]{:S(2)}) collective-permute-start(bf16[32,512]{1,0:T(8,128)(2,1)S(1)} %convert_element_type.3.x_ref), channel_id=1, source_target_pairs={{0,6},{1,7},{2,4},{3,5},{4,2},{5,3},{6,0},{7,1},{8,24},{9,25},{10,... | collective-permute-start | bytes 98312 | tf_op jit(solution)/shard_map/ppermute | solution.py:229
  6.2 0.2 collective-permute-start
  6.5 2.2 %shard_map.73 = (bf16[512,4096]{1,0:T(8,128)(2,1)S(1)}, bf16[32,512]{1,0:T(8,128)(2,1)S(1)}) custom-call(bf16[32,512]{1,0:T(8,128)(2,1)S(1)} %convert_element_type.3.x_ref, bf16[512,4096]{1,0:T(8,128)(2,1)} %w_ref.1), custom_call_target="tpu_custom_call" | custom-call | bytes 4227072 | tf_op jit(solution)/shard_map/pallas_call | solution.py:23
  8.7 0.0 collective-permute-done.2.refs_3_
  8.7 1.9 %collective-permute-done.1.refs_2_ = bf16[32,512]{1,0:T(8,128)(2,1)S(1)} collective-permute-done((bf16[32,512]{1,0:T(8,128)(2,1)S(1)}, bf16[32,512]{1,0:T(8,128)(2,1)S(1)}, u32[]{:S(2)}, u32[]{:S(2)}) %collective-permute-start.1) | collective-permute-done | bytes 32800 | tf_op jit(solution)/shard_map/ppermute | solution.py:229
  10.6 0.0 collective-permute-done.refs_1_
  10.6 0.0 copy-done
  10.6 0.1 shard_map.74.refs_0_
  10.8 2.5 %collective-permute-start.5 = (bf16[128,512]{1,0:T(8,128)(2,1)S(1)}, bf16[128,512]{1,0:T(8,128)(2,1)S(1)}, u32[]{:S(2)}, u32[]{:S(2)}) collective-permute-start(bf16[128,512]{1,0:T(8,128)(2,1)S(1)} %shard_map.74.refs_0_), channel_id=1, source_target_pairs={{0,17},{1,16},{2,19},{3,18},{4,21},{5,20},{6,23},{7,22},{8,12},{9,... | collective-permute-start | bytes 393224 | tf_op jit(solution)/shard_map/ppermute | solution.py:229
  13.3 0.5 %collective-permute-start.4 = (bf16[128,512]{1,0:T(8,128)(2,1)S(1)}, bf16[128,512]{1,0:T(8,128)(2,1)S(1)}, u32[]{:S(2)}, u32[]{:S(2)}) collective-permute-start(bf16[128,512]{1,0:T(8,128)(2,1)S(1)} %shard_map.74.refs_0_), channel_id=1, source_target_pairs={{0,16},{1,17},{2,18},{3,19},{4,20},{5,21},{6,22},{7,23},{8,14},{9,... | collective-permute-start | bytes 393224 | tf_op jit(solution)/shard_map/ppermute | solution.py:229
  13.8 0.5 %collective-permute-start.3 = (bf16[128,512]{1,0:T(8,128)(2,1)S(1)}, bf16[128,512]{1,0:T(8,128)(2,1)S(1)}, u32[]{:S(2)}, u32[]{:S(2)}) collective-permute-start(bf16[128,512]{1,0:T(8,128)(2,1)S(1)} %shard_map.74.refs_0_), channel_id=1, source_target_pairs={{0,1},{1,0},{2,3},{3,2},{4,5},{5,4},{6,7},{7,6},{8,10},{9,11},{10,... | collective-permute-start | bytes 393224 | tf_op jit(solution)/shard_map/ppermute | solution.py:229
  14.3 2.3 %shard_map.75 = (bf16[4,16,128,128]{3,2,1,0:T(8,128)(2,1)S(1)}, f32[32,512]{1,0:T(8,128)S(1)}, s32[4,16]{1,0:T(4,128)S(1)}, bf16[128,512]{1,0:T(8,128)(2,1)S(1)}) custom-call(bf16[128,512]{1,0:T(8,128)(2,1)S(1)} %shard_map.74.refs_0_, s32[4,16]{1,0:T(4,128)} %refs_1_.1, s32[4]{0:T(128)} %refs_2_.1, bf16[4,16,128,128]{3,2,1,0:T(8,128)(2,1)} %refs_3_.1, ...), custom_call_target="tpu_custom_call" | custom-call | bytes 2294032 | tf_op jit(solution)/shard_map/pallas_call | solution.py:23
  16.6 0.7 %shard_map.76 = (f32[32,512]{1,0:T(8,128)S(1)}, bf16[128,512]{1,0:T(8,128)(2,1)S(1)}) custom-call(bf16[128,512]{1,0:T(8,128)(2,1)S(1)} %get-tuple-element.25.blocks_ref, bf16[512,4096]{1,0:T(8,128)(2,1)S(1)} %get-tuple-element.24.w_ref), custom_call_target="tpu_custom_call" | custom-call | flops 67108864 | bytes 4325376 | tf_op jit(solution)/shard_map/pallas_call | solution.py:23
  17.4 0.0 collective-permute-start.6
  17.4 0.0 collective-permute-done.5.refs_3_
  17.4 0.5 %collective-permute-start.9 = (bf16[128,512]{1,0:T(8,128)(2,1)S(1)}, bf16[128,512]{1,0:T(8,128)(2,1)S(1)}, u32[]{:S(2)}, u32[]{:S(2)}) collective-permute-start(bf16[128,512]{1,0:T(8,128)(2,1)S(1)} %collective-permute-done.5.refs_3_), channel_id=1, source_target_pairs={{0,8},{1,9},{2,10},{3,11},{4,12},{5,13},{6,14},{7,15},{8,0},{9,1},... | collective-permute-start | bytes 393224 | tf_op jit(solution)/shard_map/ppermute | solution.py:234
  17.9 0.3 collective-permute-done.4.refs_2_
  18.2 0.0 collective-permute-start.8
  18.2 0.5 %collective-permute-done.3.refs_1_ = bf16[128,512]{1,0:T(8,128)(2,1)S(1)} collective-permute-done((bf16[128,512]{1,0:T(8,128)(2,1)S(1)}, bf16[128,512]{1,0:T(8,128)(2,1)S(1)}, u32[]{:S(2)}, u32[]{:S(2)}) %collective-permute-start.3) | collective-permute-done | bytes 131104 | tf_op jit(solution)/shard_map/ppermute | solution.py:229
  18.8 0.0 collective-permute-start.7
  18.8 0.0 collective-permute-done.6.refs_4_
  18.8 0.8 %shard_map.77 = (f32[32,512]{1,0:T(8,128)S(1)}, bf16[128,32,128]{2,1,0:T(8,128)(2,1)S(1)}) custom-call(bf16[512,4096]{1,0:T(8,128)(2,1)S(1)} %get-tuple-element.24.w_ref, f32[32,512]{1,0:T(8,128)S(1)} %get-tuple-element.26.start_ref, bf16[128,512]{1,0:T(8,128)(2,1)S(1)} %get-tuple-element.27.refs_0_, bf16[128,512]{1,0:T(8,128)(2,1)S(1)} %collective-permute-done.3.refs_1_, ...), custom_call_target="tpu_custom_call" | custom-call | flops 67108864 | bytes 4915200 | tf_op jit(solution)/shard_map/pallas_call | solution.py:23
  19.6 0.0 collective-permute-done.9.refs_7_
  19.6 0.0 collective-permute-done.8.refs_6_
  19.6 0.5 %collective-permute-done.7.refs_5_ = bf16[128,512]{1,0:T(8,128)(2,1)S(1)} collective-permute-done((bf16[128,512]{1,0:T(8,128)(2,1)S(1)}, bf16[128,512]{1,0:T(8,128)(2,1)S(1)}, u32[]{:S(2)}, u32[]{:S(2)}) %collective-permute-start.7) | collective-permute-done | bytes 131104 | tf_op jit(solution)/shard_map/ppermute | solution.py:234
  20.1 0.5 %shard_map.78 = (bf16[32,512]{1,0:T(8,128)(2,1)S(1)}, bf16[128,32,128]{2,1,0:T(8,128)(2,1)S(1)}) custom-call(s32[4]{0:T(128)S(1)} %copy-done, s32[4,16]{1,0:T(4,128)S(1)} %get-tuple-element.22.refs_1_, bf16[4,16,128,128]{3,2,1,0:T(8,128)(2,1)S(1)} %get-tuple-element.23.refs_2_, ...), custom_call_target="tpu_custom_call", output_to_operand_aliasing={{1}: (8, {})} | custom-call | flops 67108864 | bytes 3670288 | tf_op jit(solution)/shard_map/pallas_call | solution.py:23
  20.7 1.3 %collective-permute-start.12 = (bf16[32,512]{1,0:T(8,128)(2,1)S(1)}, bf16[32,512]{1,0:T(8,128)(2,1)S(1)}, u32[]{:S(2)}, u32[]{:S(2)}) collective-permute-start(bf16[32,512]{1,0:T(8,128)(2,1)S(1)} %get-tuple-element.31.refs_0_), channel_id=1, source_target_pairs={{0,4},{1,5},{2,6},{3,7},{4,0},{5,1},{6,2},{7,3},{8,25},{9,24},{10,... | collective-permute-start | bytes 98312 | tf_op jit(solution)/shard_map/ppermute | solution.py:229
  22.0 1.0 %collective-permute-start.11 = (bf16[32,512]{1,0:T(8,128)(2,1)S(1)}, bf16[32,512]{1,0:T(8,128)(2,1)S(1)}, u32[]{:S(2)}, u32[]{:S(2)}) collective-permute-start(bf16[32,512]{1,0:T(8,128)(2,1)S(1)} %get-tuple-element.31.refs_0_), channel_id=1, source_target_pairs={{0,6},{1,7},{2,4},{3,5},{4,2},{5,3},{6,0},{7,1},{8,24},{9,25},{10,... | collective-permute-start | bytes 98312 | tf_op jit(solution)/shard_map/ppermute | solution.py:229
  23.0 1.2 %collective-permute-start.10 = (bf16[32,512]{1,0:T(8,128)(2,1)S(1)}, bf16[32,512]{1,0:T(8,128)(2,1)S(1)}, u32[]{:S(2)}, u32[]{:S(2)}) collective-permute-start(bf16[32,512]{1,0:T(8,128)(2,1)S(1)} %get-tuple-element.31.refs_0_), channel_id=1, source_target_pairs={{0,2},{1,3},{2,0},{3,1},{4,6},{5,7},{6,4},{7,5},{8,9},{9,8},{10,11... | collective-permute-start | bytes 98312 | tf_op jit(solution)/shard_map/ppermute | solution.py:229
  24.2 1.3 %collective-permute-done.12.refs_3_ = bf16[32,512]{1,0:T(8,128)(2,1)S(1)} collective-permute-done((bf16[32,512]{1,0:T(8,128)(2,1)S(1)}, bf16[32,512]{1,0:T(8,128)(2,1)S(1)}, u32[]{:S(2)}, u32[]{:S(2)}) %collective-permute-start.12) | collective-permute-done | bytes 32800 | tf_op jit(solution)/shard_map/ppermute | solution.py:229
  25.5 2.1 %collective-permute-done.11.refs_2_ = bf16[32,512]{1,0:T(8,128)(2,1)S(1)} collective-permute-done((bf16[32,512]{1,0:T(8,128)(2,1)S(1)}, bf16[32,512]{1,0:T(8,128)(2,1)S(1)}, u32[]{:S(2)}, u32[]{:S(2)}) %collective-permute-start.11) | collective-permute-done | bytes 32800 | tf_op jit(solution)/shard_map/ppermute | solution.py:229
  27.7 0.0 collective-permute-done.10.refs_1_
  27.7 2.0 %collective-permute-start.15 = (bf16[128,512]{1,0:T(8,128)(2,1)S(1)}, bf16[128,512]{1,0:T(8,128)(2,1)S(1)}, u32[]{:S(2)}, u32[]{:S(2)}) collective-permute-start(bf16[128,512]{1,0:T(8,128)(2,1)S(1)} %shard_map.79.blocks_ref), channel_id=1, source_target_pairs={{0,17},{1,16},{2,19},{3,18},{4,21},{5,20},{6,23},{7,22},{8,12},{9,... | collective-permute-start | bytes 393224 | tf_op jit(solution)/shard_map/ppermute | solution.py:229
  29.7 0.5 %collective-permute-start.14 = (bf16[128,512]{1,0:T(8,128)(2,1)S(1)}, bf16[128,512]{1,0:T(8,128)(2,1)S(1)}, u32[]{:S(2)}, u32[]{:S(2)}) collective-permute-start(bf16[128,512]{1,0:T(8,128)(2,1)S(1)} %shard_map.79.blocks_ref), channel_id=1, source_target_pairs={{0,16},{1,17},{2,18},{3,19},{4,20},{5,21},{6,22},{7,23},{8,14},{9,... | collective-permute-start | bytes 393224 | tf_op jit(solution)/shard_map/ppermute | solution.py:229
  30.2 1.0 %collective-permute-start.13 = (bf16[128,512]{1,0:T(8,128)(2,1)S(1)}, bf16[128,512]{1,0:T(8,128)(2,1)S(1)}, u32[]{:S(2)}, u32[]{:S(2)}) collective-permute-start(bf16[128,512]{1,0:T(8,128)(2,1)S(1)} %shard_map.79.blocks_ref), channel_id=1, source_target_pairs={{0,1},{1,0},{2,3},{3,2},{4,5},{5,4},{6,7},{7,6},{8,10},{9,11},{10,... | collective-permute-start | bytes 393224 | tf_op jit(solution)/shard_map/ppermute | solution.py:229
  31.3 0.7 %shard_map.80 = (f32[32,512]{1,0:T(8,128)S(1)}, bf16[128,512]{1,0:T(8,128)(2,1)S(1)}) custom-call(bf16[128,512]{1,0:T(8,128)(2,1)S(1)} %shard_map.79.blocks_ref, bf16[512,4096]{1,0:T(8,128)(2,1)S(1)} %get-tuple-element.24.w_ref), custom_call_target="tpu_custom_call" | custom-call | flops 67108864 | bytes 4325376 | tf_op jit(solution)/shard_map/pallas_call | solution.py:23
  32.0 0.0 collective-permute-start.16
  32.0 1.6 %collective-permute-done.15.refs_3_ = bf16[128,512]{1,0:T(8,128)(2,1)S(1)} collective-permute-done((bf16[128,512]{1,0:T(8,128)(2,1)S(1)}, bf16[128,512]{1,0:T(8,128)(2,1)S(1)}, u32[]{:S(2)}, u32[]{:S(2)}) %collective-permute-start.15) | collective-permute-done | bytes 131104 | tf_op jit(solution)/shard_map/ppermute | solution.py:229
  33.6 0.0 collective-permute-start.19
  33.6 1.0 %collective-permute-done.14.refs_2_ = bf16[128,512]{1,0:T(8,128)(2,1)S(1)} collective-permute-done((bf16[128,512]{1,0:T(8,128)(2,1)S(1)}, bf16[128,512]{1,0:T(8,128)(2,1)S(1)}, u32[]{:S(2)}, u32[]{:S(2)}) %collective-permute-start.14) | collective-permute-done | bytes 131104 | tf_op jit(solution)/shard_map/ppermute | solution.py:229
  34.7 0.0 collective-permute-start.18
  34.7 0.5 %collective-permute-done.13.refs_1_ = bf16[128,512]{1,0:T(8,128)(2,1)S(1)} collective-permute-done((bf16[128,512]{1,0:T(8,128)(2,1)S(1)}, bf16[128,512]{1,0:T(8,128)(2,1)S(1)}, u32[]{:S(2)}, u32[]{:S(2)}) %collective-permute-start.13) | collective-permute-done | bytes 131104 | tf_op jit(solution)/shard_map/ppermute | solution.py:229
  35.2 0.0 collective-permute-start.17
  35.2 0.0 collective-permute-done.16.refs_4_
  35.2 0.8 %shard_map.81 = (f32[32,512]{1,0:T(8,128)S(1)}, bf16[128,32,128]{2,1,0:T(8,128)(2,1)S(1)}) custom-call(bf16[512,4096]{1,0:T(8,128)(2,1)S(1)} %get-tuple-element.24.w_ref, f32[32,512]{1,0:T(8,128)S(1)} %get-tuple-element.32.start_ref, bf16[128,512]{1,0:T(8,128)(2,1)S(1)} %get-tuple-element.33.refs_0_, bf16[128,512]{1,0:T(8,128)(2,1)S(1)} %collective-permute-done.13.refs_1_, ...), custom_call_target="tpu_custom_call" | custom-call | flops 67108864 | bytes 4915200 | tf_op jit(solution)/shard_map/pallas_call | solution.py:23
  36.0 0.0 collective-permute-done.19.refs_7_
  36.0 0.0 collective-permute-done.18.refs_6_
  36.1 0.5 %collective-permute-done.17.refs_5_ = bf16[128,512]{1,0:T(8,128)(2,1)S(1)} collective-permute-done((bf16[128,512]{1,0:T(8,128)(2,1)S(1)}, bf16[128,512]{1,0:T(8,128)(2,1)S(1)}, u32[]{:S(2)}, u32[]{:S(2)}) %collective-permute-start.17) | collective-permute-done | bytes 131104 | tf_op jit(solution)/shard_map/ppermute | solution.py:234
  36.5 1.2 %shard_map.82 = (f32[32,512]{1,0:T(8,128)}, bf16[128,32,128]{2,1,0:T(8,128)(2,1)S(1)}) custom-call(s32[4]{0:T(128)S(1)} %copy-done, s32[4,16]{1,0:T(4,128)S(1)} %get-tuple-element.22.refs_1_, bf16[4,16,128,128]{3,2,1,0:T(8,128)(2,1)S(1)} %get-tuple-element.23.refs_2_, f32[32,512]{1,0:T(8,128)S(1)} %get-tuple-element.34.refs_3_, ...), custom_call_target="tpu_custom_call", output_to_operand_aliasing={{1}: (8, {})} | custom-call | flops 67108864 | bytes 3670288 | tf_op jit(solution)/shard_map/pallas_call | solution.py:23
  (1 shorter events, 0.0 us)
Async XLA Ops:
  0.0 10.6 %copy-start = (s32[4]{0:T(128)S(1)}, s32[4]{0:T(128)}, u32[]{:S(2)}) copy-start(s32[4]{0:T(128)} %refs_0_.3) | copy-start | bytes 52
  0.9 7.8 %collective-permute-start.2 = (bf16[32,512]{1,0:T(8,128)(2,1)S(1)}, bf16[32,512]{1,0:T(8,128)(2,1)S(1)}, u32[]{:S(2)}, u32[]{:S(2)}) collective-permute-start(bf16[32,512]{1,0:T(8,128)(2,1)S(1)} %convert_element_type.3.x_ref), channel_id=1, source_target_pairs={{0,4},{1,5},{2,6},{3,7},{4,0},{5,1},{6,2},{7,3},{8,25},{9,24},{10,... | collective-permute-start | bytes 98312 | tf_op jit(solution)/shard_map/ppermute | solution.py:229
  4.9 5.7 %collective-permute-start.1 = (bf16[32,512]{1,0:T(8,128)(2,1)S(1)}, bf16[32,512]{1,0:T(8,128)(2,1)S(1)}, u32[]{:S(2)}, u32[]{:S(2)}) collective-permute-start(bf16[32,512]{1,0:T(8,128)(2,1)S(1)} %convert_element_type.3.x_ref), channel_id=1, source_target_pairs={{0,6},{1,7},{2,4},{3,5},{4,2},{5,3},{6,0},{7,1},{8,24},{9,25},{10,... | collective-permute-start | bytes 98312 | tf_op jit(solution)/shard_map/ppermute | solution.py:229
  6.2 4.4 %collective-permute-start = (bf16[32,512]{1,0:T(8,128)(2,1)S(1)}, bf16[32,512]{1,0:T(8,128)(2,1)S(1)}, u32[]{:S(2)}, u32[]{:S(2)}) collective-permute-start(bf16[32,512]{1,0:T(8,128)(2,1)S(1)} %convert_element_type.3.x_ref), channel_id=1, source_target_pairs={{0,2},{1,3},{2,0},{3,1},{4,6},{5,7},{6,4},{7,5},{8,9},{9,8},{10,11... | collective-permute-start | bytes 98312 | tf_op jit(solution)/shard_map/ppermute | solution.py:229
  10.8 6.6 %collective-permute-start.5 = (bf16[128,512]{1,0:T(8,128)(2,1)S(1)}, bf16[128,512]{1,0:T(8,128)(2,1)S(1)}, u32[]{:S(2)}, u32[]{:S(2)}) collective-permute-start(bf16[128,512]{1,0:T(8,128)(2,1)S(1)} %shard_map.74.refs_0_), channel_id=1, source_target_pairs={{0,17},{1,16},{2,19},{3,18},{4,21},{5,20},{6,23},{7,22},{8,12},{9,... | collective-permute-start | bytes 393224 | tf_op jit(solution)/shard_map/ppermute | solution.py:229
  13.3 5.0 %collective-permute-start.4 = (bf16[128,512]{1,0:T(8,128)(2,1)S(1)}, bf16[128,512]{1,0:T(8,128)(2,1)S(1)}, u32[]{:S(2)}, u32[]{:S(2)}) collective-permute-start(bf16[128,512]{1,0:T(8,128)(2,1)S(1)} %shard_map.74.refs_0_), channel_id=1, source_target_pairs={{0,16},{1,17},{2,18},{3,19},{4,20},{5,21},{6,22},{7,23},{8,14},{9,... | collective-permute-start | bytes 393224 | tf_op jit(solution)/shard_map/ppermute | solution.py:229
  13.8 5.0 %collective-permute-start.3 = (bf16[128,512]{1,0:T(8,128)(2,1)S(1)}, bf16[128,512]{1,0:T(8,128)(2,1)S(1)}, u32[]{:S(2)}, u32[]{:S(2)}) collective-permute-start(bf16[128,512]{1,0:T(8,128)(2,1)S(1)} %shard_map.74.refs_0_), channel_id=1, source_target_pairs={{0,1},{1,0},{2,3},{3,2},{4,5},{5,4},{6,7},{7,6},{8,10},{9,11},{10,... | collective-permute-start | bytes 393224 | tf_op jit(solution)/shard_map/ppermute | solution.py:229
  17.4 1.4 %collective-permute-start.6 = (bf16[128,512]{1,0:T(8,128)(2,1)S(1)}, bf16[128,512]{1,0:T(8,128)(2,1)S(1)}, u32[]{:S(2)}, u32[]{:S(2)}) collective-permute-start(bf16[128,512]{1,0:T(8,128)(2,1)S(1)} %get-tuple-element.27.refs_0_), channel_id=1, source_target_pairs={{0,8},{1,9},{2,10},{3,11},{4,12},{5,13},{6,14},{7,15},{8,0},{9,1},... | collective-permute-start | bytes 393224 | tf_op jit(solution)/shard_map/ppermute | solution.py:234
  17.4 2.2 %collective-permute-start.9 = (bf16[128,512]{1,0:T(8,128)(2,1)S(1)}, bf16[128,512]{1,0:T(8,128)(2,1)S(1)}, u32[]{:S(2)}, u32[]{:S(2)}) collective-permute-start(bf16[128,512]{1,0:T(8,128)(2,1)S(1)} %collective-permute-done.5.refs_3_), channel_id=1, source_target_pairs={{0,8},{1,9},{2,10},{3,11},{4,12},{5,13},{6,14},{7,15},{8,0},{9,1},... | collective-permute-start | bytes 393224 | tf_op jit(solution)/shard_map/ppermute | solution.py:234
  18.2 1.4 %collective-permute-start.8 = (bf16[128,512]{1,0:T(8,128)(2,1)S(1)}, bf16[128,512]{1,0:T(8,128)(2,1)S(1)}, u32[]{:S(2)}, u32[]{:S(2)}) collective-permute-start(bf16[128,512]{1,0:T(8,128)(2,1)S(1)} %collective-permute-done.4.refs_2_), channel_id=1, source_target_pairs={{0,8},{1,9},{2,10},{3,11},{4,12},{5,13},{6,14},{7,15},{8,0},{9,1},... | collective-permute-start | bytes 393224 | tf_op jit(solution)/shard_map/ppermute | solution.py:234
  18.8 1.3 %collective-permute-start.7 = (bf16[128,512]{1,0:T(8,128)(2,1)S(1)}, bf16[128,512]{1,0:T(8,128)(2,1)S(1)}, u32[]{:S(2)}, u32[]{:S(2)}) collective-permute-start(bf16[128,512]{1,0:T(8,128)(2,1)S(1)} %collective-permute-done.3.refs_1_), channel_id=1, source_target_pairs={{0,8},{1,9},{2,10},{3,11},{4,12},{5,13},{6,14},{7,15},{8,0},{9,1},... | collective-permute-start | bytes 393224 | tf_op jit(solution)/shard_map/ppermute | solution.py:234
  20.7 4.9 %collective-permute-start.12 = (bf16[32,512]{1,0:T(8,128)(2,1)S(1)}, bf16[32,512]{1,0:T(8,128)(2,1)S(1)}, u32[]{:S(2)}, u32[]{:S(2)}) collective-permute-start(bf16[32,512]{1,0:T(8,128)(2,1)S(1)} %get-tuple-element.31.refs_0_), channel_id=1, source_target_pairs={{0,4},{1,5},{2,6},{3,7},{4,0},{5,1},{6,2},{7,3},{8,25},{9,24},{10,... | collective-permute-start | bytes 98312 | tf_op jit(solution)/shard_map/ppermute | solution.py:229
  22.0 5.7 %collective-permute-start.11 = (bf16[32,512]{1,0:T(8,128)(2,1)S(1)}, bf16[32,512]{1,0:T(8,128)(2,1)S(1)}, u32[]{:S(2)}, u32[]{:S(2)}) collective-permute-start(bf16[32,512]{1,0:T(8,128)(2,1)S(1)} %get-tuple-element.31.refs_0_), channel_id=1, source_target_pairs={{0,6},{1,7},{2,4},{3,5},{4,2},{5,3},{6,0},{7,1},{8,24},{9,25},{10,... | collective-permute-start | bytes 98312 | tf_op jit(solution)/shard_map/ppermute | solution.py:229
  23.0 4.7 %collective-permute-start.10 = (bf16[32,512]{1,0:T(8,128)(2,1)S(1)}, bf16[32,512]{1,0:T(8,128)(2,1)S(1)}, u32[]{:S(2)}, u32[]{:S(2)}) collective-permute-start(bf16[32,512]{1,0:T(8,128)(2,1)S(1)} %get-tuple-element.31.refs_0_), channel_id=1, source_target_pairs={{0,2},{1,3},{2,0},{3,1},{4,6},{5,7},{6,4},{7,5},{8,9},{9,8},{10,11... | collective-permute-start | bytes 98312 | tf_op jit(solution)/shard_map/ppermute | solution.py:229
  27.7 5.9 %collective-permute-start.15 = (bf16[128,512]{1,0:T(8,128)(2,1)S(1)}, bf16[128,512]{1,0:T(8,128)(2,1)S(1)}, u32[]{:S(2)}, u32[]{:S(2)}) collective-permute-start(bf16[128,512]{1,0:T(8,128)(2,1)S(1)} %shard_map.79.blocks_ref), channel_id=1, source_target_pairs={{0,17},{1,16},{2,19},{3,18},{4,21},{5,20},{6,23},{7,22},{8,12},{9,... | collective-permute-start | bytes 393224 | tf_op jit(solution)/shard_map/ppermute | solution.py:229
  29.7 5.0 %collective-permute-start.14 = (bf16[128,512]{1,0:T(8,128)(2,1)S(1)}, bf16[128,512]{1,0:T(8,128)(2,1)S(1)}, u32[]{:S(2)}, u32[]{:S(2)}) collective-permute-start(bf16[128,512]{1,0:T(8,128)(2,1)S(1)} %shard_map.79.blocks_ref), channel_id=1, source_target_pairs={{0,16},{1,17},{2,18},{3,19},{4,20},{5,21},{6,22},{7,23},{8,14},{9,... | collective-permute-start | bytes 393224 | tf_op jit(solution)/shard_map/ppermute | solution.py:229
  30.2 5.0 %collective-permute-start.13 = (bf16[128,512]{1,0:T(8,128)(2,1)S(1)}, bf16[128,512]{1,0:T(8,128)(2,1)S(1)}, u32[]{:S(2)}, u32[]{:S(2)}) collective-permute-start(bf16[128,512]{1,0:T(8,128)(2,1)S(1)} %shard_map.79.blocks_ref), channel_id=1, source_target_pairs={{0,1},{1,0},{2,3},{3,2},{4,5},{5,4},{6,7},{7,6},{8,10},{9,11},{10,... | collective-permute-start | bytes 393224 | tf_op jit(solution)/shard_map/ppermute | solution.py:229
  32.0 3.2 %collective-permute-start.16 = (bf16[128,512]{1,0:T(8,128)(2,1)S(1)}, bf16[128,512]{1,0:T(8,128)(2,1)S(1)}, u32[]{:S(2)}, u32[]{:S(2)}) collective-permute-start(bf16[128,512]{1,0:T(8,128)(2,1)S(1)} %get-tuple-element.33.refs_0_), channel_id=1, source_target_pairs={{0,8},{1,9},{2,10},{3,11},{4,12},{5,13},{6,14},{7,15},{8,0},{9,1},... | collective-permute-start | bytes 393224 | tf_op jit(solution)/shard_map/ppermute | solution.py:234
  33.6 2.4 %collective-permute-start.19 = (bf16[128,512]{1,0:T(8,128)(2,1)S(1)}, bf16[128,512]{1,0:T(8,128)(2,1)S(1)}, u32[]{:S(2)}, u32[]{:S(2)}) collective-permute-start(bf16[128,512]{1,0:T(8,128)(2,1)S(1)} %collective-permute-done.15.refs_3_), channel_id=1, source_target_pairs={{0,8},{1,9},{2,10},{3,11},{4,12},{5,13},{6,14},{7,15},{8,0},{9,1},... | collective-permute-start | bytes 393224 | tf_op jit(solution)/shard_map/ppermute | solution.py:234
  34.7 1.4 %collective-permute-start.18 = (bf16[128,512]{1,0:T(8,128)(2,1)S(1)}, bf16[128,512]{1,0:T(8,128)(2,1)S(1)}, u32[]{:S(2)}, u32[]{:S(2)}) collective-permute-start(bf16[128,512]{1,0:T(8,128)(2,1)S(1)} %collective-permute-done.14.refs_2_), channel_id=1, source_target_pairs={{0,8},{1,9},{2,10},{3,11},{4,12},{5,13},{6,14},{7,15},{8,0},{9,1},... | collective-permute-start | bytes 393224 | tf_op jit(solution)/shard_map/ppermute | solution.py:234
  35.2 1.3 %collective-permute-start.17 = (bf16[128,512]{1,0:T(8,128)(2,1)S(1)}, bf16[128,512]{1,0:T(8,128)(2,1)S(1)}, u32[]{:S(2)}, u32[]{:S(2)}) collective-permute-start(bf16[128,512]{1,0:T(8,128)(2,1)S(1)} %collective-permute-done.13.refs_1_), channel_id=1, source_target_pairs={{0,8},{1,9},{2,10},{3,11},{4,12},{5,13},{6,14},{7,15},{8,0},{9,1},... | collective-permute-start | bytes 393224 | tf_op jit(solution)/shard_map/ppermute | solution.py:234

commit v6 on v5

--- a/solution.py
+++ b/solution.py
@@ -76,8 +76,10 @@
     ]
     for move in moves:
         move.start()
-    w_moves = pieces(w_hbm, wide_ref, p_dev, w_sems)
     again_ref[...] = x_ref[...]
+    for p in range(p_dev):
+        for k in range(w_ref.shape[1]):
+            w_ref[p, k] = w_hbm[p, k].T
     for move in moves:
         move.wait()
     area, local = lax.axis_index("area"), lax.axis_index("local")
@@ -99,10 +101,6 @@
             place = jnp.where((away == by) & (held == 1), at, place)
     place = dc * len(places[0]) + place
     slots_ref[...] = place * p_dev + (inside & (p_dev - 1))
-    for p, move in enumerate(w_moves):
-        move.wait()
-        for k in range(w_ref.shape[1]):
-            w_ref[p, k] = wide_ref[p, k].T
 
 
 def count_of(counts_ref, area):
@@ -265,8 +263,8 @@
                     pltpu.VMEM(x.shape, x.dtype)
                     for x in (long_w, drive, columns, column)
                 ],
-                [column] + [in_hbm(x) for x in (columns, area_map, long_w, drive)],
-                [VMEM] + [HBM] * 4,
+                [column, in_hbm(columns), in_hbm(area_map), long_w, in_hbm(drive)],
+                [VMEM, HBM, HBM, VMEM, HBM],
                 0,
                 scratch=[
                     pltpu.VMEM(columns.shape, columns.dtype),

time: 37.9 us -> 37.9 us (level)
  waiting for transfers between devices: 10.4 us -> 12 us
  Pallas kernels: 9.46 us -> 8.22 us
  starting transfers between devices: 16.8 us -> 16.3 us
    ppermute x12, waiting for transfers between devices: 9.44 us -> 11 us  [swap(): lax.ppermute(x, AXES, [(i, i ^ far[i // locs % CORES]) for i in range(dev...]
    pallas_call x10, Pallas kernels: 9.46 us -> 8.22 us  [call(): pl.pallas_call(kernel, out_shape=out, in_specs=in_specs, out_specs=out_sp...]
    ppermute x8, starting transfers between devices: 0.54 us -> 0.04 us  [across(): return lax.ppermute(x, AXES, [(i, i ^ locs) for i in range(devices)])]
  transfers between devices with their start and end apart: 20 -> 20, of which waited for: 10 -> 11; matrix products, arithmetic and copies ran while one was open for 0% -> 0% of each run, Pallas kernels for 20% -> 17%
where the time goes in v6:
time: 37.9 us; the launch traced here: 37.7 us
  starting transfers between devices  16.3 us (43%)
  waiting for transfers between devices  12 us (32%)
  Pallas kernels  8.22 us (22%)
  other arithmetic  0.99 us (3%)
    ppermute x12, starting transfers between devices, swap(): lax.ppermute(x, AXES, [(i, i ^ far[i // locs % CORES]) for i in range(dev...  16.3 us
    ppermute x12, waiting for transfers between devices, swap(): lax.ppermute(x, AXES, [(i, i ^ far[i // locs % CORES]) for i in range(dev...  11 us
    pallas_call x10, Pallas kernels, call(): pl.pallas_call(kernel, out_shape=out, in_specs=in_specs, out_specs=out_sp...  8.22 us
    ppermute x8, waiting for transfers between devices, across(): return lax.ppermute(x, AXES, [(i, i ^ locs) for i in range(devices)])  1.01 us
    convert_element_type x1, other arithmetic, body(): mine = rates_init.astype(jnp.bfloat16)  0.99 us
  transfers between devices with their start and end apart: 20, of which 11 were waited for; matrix products, arithmetic and copies ran while one was open for 0% of the time, Pallas kernels for 17%

profile of v6, /device:TPU:0, one launch (start us, length us, event | category | flops | bytes accessed | tf_op | source)
XLA Modules:
  0.0 37.7 jit_solution(14360603680791297087)
XLA Ops:
  0.0 0.0 copy-start.1
  0.0 0.0 copy-start
  0.0 1.0 %convert_element_type.3.x_ref = bf16[32,512]{1,0:T(8,128)(2,1)S(1)} convert(f32[32,512]{1,0:T(8,128)} %param.7) | non-fusion elementwise | flops 16384 | bytes 98304 | tf_op jit(solution)/shard_map/convert_element_type | solution.py:234
  1.0 4.0 %collective-permute-start.2 = (bf16[32,512]{1,0:T(8,128)(2,1)S(1)}, bf16[32,512]{1,0:T(8,128)(2,1)S(1)}, u32[]{:S(2)}, u32[]{:S(2)}) collective-permute-start(bf16[32,512]{1,0:T(8,128)(2,1)S(1)} %convert_element_type.3.x_ref), channel_id=1, source_target_pairs={{0,4},{1,5},{2,6},{3,7},{4,0},{5,1},{6,2},{7,3},{8,25},{9,24},{10,... | collective-permute-start | bytes 98312 | tf_op jit(solution)/shard_map/ppermute | solution.py:227
  5.0 1.3 %collective-permute-start.1 = (bf16[32,512]{1,0:T(8,128)(2,1)S(1)}, bf16[32,512]{1,0:T(8,128)(2,1)S(1)}, u32[]{:S(2)}, u32[]{:S(2)}) collective-permute-start(bf16[32,512]{1,0:T(8,128)(2,1)S(1)} %convert_element_type.3.x_ref), channel_id=1, source_target_pairs={{0,6},{1,7},{2,4},{3,5},{4,2},{5,3},{6,0},{7,1},{8,24},{9,25},{10,... | collective-permute-start | bytes 98312 | tf_op jit(solution)/shard_map/ppermute | solution.py:227
  6.4 0.2 collective-permute-start
  6.6 2.2 %shard_map.73 = (bf16[512,4096]{1,0:T(8,128)(2,1)S(1)}, bf16[32,512]{1,0:T(8,128)(2,1)S(1)}) custom-call(bf16[32,512]{1,0:T(8,128)(2,1)S(1)} %convert_element_type.3.x_ref, bf16[512,4096]{1,0:T(8,128)(2,1)} %w_ref.1), custom_call_target="tpu_custom_call" | custom-call | bytes 4227072 | tf_op jit(solution)/shard_map/pallas_call | solution.py:23
  8.8 0.0 collective-permute-done.2.refs_3_
  8.8 1.9 %collective-permute-done.1.refs_2_ = bf16[32,512]{1,0:T(8,128)(2,1)S(1)} collective-permute-done((bf16[32,512]{1,0:T(8,128)(2,1)S(1)}, bf16[32,512]{1,0:T(8,128)(2,1)S(1)}, u32[]{:S(2)}, u32[]{:S(2)}) %collective-permute-start.1) | collective-permute-done | bytes 32800 | tf_op jit(solution)/shard_map/ppermute | solution.py:227
  10.8 0.0 collective-permute-done.refs_1_
  10.8 0.0 copy-done.1
  10.8 0.1 shard_map.74.refs_0_
  10.9 2.5 %collective-permute-start.5 = (bf16[128,512]{1,0:T(8,128)(2,1)S(1)}, bf16[128,512]{1,0:T(8,128)(2,1)S(1)}, u32[]{:S(2)}, u32[]{:S(2)}) collective-permute-start(bf16[128,512]{1,0:T(8,128)(2,1)S(1)} %shard_map.74.refs_0_), channel_id=1, source_target_pairs={{0,17},{1,16},{2,19},{3,18},{4,21},{5,20},{6,23},{7,22},{8,12},{9,... | collective-permute-start | bytes 393224 | tf_op jit(solution)/shard_map/ppermute | solution.py:227
  13.4 0.5 %collective-permute-start.4 = (bf16[128,512]{1,0:T(8,128)(2,1)S(1)}, bf16[128,512]{1,0:T(8,128)(2,1)S(1)}, u32[]{:S(2)}, u32[]{:S(2)}) collective-permute-start(bf16[128,512]{1,0:T(8,128)(2,1)S(1)} %shard_map.74.refs_0_), channel_id=1, source_target_pairs={{0,16},{1,17},{2,18},{3,19},{4,20},{5,21},{6,22},{7,23},{8,14},{9,... | collective-permute-start | bytes 393224 | tf_op jit(solution)/shard_map/ppermute | solution.py:227
  13.9 0.5 %collective-permute-start.3 = (bf16[128,512]{1,0:T(8,128)(2,1)S(1)}, bf16[128,512]{1,0:T(8,128)(2,1)S(1)}, u32[]{:S(2)}, u32[]{:S(2)}) collective-permute-start(bf16[128,512]{1,0:T(8,128)(2,1)S(1)} %shard_map.74.refs_0_), channel_id=1, source_target_pairs={{0,1},{1,0},{2,3},{3,2},{4,5},{5,4},{6,7},{7,6},{8,10},{9,11},{10,... | collective-permute-start | bytes 393224 | tf_op jit(solution)/shard_map/ppermute | solution.py:227
  14.5 0.0 copy-done
  14.5 1.1 %shard_map.75 = (bf16[4,16,128,128]{3,2,1,0:T(8,128)(2,1)S(1)}, f32[32,512]{1,0:T(8,128)S(1)}, s32[4,16]{1,0:T(4,128)S(1)}, bf16[128,512]{1,0:T(8,128)(2,1)S(1)}) custom-call(bf16[128,512]{1,0:T(8,128)(2,1)S(1)} %shard_map.74.refs_0_, s32[4,16]{1,0:T(4,128)} %refs_1_.1, s32[4]{0:T(128)} %refs_2_.1, bf16[4,16,128,128]{3,2,1,0:T(8,128)(2,1)S(1)} %copy-done, ...), custom_call_target="tpu_custom_call" | custom-call | bytes 2294032 | tf_op jit(solution)/shard_map/pallas_call | solution.py:23
  15.5 0.7 %shard_map.76 = (f32[32,512]{1,0:T(8,128)S(1)}, bf16[128,512]{1,0:T(8,128)(2,1)S(1)}) custom-call(bf16[128,512]{1,0:T(8,128)(2,1)S(1)} %get-tuple-element.25.blocks_ref, bf16[512,4096]{1,0:T(8,128)(2,1)S(1)} %get-tuple-element.24.w_ref), custom_call_target="tpu_custom_call" | custom-call | flops 67108864 | bytes 4325376 | tf_op jit(solution)/shard_map/pallas_call | solution.py:23
  16.3 0.0 collective-permute-start.6
  16.3 0.5 %collective-permute-done.5.refs_3_ = bf16[128,512]{1,0:T(8,128)(2,1)S(1)} collective-permute-done((bf16[128,512]{1,0:T(8,128)(2,1)S(1)}, bf16[128,512]{1,0:T(8,128)(2,1)S(1)}, u32[]{:S(2)}, u32[]{:S(2)}) %collective-permute-start.5) | collective-permute-done | bytes 131104 | tf_op jit(solution)/shard_map/ppermute | solution.py:227
  16.8 0.0 collective-permute-start.9
  16.8 1.5 %collective-permute-done.4.refs_2_ = bf16[128,512]{1,0:T(8,128)(2,1)S(1)} collective-permute-done((bf16[128,512]{1,0:T(8,128)(2,1)S(1)}, bf16[128,512]{1,0:T(8,128)(2,1)S(1)}, u32[]{:S(2)}, u32[]{:S(2)}) %collective-permute-start.4) | collective-permute-done | bytes 131104 | tf_op jit(solution)/shard_map/ppermute | solution.py:227
  18.4 0.0 collective-permute-start.8
  18.4 0.5 %collective-permute-done.3.refs_1_ = bf16[128,512]{1,0:T(8,128)(2,1)S(1)} collective-permute-done((bf16[128,512]{1,0:T(8,128)(2,1)S(1)}, bf16[128,512]{1,0:T(8,128)(2,1)S(1)}, u32[]{:S(2)}, u32[]{:S(2)}) %collective-permute-start.3) | collective-permute-done | bytes 131104 | tf_op jit(solution)/shard_map/ppermute | solution.py:227
  18.9 0.0 collective-permute-start.7
  18.9 0.0 collective-permute-done.6.refs_4_
  18.9 0.8 %shard_map.77 = (f32[32,512]{1,0:T(8,128)S(1)}, bf16[128,32,128]{2,1,0:T(8,128)(2,1)S(1)}) custom-call(bf16[512,4096]{1,0:T(8,128)(2,1)S(1)} %get-tuple-element.24.w_ref, f32[32,512]{1,0:T(8,128)S(1)} %get-tuple-element.26.start_ref, bf16[128,512]{1,0:T(8,128)(2,1)S(1)} %get-tuple-element.27.refs_0_, bf16[128,512]{1,0:T(8,128)(2,1)S(1)} %collective-permute-done.3.refs_1_, ...), custom_call_target="tpu_custom_call" | custom-call | flops 67108864 | bytes 4915200 | tf_op jit(solution)/shard_map/pallas_call | solution.py:23
  19.7 0.0 collective-permute-done.9.refs_7_
  19.8 0.0 collective-permute-done.8.refs_6_
  19.8 0.5 %collective-permute-done.7.refs_5_ = bf16[128,512]{1,0:T(8,128)(2,1)S(1)} collective-permute-done((bf16[128,512]{1,0:T(8,128)(2,1)S(1)}, bf16[128,512]{1,0:T(8,128)(2,1)S(1)}, u32[]{:S(2)}, u32[]{:S(2)}) %collective-permute-start.7) | collective-permute-done | bytes 131104 | tf_op jit(solution)/shard_map/ppermute | solution.py:232
  20.3 0.5 %shard_map.78 = (bf16[32,512]{1,0:T(8,128)(2,1)S(1)}, bf16[128,32,128]{2,1,0:T(8,128)(2,1)S(1)}) custom-call(s32[4]{0:T(128)S(1)} %copy-done.1, s32[4,16]{1,0:T(4,128)S(1)} %get-tuple-element.22.refs_1_, bf16[4,16,128,128]{3,2,1,0:T(8,128)(2,1)S(1)} %get-tuple-element.23.refs_2_, ...), custom_call_target="tpu_custom_call", output_to_operand_aliasing={{1}: (8, {})} | custom-call | flops 67108864 | bytes 3670288 | tf_op jit(solution)/shard_map/pallas_call | solution.py:23
  20.8 1.3 %collective-permute-start.12 = (bf16[32,512]{1,0:T(8,128)(2,1)S(1)}, bf16[32,512]{1,0:T(8,128)(2,1)S(1)}, u32[]{:S(2)}, u32[]{:S(2)}) collective-permute-start(bf16[32,512]{1,0:T(8,128)(2,1)S(1)} %get-tuple-element.31.refs_0_), channel_id=1, source_target_pairs={{0,4},{1,5},{2,6},{3,7},{4,0},{5,1},{6,2},{7,3},{8,25},{9,24},{10,... | collective-permute-start | bytes 98312 | tf_op jit(solution)/shard_map/ppermute | solution.py:227
  22.1 1.0 %collective-permute-start.11 = (bf16[32,512]{1,0:T(8,128)(2,1)S(1)}, bf16[32,512]{1,0:T(8,128)(2,1)S(1)}, u32[]{:S(2)}, u32[]{:S(2)}) collective-permute-start(bf16[32,512]{1,0:T(8,128)(2,1)S(1)} %get-tuple-element.31.refs_0_), channel_id=1, source_target_pairs={{0,6},{1,7},{2,4},{3,5},{4,2},{5,3},{6,0},{7,1},{8,24},{9,25},{10,... | collective-permute-start | bytes 98312 | tf_op jit(solution)/shard_map/ppermute | solution.py:227
  23.1 1.2 %collective-permute-start.10 = (bf16[32,512]{1,0:T(8,128)(2,1)S(1)}, bf16[32,512]{1,0:T(8,128)(2,1)S(1)}, u32[]{:S(2)}, u32[]{:S(2)}) collective-permute-start(bf16[32,512]{1,0:T(8,128)(2,1)S(1)} %get-tuple-element.31.refs_0_), channel_id=1, source_target_pairs={{0,2},{1,3},{2,0},{3,1},{4,6},{5,7},{6,4},{7,5},{8,9},{9,8},{10,11... | collective-permute-start | bytes 98312 | tf_op jit(solution)/shard_map/ppermute | solution.py:227
  24.4 1.3 %collective-permute-done.12.refs_3_ = bf16[32,512]{1,0:T(8,128)(2,1)S(1)} collective-permute-done((bf16[32,512]{1,0:T(8,128)(2,1)S(1)}, bf16[32,512]{1,0:T(8,128)(2,1)S(1)}, u32[]{:S(2)}, u32[]{:S(2)}) %collective-permute-start.12) | collective-permute-done | bytes 32800 | tf_op jit(solution)/shard_map/ppermute | solution.py:227
  25.7 2.1 %collective-permute-done.11.refs_2_ = bf16[32,512]{1,0:T(8,128)(2,1)S(1)} collective-permute-done((bf16[32,512]{1,0:T(8,128)(2,1)S(1)}, bf16[32,512]{1,0:T(8,128)(2,1)S(1)}, u32[]{:S(2)}, u32[]{:S(2)}) %collective-permute-start.11) | collective-permute-done | bytes 32800 | tf_op jit(solution)/shard_map/ppermute | solution.py:227
  27.8 0.0 collective-permute-done.10.refs_1_
  27.8 1.8 %collective-permute-start.15 = (bf16[128,512]{1,0:T(8,128)(2,1)S(1)}, bf16[128,512]{1,0:T(8,128)(2,1)S(1)}, u32[]{:S(2)}, u32[]{:S(2)}) collective-permute-start(bf16[128,512]{1,0:T(8,128)(2,1)S(1)} %shard_map.79.blocks_ref), channel_id=1, source_target_pairs={{0,17},{1,16},{2,19},{3,18},{4,21},{5,20},{6,23},{7,22},{8,12},{9,... | collective-permute-start | bytes 393224 | tf_op jit(solution)/shard_map/ppermute | solution.py:227
  29.7 0.5 %collective-permute-start.14 = (bf16[128,512]{1,0:T(8,128)(2,1)S(1)}, bf16[128,512]{1,0:T(8,128)(2,1)S(1)}, u32[]{:S(2)}, u32[]{:S(2)}) collective-permute-start(bf16[128,512]{1,0:T(8,128)(2,1)S(1)} %shard_map.79.blocks_ref), channel_id=1, source_target_pairs={{0,16},{1,17},{2,18},{3,19},{4,20},{5,21},{6,22},{7,23},{8,14},{9,... | collective-permute-start | bytes 393224 | tf_op jit(solution)/shard_map/ppermute | solution.py:227
  30.2 1.2 %collective-permute-start.13 = (bf16[128,512]{1,0:T(8,128)(2,1)S(1)}, bf16[128,512]{1,0:T(8,128)(2,1)S(1)}, u32[]{:S(2)}, u32[]{:S(2)}) collective-permute-start(bf16[128,512]{1,0:T(8,128)(2,1)S(1)} %shard_map.79.blocks_ref), channel_id=1, source_target_pairs={{0,1},{1,0},{2,3},{3,2},{4,5},{5,4},{6,7},{7,6},{8,10},{9,11},{10,... | collective-permute-start | bytes 393224 | tf_op jit(solution)/shard_map/ppermute | solution.py:227
  31.4 0.7 %shard_map.80 = (f32[32,512]{1,0:T(8,128)S(1)}, bf16[128,512]{1,0:T(8,128)(2,1)S(1)}) custom-call(bf16[128,512]{1,0:T(8,128)(2,1)S(1)} %shard_map.79.blocks_ref, bf16[512,4096]{1,0:T(8,128)(2,1)S(1)} %get-tuple-element.24.w_ref), custom_call_target="tpu_custom_call" | custom-call | flops 67108864 | bytes 4325376 | tf_op jit(solution)/shard_map/pallas_call | solution.py:23
  32.1 0.0 collective-permute-start.16
  32.1 1.6 %collective-permute-done.15.refs_3_ = bf16[128,512]{1,0:T(8,128)(2,1)S(1)} collective-permute-done((bf16[128,512]{1,0:T(8,128)(2,1)S(1)}, bf16[128,512]{1,0:T(8,128)(2,1)S(1)}, u32[]{:S(2)}, u32[]{:S(2)}) %collective-permute-start.15) | collective-permute-done | bytes 131104 | tf_op jit(solution)/shard_map/ppermute | solution.py:227
  33.8 0.0 collective-permute-start.19
  33.8 0.9 %collective-permute-done.14.refs_2_ = bf16[128,512]{1,0:T(8,128)(2,1)S(1)} collective-permute-done((bf16[128,512]{1,0:T(8,128)(2,1)S(1)}, bf16[128,512]{1,0:T(8,128)(2,1)S(1)}, u32[]{:S(2)}, u32[]{:S(2)}) %collective-permute-start.14) | collective-permute-done | bytes 131104 | tf_op jit(solution)/shard_map/ppermute | solution.py:227
  34.6 0.0 collective-permute-start.18
  34.6 0.5 %collective-permute-done.13.refs_1_ = bf16[128,512]{1,0:T(8,128)(2,1)S(1)} collective-permute-done((bf16[128,512]{1,0:T(8,128)(2,1)S(1)}, bf16[128,512]{1,0:T(8,128)(2,1)S(1)}, u32[]{:S(2)}, u32[]{:S(2)}) %collective-permute-start.13) | collective-permute-done | bytes 131104 | tf_op jit(solution)/shard_map/ppermute | solution.py:227
  35.2 0.0 collective-permute-start.17
  35.2 0.0 collective-permute-done.16.refs_4_
  35.2 0.8 %shard_map.81 = (f32[32,512]{1,0:T(8,128)S(1)}, bf16[128,32,128]{2,1,0:T(8,128)(2,1)S(1)}) custom-call(bf16[512,4096]{1,0:T(8,128)(2,1)S(1)} %get-tuple-element.24.w_ref, f32[32,512]{1,0:T(8,128)S(1)} %get-tuple-element.32.start_ref, bf16[128,512]{1,0:T(8,128)(2,1)S(1)} %get-tuple-element.33.refs_0_, bf16[128,512]{1,0:T(8,128)(2,1)S(1)} %collective-permute-done.13.refs_1_, ...), custom_call_target="tpu_custom_call" | custom-call | flops 67108864 | bytes 4915200 | tf_op jit(solution)/shard_map/pallas_call | solution.py:23
  36.0 0.0 collective-permute-done.19.refs_7_
  36.0 0.0 collective-permute-done.18.refs_6_
  36.0 0.5 %collective-permute-done.17.refs_5_ = bf16[128,512]{1,0:T(8,128)(2,1)S(1)} collective-permute-done((bf16[128,512]{1,0:T(8,128)(2,1)S(1)}, bf16[128,512]{1,0:T(8,128)(2,1)S(1)}, u32[]{:S(2)}, u32[]{:S(2)}) %collective-permute-start.17) | collective-permute-done | bytes 131104 | tf_op jit(solution)/shard_map/ppermute | solution.py:232
  36.5 1.2 %shard_map.82 = (f32[32,512]{1,0:T(8,128)}, bf16[128,32,128]{2,1,0:T(8,128)(2,1)S(1)}) custom-call(s32[4]{0:T(128)S(1)} %copy-done.1, s32[4,16]{1,0:T(4,128)S(1)} %get-tuple-element.22.refs_1_, bf16[4,16,128,128]{3,2,1,0:T(8,128)(2,1)S(1)} %get-tuple-element.23.refs_2_, f32[32,512]{1,0:T(8,128)S(1)} %get-tuple-element.34.refs_3_, ...), custom_call_target="tpu_custom_call", output_to_operand_aliasing={{1}: (8, {})} | custom-call | flops 67108864 | bytes 3670288 | tf_op jit(solution)/shard_map/pallas_call | solution.py:23
  (1 shorter events, 0.0 us)
Async XLA Ops:
  0.0 10.8 %copy-start.1 = (s32[4]{0:T(128)S(1)}, s32[4]{0:T(128)}, u32[]{:S(2)}) copy-start(s32[4]{0:T(128)} %refs_0_.3) | copy-start | bytes 52
  0.0 14.5 %copy-start = (bf16[4,16,128,128]{3,2,1,0:T(8,128)(2,1)S(1)}, bf16[4,16,128,128]{3,2,1,0:T(8,128)(2,1)}, u32[]{:S(2)}) copy-start(bf16[4,16,128,128]{3,2,1,0:T(8,128)(2,1)} %refs_3_.1) | copy-start | bytes 6291460
  1.0 7.8 %collective-permute-start.2 = (bf16[32,512]{1,0:T(8,128)(2,1)S(1)}, bf16[32,512]{1,0:T(8,128)(2,1)S(1)}, u32[]{:S(2)}, u32[]{:S(2)}) collective-permute-start(bf16[32,512]{1,0:T(8,128)(2,1)S(1)} %convert_element_type.3.x_ref), channel_id=1, source_target_pairs={{0,4},{1,5},{2,6},{3,7},{4,0},{5,1},{6,2},{7,3},{8,25},{9,24},{10,... | collective-permute-start | bytes 98312 | tf_op jit(solution)/shard_map/ppermute | solution.py:227
  5.0 5.7 %collective-permute-start.1 = (bf16[32,512]{1,0:T(8,128)(2,1)S(1)}, bf16[32,512]{1,0:T(8,128)(2,1)S(1)}, u32[]{:S(2)}, u32[]{:S(2)}) collective-permute-start(bf16[32,512]{1,0:T(8,128)(2,1)S(1)} %convert_element_type.3.x_ref), channel_id=1, source_target_pairs={{0,6},{1,7},{2,4},{3,5},{4,2},{5,3},{6,0},{7,1},{8,24},{9,25},{10,... | collective-permute-start | bytes 98312 | tf_op jit(solution)/shard_map/ppermute | solution.py:227
  6.4 4.4 %collective-permute-start = (bf16[32,512]{1,0:T(8,128)(2,1)S(1)}, bf16[32,512]{1,0:T(8,128)(2,1)S(1)}, u32[]{:S(2)}, u32[]{:S(2)}) collective-permute-start(bf16[32,512]{1,0:T(8,128)(2,1)S(1)} %convert_element_type.3.x_ref), channel_id=1, source_target_pairs={{0,2},{1,3},{2,0},{3,1},{4,6},{5,7},{6,4},{7,5},{8,9},{9,8},{10,11... | collective-permute-start | bytes 98312 | tf_op jit(solution)/shard_map/ppermute | solution.py:227
  10.9 5.9 %collective-permute-start.5 = (bf16[128,512]{1,0:T(8,128)(2,1)S(1)}, bf16[128,512]{1,0:T(8,128)(2,1)S(1)}, u32[]{:S(2)}, u32[]{:S(2)}) collective-permute-start(bf16[128,512]{1,0:T(8,128)(2,1)S(1)} %shard_map.74.refs_0_), channel_id=1, source_target_pairs={{0,17},{1,16},{2,19},{3,18},{4,21},{5,20},{6,23},{7,22},{8,12},{9,... | collective-permute-start | bytes 393224 | tf_op jit(solution)/shard_map/ppermute | solution.py:227
  13.4 5.0 %collective-permute-start.4 = (bf16[128,512]{1,0:T(8,128)(2,1)S(1)}, bf16[128,512]{1,0:T(8,128)(2,1)S(1)}, u32[]{:S(2)}, u32[]{:S(2)}) collective-permute-start(bf16[128,512]{1,0:T(8,128)(2,1)S(1)} %shard_map.74.refs_0_), channel_id=1, source_target_pairs={{0,16},{1,17},{2,18},{3,19},{4,20},{5,21},{6,22},{7,23},{8,14},{9,... | collective-permute-start | bytes 393224 | tf_op jit(solution)/shard_map/ppermute | solution.py:227
  13.9 5.0 %collective-permute-start.3 = (bf16[128,512]{1,0:T(8,128)(2,1)S(1)}, bf16[128,512]{1,0:T(8,128)(2,1)S(1)}, u32[]{:S(2)}, u32[]{:S(2)}) collective-permute-start(bf16[128,512]{1,0:T(8,128)(2,1)S(1)} %shard_map.74.refs_0_), channel_id=1, source_target_pairs={{0,1},{1,0},{2,3},{3,2},{4,5},{5,4},{6,7},{7,6},{8,10},{9,11},{10,... | collective-permute-start | bytes 393224 | tf_op jit(solution)/shard_map/ppermute | solution.py:227
  16.3 2.7 %collective-permute-start.6 = (bf16[128,512]{1,0:T(8,128)(2,1)S(1)}, bf16[128,512]{1,0:T(8,128)(2,1)S(1)}, u32[]{:S(2)}, u32[]{:S(2)}) collective-permute-start(bf16[128,512]{1,0:T(8,128)(2,1)S(1)} %get-tuple-element.27.refs_0_), channel_id=1, source_target_pairs={{0,8},{1,9},{2,10},{3,11},{4,12},{5,13},{6,14},{7,15},{8,0},{9,1},... | collective-permute-start | bytes 393224 | tf_op jit(solution)/shard_map/ppermute | solution.py:232
  16.8 2.9 %collective-permute-start.9 = (bf16[128,512]{1,0:T(8,128)(2,1)S(1)}, bf16[128,512]{1,0:T(8,128)(2,1)S(1)}, u32[]{:S(2)}, u32[]{:S(2)}) collective-permute-start(bf16[128,512]{1,0:T(8,128)(2,1)S(1)} %collective-permute-done.5.refs_3_), channel_id=1, source_target_pairs={{0,8},{1,9},{2,10},{3,11},{4,12},{5,13},{6,14},{7,15},{8,0},{9,1},... | collective-permute-start | bytes 393224 | tf_op jit(solution)/shard_map/ppermute | solution.py:232
  18.4 1.4 %collective-permute-start.8 = (bf16[128,512]{1,0:T(8,128)(2,1)S(1)}, bf16[128,512]{1,0:T(8,128)(2,1)S(1)}, u32[]{:S(2)}, u32[]{:S(2)}) collective-permute-start(bf16[128,512]{1,0:T(8,128)(2,1)S(1)} %collective-permute-done.4.refs_2_), channel_id=1, source_target_pairs={{0,8},{1,9},{2,10},{3,11},{4,12},{5,13},{6,14},{7,15},{8,0},{9,1},... | collective-permute-start | bytes 393224 | tf_op jit(solution)/shard_map/ppermute | solution.py:232
  18.9 1.3 %collective-permute-start.7 = (bf16[128,512]{1,0:T(8,128)(2,1)S(1)}, bf16[128,512]{1,0:T(8,128)(2,1)S(1)}, u32[]{:S(2)}, u32[]{:S(2)}) collective-permute-start(bf16[128,512]{1,0:T(8,128)(2,1)S(1)} %collective-permute-done.3.refs_1_), channel_id=1, source_target_pairs={{0,8},{1,9},{2,10},{3,11},{4,12},{5,13},{6,14},{7,15},{8,0},{9,1},... | collective-permute-start | bytes 393224 | tf_op jit(solution)/shard_map/ppermute | solution.py:232
  20.8 4.9 %collective-permute-start.12 = (bf16[32,512]{1,0:T(8,128)(2,1)S(1)}, bf16[32,512]{1,0:T(8,128)(2,1)S(1)}, u32[]{:S(2)}, u32[]{:S(2)}) collective-permute-start(bf16[32,512]{1,0:T(8,128)(2,1)S(1)} %get-tuple-element.31.refs_0_), channel_id=1, source_target_pairs={{0,4},{1,5},{2,6},{3,7},{4,0},{5,1},{6,2},{7,3},{8,25},{9,24},{10,... | collective-permute-start | bytes 98312 | tf_op jit(solution)/shard_map/ppermute | solution.py:227
  22.1 5.7 %collective-permute-start.11 = (bf16[32,512]{1,0:T(8,128)(2,1)S(1)}, bf16[32,512]{1,0:T(8,128)(2,1)S(1)}, u32[]{:S(2)}, u32[]{:S(2)}) collective-permute-start(bf16[32,512]{1,0:T(8,128)(2,1)S(1)} %get-tuple-element.31.refs_0_), channel_id=1, source_target_pairs={{0,6},{1,7},{2,4},{3,5},{4,2},{5,3},{6,0},{7,1},{8,24},{9,25},{10,... | collective-permute-start | bytes 98312 | tf_op jit(solution)/shard_map/ppermute | solution.py:227
  23.1 4.7 %collective-permute-start.10 = (bf16[32,512]{1,0:T(8,128)(2,1)S(1)}, bf16[32,512]{1,0:T(8,128)(2,1)S(1)}, u32[]{:S(2)}, u32[]{:S(2)}) collective-permute-start(bf16[32,512]{1,0:T(8,128)(2,1)S(1)} %get-tuple-element.31.refs_0_), channel_id=1, source_target_pairs={{0,2},{1,3},{2,0},{3,1},{4,6},{5,7},{6,4},{7,5},{8,9},{9,8},{10,11... | collective-permute-start | bytes 98312 | tf_op jit(solution)/shard_map/ppermute | solution.py:227
  27.8 5.9 %collective-permute-start.15 = (bf16[128,512]{1,0:T(8,128)(2,1)S(1)}, bf16[128,512]{1,0:T(8,128)(2,1)S(1)}, u32[]{:S(2)}, u32[]{:S(2)}) collective-permute-start(bf16[128,512]{1,0:T(8,128)(2,1)S(1)} %shard_map.79.blocks_ref), channel_id=1, source_target_pairs={{0,17},{1,16},{2,19},{3,18},{4,21},{5,20},{6,23},{7,22},{8,12},{9,... | collective-permute-start | bytes 393224 | tf_op jit(solution)/shard_map/ppermute | solution.py:227
  29.7 5.0 %collective-permute-start.14 = (bf16[128,512]{1,0:T(8,128)(2,1)S(1)}, bf16[128,512]{1,0:T(8,128)(2,1)S(1)}, u32[]{:S(2)}, u32[]{:S(2)}) collective-permute-start(bf16[128,512]{1,0:T(8,128)(2,1)S(1)} %shard_map.79.blocks_ref), channel_id=1, source_target_pairs={{0,16},{1,17},{2,18},{3,19},{4,20},{5,21},{6,22},{7,23},{8,14},{9,... | collective-permute-start | bytes 393224 | tf_op jit(solution)/shard_map/ppermute | solution.py:227
  30.2 5.0 %collective-permute-start.13 = (bf16[128,512]{1,0:T(8,128)(2,1)S(1)}, bf16[128,512]{1,0:T(8,128)(2,1)S(1)}, u32[]{:S(2)}, u32[]{:S(2)}) collective-permute-start(bf16[128,512]{1,0:T(8,128)(2,1)S(1)} %shard_map.79.blocks_ref), channel_id=1, source_target_pairs={{0,1},{1,0},{2,3},{3,2},{4,5},{5,4},{6,7},{7,6},{8,10},{9,11},{10,... | collective-permute-start | bytes 393224 | tf_op jit(solution)/shard_map/ppermute | solution.py:227
  32.1 3.1 %collective-permute-start.16 = (bf16[128,512]{1,0:T(8,128)(2,1)S(1)}, bf16[128,512]{1,0:T(8,128)(2,1)S(1)}, u32[]{:S(2)}, u32[]{:S(2)}) collective-permute-start(bf16[128,512]{1,0:T(8,128)(2,1)S(1)} %get-tuple-element.33.refs_0_), channel_id=1, source_target_pairs={{0,8},{1,9},{2,10},{3,11},{4,12},{5,13},{6,14},{7,15},{8,0},{9,1},... | collective-permute-start | bytes 393224 | tf_op jit(solution)/shard_map/ppermute | solution.py:232
  33.8 2.3 %collective-permute-start.19 = (bf16[128,512]{1,0:T(8,128)(2,1)S(1)}, bf16[128,512]{1,0:T(8,128)(2,1)S(1)}, u32[]{:S(2)}, u32[]{:S(2)}) collective-permute-start(bf16[128,512]{1,0:T(8,128)(2,1)S(1)} %collective-permute-done.15.refs_3_), channel_id=1, source_target_pairs={{0,8},{1,9},{2,10},{3,11},{4,12},{5,13},{6,14},{7,15},{8,0},{9,1},... | collective-permute-start | bytes 393224 | tf_op jit(solution)/shard_map/ppermute | solution.py:232
  34.6 1.4 %collective-permute-start.18 = (bf16[128,512]{1,0:T(8,128)(2,1)S(1)}, bf16[128,512]{1,0:T(8,128)(2,1)S(1)}, u32[]{:S(2)}, u32[]{:S(2)}) collective-permute-start(bf16[128,512]{1,0:T(8,128)(2,1)S(1)} %collective-permute-done.14.refs_2_), channel_id=1, source_target_pairs={{0,8},{1,9},{2,10},{3,11},{4,12},{5,13},{6,14},{7,15},{8,0},{9,1},... | collective-permute-start | bytes 393224 | tf_op jit(solution)/shard_map/ppermute | solution.py:232
  35.2 1.3 %collective-permute-start.17 = (bf16[128,512]{1,0:T(8,128)(2,1)S(1)}, bf16[128,512]{1,0:T(8,128)(2,1)S(1)}, u32[]{:S(2)}, u32[]{:S(2)}) collective-permute-start(bf16[128,512]{1,0:T(8,128)(2,1)S(1)} %collective-permute-done.13.refs_1_), channel_id=1, source_target_pairs={{0,8},{1,9},{2,10},{3,11},{4,12},{5,13},{6,14},{7,15},{8,0},{9,1},... | collective-permute-start | bytes 393224 | tf_op jit(solution)/shard_map/ppermute | solution.py:232

commit v7 on v5

--- a/solution.py
+++ b/solution.py
@@ -78,6 +78,10 @@
         move.start()
     w_moves = pieces(w_hbm, wide_ref, p_dev, w_sems)
     again_ref[...] = x_ref[...]
+    for p, move in enumerate(w_moves):
+        move.wait()
+        for k in range(w_ref.shape[1]):
+            w_ref[p, k] = wide_ref[p, k].T
     for move in moves:
         move.wait()
     area, local = lax.axis_index("area"), lax.axis_index("local")
@@ -99,10 +103,6 @@
             place = jnp.where((away == by) & (held == 1), at, place)
     place = dc * len(places[0]) + place
     slots_ref[...] = place * p_dev + (inside & (p_dev - 1))
-    for p, move in enumerate(w_moves):
-        move.wait()
-        for k in range(w_ref.shape[1]):
-            w_ref[p, k] = wide_ref[p, k].T
 
 
 def count_of(counts_ref, area):

time: 37.9 us -> 37.7 us (level)
  no operation moved by 1% of the time
where the time goes in v7:
time: 37.7 us; the launch traced here: 37.5 us
  starting transfers between devices  16.8 us (45%)
  waiting for transfers between devices  10.6 us (28%)
  Pallas kernels  9.15 us (24%)
  other arithmetic  0.86 us (2%)
    ppermute x12, starting transfers between devices, swap(): lax.ppermute(x, AXES, [(i, i ^ far[i // locs % CORES]) for i in range(dev...  16.3 us
    ppermute x12, waiting for transfers between devices, swap(): lax.ppermute(x, AXES, [(i, i ^ far[i // locs % CORES]) for i in range(dev...  9.58 us
    pallas_call x10, Pallas kernels, call(): pl.pallas_call(kernel, out_shape=out, in_specs=in_specs, out_specs=out_sp...  9.15 us
    ppermute x8, waiting for transfers between devices, across(): return lax.ppermute(x, AXES, [(i, i ^ locs) for i in range(devices)])  1.01 us
    convert_element_type x1, other arithmetic, body(): mine = rates_init.astype(jnp.bfloat16)  0.86 us
  transfers between devices with their start and end apart: 20, of which 10 were waited for; matrix products, arithmetic and copies ran while one was open for 0% of the time, Pallas kernels for 20%

profile of v7, /device:TPU:0, one launch (start us, length us, event | category | flops | bytes accessed | tf_op | source)
XLA Modules:
  0.0 37.5 jit_solution(9878569635506181240)
XLA Ops:
  0.0 0.0 copy-start
  0.0 0.9 %convert_element_type.3.x_ref = bf16[32,512]{1,0:T(8,128)(2,1)S(1)} convert(f32[32,512]{1,0:T(8,128)} %param.7) | non-fusion elementwise | flops 16384 | bytes 98304 | tf_op jit(solution)/shard_map/convert_element_type | solution.py:236
  0.9 4.0 %collective-permute-start.2 = (bf16[32,512]{1,0:T(8,128)(2,1)S(1)}, bf16[32,512]{1,0:T(8,128)(2,1)S(1)}, u32[]{:S(2)}, u32[]{:S(2)}) collective-permute-start(bf16[32,512]{1,0:T(8,128)(2,1)S(1)} %convert_element_type.3.x_ref), channel_id=1, source_target_pairs={{0,4},{1,5},{2,6},{3,7},{4,0},{5,1},{6,2},{7,3},{8,25},{9,24},{10,... | collective-permute-start | bytes 98312 | tf_op jit(solution)/shard_map/ppermute | solution.py:229
  4.9 1.3 %collective-permute-start.1 = (bf16[32,512]{1,0:T(8,128)(2,1)S(1)}, bf16[32,512]{1,0:T(8,128)(2,1)S(1)}, u32[]{:S(2)}, u32[]{:S(2)}) collective-permute-start(bf16[32,512]{1,0:T(8,128)(2,1)S(1)} %convert_element_type.3.x_ref), channel_id=1, source_target_pairs={{0,6},{1,7},{2,4},{3,5},{4,2},{5,3},{6,0},{7,1},{8,24},{9,25},{10,... | collective-permute-start | bytes 98312 | tf_op jit(solution)/shard_map/ppermute | solution.py:229
  6.2 0.2 collective-permute-start
  6.5 2.2 %shard_map.73 = (bf16[512,4096]{1,0:T(8,128)(2,1)S(1)}, bf16[32,512]{1,0:T(8,128)(2,1)S(1)}) custom-call(bf16[32,512]{1,0:T(8,128)(2,1)S(1)} %convert_element_type.3.x_ref, bf16[512,4096]{1,0:T(8,128)(2,1)} %w_ref.1), custom_call_target="tpu_custom_call" | custom-call | bytes 4227072 | tf_op jit(solution)/shard_map/pallas_call | solution.py:23
  8.7 0.0 collective-permute-done.2.refs_3_
  8.7 1.9 %collective-permute-done.1.refs_2_ = bf16[32,512]{1,0:T(8,128)(2,1)S(1)} collective-permute-done((bf16[32,512]{1,0:T(8,128)(2,1)S(1)}, bf16[32,512]{1,0:T(8,128)(2,1)S(1)}, u32[]{:S(2)}, u32[]{:S(2)}) %collective-permute-start.1) | collective-permute-done | bytes 32800 | tf_op jit(solution)/shard_map/ppermute | solution.py:229
  10.6 0.0 collective-permute-done.refs_1_
  10.6 0.0 copy-done
  10.6 0.1 shard_map.74.refs_0_
  10.8 2.5 %collective-permute-start.5 = (bf16[128,512]{1,0:T(8,128)(2,1)S(1)}, bf16[128,512]{1,0:T(8,128)(2,1)S(1)}, u32[]{:S(2)}, u32[]{:S(2)}) collective-permute-start(bf16[128,512]{1,0:T(8,128)(2,1)S(1)} %shard_map.74.refs_0_), channel_id=1, source_target_pairs={{0,17},{1,16},{2,19},{3,18},{4,21},{5,20},{6,23},{7,22},{8,12},{9,... | collective-permute-start | bytes 393224 | tf_op jit(solution)/shard_map/ppermute | solution.py:229
  13.3 0.5 %collective-permute-start.4 = (bf16[128,512]{1,0:T(8,128)(2,1)S(1)}, bf16[128,512]{1,0:T(8,128)(2,1)S(1)}, u32[]{:S(2)}, u32[]{:S(2)}) collective-permute-start(bf16[128,512]{1,0:T(8,128)(2,1)S(1)} %shard_map.74.refs_0_), channel_id=1, source_target_pairs={{0,16},{1,17},{2,18},{3,19},{4,20},{5,21},{6,22},{7,23},{8,14},{9,... | collective-permute-start | bytes 393224 | tf_op jit(solution)/shard_map/ppermute | solution.py:229
  13.8 0.5 %collective-permute-start.3 = (bf16[128,512]{1,0:T(8,128)(2,1)S(1)}, bf16[128,512]{1,0:T(8,128)(2,1)S(1)}, u32[]{:S(2)}, u32[]{:S(2)}) collective-permute-start(bf16[128,512]{1,0:T(8,128)(2,1)S(1)} %shard_map.74.refs_0_), channel_id=1, source_target_pairs={{0,1},{1,0},{2,3},{3,2},{4,5},{5,4},{6,7},{7,6},{8,10},{9,11},{10,... | collective-permute-start | bytes 393224 | tf_op jit(solution)/shard_map/ppermute | solution.py:229
  14.3 2.0 %shard_map.75 = (bf16[4,16,128,128]{3,2,1,0:T(8,128)(2,1)S(1)}, f32[32,512]{1,0:T(8,128)S(1)}, s32[4,16]{1,0:T(4,128)S(1)}, bf16[128,512]{1,0:T(8,128)(2,1)S(1)}) custom-call(bf16[128,512]{1,0:T(8,128)(2,1)S(1)} %shard_map.74.refs_0_, s32[4,16]{1,0:T(4,128)} %refs_1_.1, s32[4]{0:T(128)} %refs_2_.1, bf16[4,16,128,128]{3,2,1,0:T(8,128)(2,1)} %refs_3_.1, ...), custom_call_target="tpu_custom_call" | custom-call | bytes 2294032 | tf_op jit(solution)/shard_map/pallas_call | solution.py:23
  16.3 0.7 %shard_map.76 = (f32[32,512]{1,0:T(8,128)S(1)}, bf16[128,512]{1,0:T(8,128)(2,1)S(1)}) custom-call(bf16[128,512]{1,0:T(8,128)(2,1)S(1)} %get-tuple-element.25.blocks_ref, bf16[512,4096]{1,0:T(8,128)(2,1)S(1)} %get-tuple-element.24.w_ref), custom_call_target="tpu_custom_call" | custom-call | flops 67108864 | bytes 4325376 | tf_op jit(solution)/shard_map/pallas_call | solution.py:23
  17.1 0.0 collective-permute-start.6
  17.1 0.0 collective-permute-done.5.refs_3_
  17.1 0.5 %collective-permute-start.9 = (bf16[128,512]{1,0:T(8,128)(2,1)S(1)}, bf16[128,512]{1,0:T(8,128)(2,1)S(1)}, u32[]{:S(2)}, u32[]{:S(2)}) collective-permute-start(bf16[128,512]{1,0:T(8,128)(2,1)S(1)} %collective-permute-done.5.refs_3_), channel_id=1, source_target_pairs={{0,8},{1,9},{2,10},{3,11},{4,12},{5,13},{6,14},{7,15},{8,0},{9,1},... | collective-permute-start | bytes 393224 | tf_op jit(solution)/shard_map/ppermute | solution.py:234
  17.6 0.6 %collective-permute-done.4.refs_2_ = bf16[128,512]{1,0:T(8,128)(2,1)S(1)} collective-permute-done((bf16[128,512]{1,0:T(8,128)(2,1)S(1)}, bf16[128,512]{1,0:T(8,128)(2,1)S(1)}, u32[]{:S(2)}, u32[]{:S(2)}) %collective-permute-start.4) | collective-permute-done | bytes 131104 | tf_op jit(solution)/shard_map/ppermute | solution.py:229
  18.2 0.0 collective-permute-start.8
  18.2 0.5 %collective-permute-done.3.refs_1_ = bf16[128,512]{1,0:T(8,128)(2,1)S(1)} collective-permute-done((bf16[128,512]{1,0:T(8,128)(2,1)S(1)}, bf16[128,512]{1,0:T(8,128)(2,1)S(1)}, u32[]{:S(2)}, u32[]{:S(2)}) %collective-permute-start.3) | collective-permute-done | bytes 131104 | tf_op jit(solution)/shard_map/ppermute | solution.py:229
  18.8 0.0 collective-permute-start.7
  18.8 0.0 collective-permute-done.6.refs_4_
  18.8 0.8 %shard_map.77 = (f32[32,512]{1,0:T(8,128)S(1)}, bf16[128,32,128]{2,1,0:T(8,128)(2,1)S(1)}) custom-call(bf16[512,4096]{1,0:T(8,128)(2,1)S(1)} %get-tuple-element.24.w_ref, f32[32,512]{1,0:T(8,128)S(1)} %get-tuple-element.26.start_ref, bf16[128,512]{1,0:T(8,128)(2,1)S(1)} %get-tuple-element.27.refs_0_, bf16[128,512]{1,0:T(8,128)(2,1)S(1)} %collective-permute-done.3.refs_1_, ...), custom_call_target="tpu_custom_call" | custom-call | flops 67108864 | bytes 4915200 | tf_op jit(solution)/shard_map/pallas_call | solution.py:23
  19.6 0.0 collective-permute-done.9.refs_7_
  19.6 0.0 collective-permute-done.8.refs_6_
  19.6 0.5 %collective-permute-done.7.refs_5_ = bf16[128,512]{1,0:T(8,128)(2,1)S(1)} collective-permute-done((bf16[128,512]{1,0:T(8,128)(2,1)S(1)}, bf16[128,512]{1,0:T(8,128)(2,1)S(1)}, u32[]{:S(2)}, u32[]{:S(2)}) %collective-permute-start.7) | collective-permute-done | bytes 131104 | tf_op jit(solution)/shard_map/ppermute | solution.py:234
  20.1 0.5 %shard_map.78 = (bf16[32,512]{1,0:T(8,128)(2,1)S(1)}, bf16[128,32,128]{2,1,0:T(8,128)(2,1)S(1)}) custom-call(s32[4]{0:T(128)S(1)} %copy-done, s32[4,16]{1,0:T(4,128)S(1)} %get-tuple-element.22.refs_1_, bf16[4,16,128,128]{3,2,1,0:T(8,128)(2,1)S(1)} %get-tuple-element.23.refs_2_, ...), custom_call_target="tpu_custom_call", output_to_operand_aliasing={{1}: (8, {})} | custom-call | flops 67108864 | bytes 3670288 | tf_op jit(solution)/shard_map/pallas_call | solution.py:23
  20.7 1.3 %collective-permute-start.12 = (bf16[32,512]{1,0:T(8,128)(2,1)S(1)}, bf16[32,512]{1,0:T(8,128)(2,1)S(1)}, u32[]{:S(2)}, u32[]{:S(2)}) collective-permute-start(bf16[32,512]{1,0:T(8,128)(2,1)S(1)} %get-tuple-element.31.refs_0_), channel_id=1, source_target_pairs={{0,4},{1,5},{2,6},{3,7},{4,0},{5,1},{6,2},{7,3},{8,25},{9,24},{10,... | collective-permute-start | bytes 98312 | tf_op jit(solution)/shard_map/ppermute | solution.py:229
  22.0 1.0 %collective-permute-start.11 = (bf16[32,512]{1,0:T(8,128)(2,1)S(1)}, bf16[32,512]{1,0:T(8,128)(2,1)S(1)}, u32[]{:S(2)}, u32[]{:S(2)}) collective-permute-start(bf16[32,512]{1,0:T(8,128)(2,1)S(1)} %get-tuple-element.31.refs_0_), channel_id=1, source_target_pairs={{0,6},{1,7},{2,4},{3,5},{4,2},{5,3},{6,0},{7,1},{8,24},{9,25},{10,... | collective-permute-start | bytes 98312 | tf_op jit(solution)/shard_map/ppermute | solution.py:229
  23.0 1.2 %collective-permute-start.10 = (bf16[32,512]{1,0:T(8,128)(2,1)S(1)}, bf16[32,512]{1,0:T(8,128)(2,1)S(1)}, u32[]{:S(2)}, u32[]{:S(2)}) collective-permute-start(bf16[32,512]{1,0:T(8,128)(2,1)S(1)} %get-tuple-element.31.refs_0_), channel_id=1, source_target_pairs={{0,2},{1,3},{2,0},{3,1},{4,6},{5,7},{6,4},{7,5},{8,9},{9,8},{10,11... | collective-permute-start | bytes 98312 | tf_op jit(solution)/shard_map/ppermute | solution.py:229
  24.2 1.3 %collective-permute-done.12.refs_3_ = bf16[32,512]{1,0:T(8,128)(2,1)S(1)} collective-permute-done((bf16[32,512]{1,0:T(8,128)(2,1)S(1)}, bf16[32,512]{1,0:T(8,128)(2,1)S(1)}, u32[]{:S(2)}, u32[]{:S(2)}) %collective-permute-start.12) | collective-permute-done | bytes 32800 | tf_op jit(solution)/shard_map/ppermute | solution.py:229
  25.5 2.1 %collective-permute-done.11.refs_2_ = bf16[32,512]{1,0:T(8,128)(2,1)S(1)} collective-permute-done((bf16[32,512]{1,0:T(8,128)(2,1)S(1)}, bf16[32,512]{1,0:T(8,128)(2,1)S(1)}, u32[]{:S(2)}, u32[]{:S(2)}) %collective-permute-start.11) | collective-permute-done | bytes 32800 | tf_op jit(solution)/shard_map/ppermute | solution.py:229
  27.7 0.0 collective-permute-done.10.refs_1_
  27.7 1.8 %collective-permute-start.15 = (bf16[128,512]{1,0:T(8,128)(2,1)S(1)}, bf16[128,512]{1,0:T(8,128)(2,1)S(1)}, u32[]{:S(2)}, u32[]{:S(2)}) collective-permute-start(bf16[128,512]{1,0:T(8,128)(2,1)S(1)} %shard_map.79.blocks_ref), channel_id=1, source_target_pairs={{0,17},{1,16},{2,19},{3,18},{4,21},{5,20},{6,23},{7,22},{8,12},{9,... | collective-permute-start | bytes 393224 | tf_op jit(solution)/shard_map/ppermute | solution.py:229
  29.5 0.5 %collective-permute-start.14 = (bf16[128,512]{1,0:T(8,128)(2,1)S(1)}, bf16[128,512]{1,0:T(8,128)(2,1)S(1)}, u32[]{:S(2)}, u32[]{:S(2)}) collective-permute-start(bf16[128,512]{1,0:T(8,128)(2,1)S(1)} %shard_map.79.blocks_ref), channel_id=1, source_target_pairs={{0,16},{1,17},{2,18},{3,19},{4,20},{5,21},{6,22},{7,23},{8,14},{9,... | collective-permute-start | bytes 393224 | tf_op jit(solution)/shard_map/ppermute | solution.py:229
  30.1 1.2 %collective-permute-start.13 = (bf16[128,512]{1,0:T(8,128)(2,1)S(1)}, bf16[128,512]{1,0:T(8,128)(2,1)S(1)}, u32[]{:S(2)}, u32[]{:S(2)}) collective-permute-start(bf16[128,512]{1,0:T(8,128)(2,1)S(1)} %shard_map.79.blocks_ref), channel_id=1, source_target_pairs={{0,1},{1,0},{2,3},{3,2},{4,5},{5,4},{6,7},{7,6},{8,10},{9,11},{10,... | collective-permute-start | bytes 393224 | tf_op jit(solution)/shard_map/ppermute | solution.py:229
  31.3 0.7 %shard_map.80 = (f32[32,512]{1,0:T(8,128)S(1)}, bf16[128,512]{1,0:T(8,128)(2,1)S(1)}) custom-call(bf16[128,512]{1,0:T(8,128)(2,1)S(1)} %shard_map.79.blocks_ref, bf16[512,4096]{1,0:T(8,128)(2,1)S(1)} %get-tuple-element.24.w_ref), custom_call_target="tpu_custom_call" | custom-call | flops 67108864 | bytes 4325376 | tf_op jit(solution)/shard_map/pallas_call | solution.py:23
  32.0 0.0 collective-permute-start.16
  32.0 1.6 %collective-permute-done.15.refs_3_ = bf16[128,512]{1,0:T(8,128)(2,1)S(1)} collective-permute-done((bf16[128,512]{1,0:T(8,128)(2,1)S(1)}, bf16[128,512]{1,0:T(8,128)(2,1)S(1)}, u32[]{:S(2)}, u32[]{:S(2)}) %collective-permute-start.15) | collective-permute-done | bytes 131104 | tf_op jit(solution)/shard_map/ppermute | solution.py:229
  33.6 0.0 collective-permute-start.19
  33.6 0.9 %collective-permute-done.14.refs_2_ = bf16[128,512]{1,0:T(8,128)(2,1)S(1)} collective-permute-done((bf16[128,512]{1,0:T(8,128)(2,1)S(1)}, bf16[128,512]{1,0:T(8,128)(2,1)S(1)}, u32[]{:S(2)}, u32[]{:S(2)}) %collective-permute-start.14) | collective-permute-done | bytes 131104 | tf_op jit(solution)/shard_map/ppermute | solution.py:229
  34.5 0.0 collective-permute-start.18
  34.5 0.5 %collective-permute-done.13.refs_1_ = bf16[128,512]{1,0:T(8,128)(2,1)S(1)} collective-permute-done((bf16[128,512]{1,0:T(8,128)(2,1)S(1)}, bf16[128,512]{1,0:T(8,128)(2,1)S(1)}, u32[]{:S(2)}, u32[]{:S(2)}) %collective-permute-start.13) | collective-permute-done | bytes 131104 | tf_op jit(solution)/shard_map/ppermute | solution.py:229
  35.0 0.0 collective-permute-start.17
  35.0 0.0 collective-permute-done.16.refs_4_
  35.0 0.8 %shard_map.81 = (f32[32,512]{1,0:T(8,128)S(1)}, bf16[128,32,128]{2,1,0:T(8,128)(2,1)S(1)}) custom-call(bf16[512,4096]{1,0:T(8,128)(2,1)S(1)} %get-tuple-element.24.w_ref, f32[32,512]{1,0:T(8,128)S(1)} %get-tuple-element.32.start_ref, bf16[128,512]{1,0:T(8,128)(2,1)S(1)} %get-tuple-element.33.refs_0_, bf16[128,512]{1,0:T(8,128)(2,1)S(1)} %collective-permute-done.13.refs_1_, ...), custom_call_target="tpu_custom_call" | custom-call | flops 67108864 | bytes 4915200 | tf_op jit(solution)/shard_map/pallas_call | solution.py:23
  35.9 0.0 collective-permute-done.19.refs_7_
  35.9 0.0 collective-permute-done.18.refs_6_
  35.9 0.5 %collective-permute-done.17.refs_5_ = bf16[128,512]{1,0:T(8,128)(2,1)S(1)} collective-permute-done((bf16[128,512]{1,0:T(8,128)(2,1)S(1)}, bf16[128,512]{1,0:T(8,128)(2,1)S(1)}, u32[]{:S(2)}, u32[]{:S(2)}) %collective-permute-start.17) | collective-permute-done | bytes 131104 | tf_op jit(solution)/shard_map/ppermute | solution.py:234
  36.4 1.2 %shard_map.82 = (f32[32,512]{1,0:T(8,128)}, bf16[128,32,128]{2,1,0:T(8,128)(2,1)S(1)}) custom-call(s32[4]{0:T(128)S(1)} %copy-done, s32[4,16]{1,0:T(4,128)S(1)} %get-tuple-element.22.refs_1_, bf16[4,16,128,128]{3,2,1,0:T(8,128)(2,1)S(1)} %get-tuple-element.23.refs_2_, f32[32,512]{1,0:T(8,128)S(1)} %get-tuple-element.34.refs_3_, ...), custom_call_target="tpu_custom_call", output_to_operand_aliasing={{1}: (8, {})} | custom-call | flops 67108864 | bytes 3670288 | tf_op jit(solution)/shard_map/pallas_call | solution.py:23
  (1 shorter events, 0.0 us)
Async XLA Ops:
  0.0 10.6 %copy-start = (s32[4]{0:T(128)S(1)}, s32[4]{0:T(128)}, u32[]{:S(2)}) copy-start(s32[4]{0:T(128)} %refs_0_.3) | copy-start | bytes 52
  0.9 7.8 %collective-permute-start.2 = (bf16[32,512]{1,0:T(8,128)(2,1)S(1)}, bf16[32,512]{1,0:T(8,128)(2,1)S(1)}, u32[]{:S(2)}, u32[]{:S(2)}) collective-permute-start(bf16[32,512]{1,0:T(8,128)(2,1)S(1)} %convert_element_type.3.x_ref), channel_id=1, source_target_pairs={{0,4},{1,5},{2,6},{3,7},{4,0},{5,1},{6,2},{7,3},{8,25},{9,24},{10,... | collective-permute-start | bytes 98312 | tf_op jit(solution)/shard_map/ppermute | solution.py:229
  4.9 5.7 %collective-permute-start.1 = (bf16[32,512]{1,0:T(8,128)(2,1)S(1)}, bf16[32,512]{1,0:T(8,128)(2,1)S(1)}, u32[]{:S(2)}, u32[]{:S(2)}) collective-permute-start(bf16[32,512]{1,0:T(8,128)(2,1)S(1)} %convert_element_type.3.x_ref), channel_id=1, source_target_pairs={{0,6},{1,7},{2,4},{3,5},{4,2},{5,3},{6,0},{7,1},{8,24},{9,25},{10,... | collective-permute-start | bytes 98312 | tf_op jit(solution)/shard_map/ppermute | solution.py:229
  6.2 4.4 %collective-permute-start = (bf16[32,512]{1,0:T(8,128)(2,1)S(1)}, bf16[32,512]{1,0:T(8,128)(2,1)S(1)}, u32[]{:S(2)}, u32[]{:S(2)}) collective-permute-start(bf16[32,512]{1,0:T(8,128)(2,1)S(1)} %convert_element_type.3.x_ref), channel_id=1, source_target_pairs={{0,2},{1,3},{2,0},{3,1},{4,6},{5,7},{6,4},{7,5},{8,9},{9,8},{10,11... | collective-permute-start | bytes 98312 | tf_op jit(solution)/shard_map/ppermute | solution.py:229
  10.8 6.3 %collective-permute-start.5 = (bf16[128,512]{1,0:T(8,128)(2,1)S(1)}, bf16[128,512]{1,0:T(8,128)(2,1)S(1)}, u32[]{:S(2)}, u32[]{:S(2)}) collective-permute-start(bf16[128,512]{1,0:T(8,128)(2,1)S(1)} %shard_map.74.refs_0_), channel_id=1, source_target_pairs={{0,17},{1,16},{2,19},{3,18},{4,21},{5,20},{6,23},{7,22},{8,12},{9,... | collective-permute-start | bytes 393224 | tf_op jit(solution)/shard_map/ppermute | solution.py:229
  13.3 5.0 %collective-permute-start.4 = (bf16[128,512]{1,0:T(8,128)(2,1)S(1)}, bf16[128,512]{1,0:T(8,128)(2,1)S(1)}, u32[]{:S(2)}, u32[]{:S(2)}) collective-permute-start(bf16[128,512]{1,0:T(8,128)(2,1)S(1)} %shard_map.74.refs_0_), channel_id=1, source_target_pairs={{0,16},{1,17},{2,18},{3,19},{4,20},{5,21},{6,22},{7,23},{8,14},{9,... | collective-permute-start | bytes 393224 | tf_op jit(solution)/shard_map/ppermute | solution.py:229
  13.8 5.0 %collective-permute-start.3 = (bf16[128,512]{1,0:T(8,128)(2,1)S(1)}, bf16[128,512]{1,0:T(8,128)(2,1)S(1)}, u32[]{:S(2)}, u32[]{:S(2)}) collective-permute-start(bf16[128,512]{1,0:T(8,128)(2,1)S(1)} %shard_map.74.refs_0_), channel_id=1, source_target_pairs={{0,1},{1,0},{2,3},{3,2},{4,5},{5,4},{6,7},{7,6},{8,10},{9,11},{10,... | collective-permute-start | bytes 393224 | tf_op jit(solution)/shard_map/ppermute | solution.py:229
  17.1 1.7 %collective-permute-start.6 = (bf16[128,512]{1,0:T(8,128)(2,1)S(1)}, bf16[128,512]{1,0:T(8,128)(2,1)S(1)}, u32[]{:S(2)}, u32[]{:S(2)}) collective-permute-start(bf16[128,512]{1,0:T(8,128)(2,1)S(1)} %get-tuple-element.27.refs_0_), channel_id=1, source_target_pairs={{0,8},{1,9},{2,10},{3,11},{4,12},{5,13},{6,14},{7,15},{8,0},{9,1},... | collective-permute-start | bytes 393224 | tf_op jit(solution)/shard_map/ppermute | solution.py:234
  17.1 2.5 %collective-permute-start.9 = (bf16[128,512]{1,0:T(8,128)(2,1)S(1)}, bf16[128,512]{1,0:T(8,128)(2,1)S(1)}, u32[]{:S(2)}, u32[]{:S(2)}) collective-permute-start(bf16[128,512]{1,0:T(8,128)(2,1)S(1)} %collective-permute-done.5.refs_3_), channel_id=1, source_target_pairs={{0,8},{1,9},{2,10},{3,11},{4,12},{5,13},{6,14},{7,15},{8,0},{9,1},... | collective-permute-start | bytes 393224 | tf_op jit(solution)/shard_map/ppermute | solution.py:234
  18.2 1.4 %collective-permute-start.8 = (bf16[128,512]{1,0:T(8,128)(2,1)S(1)}, bf16[128,512]{1,0:T(8,128)(2,1)S(1)}, u32[]{:S(2)}, u32[]{:S(2)}) collective-permute-start(bf16[128,512]{1,0:T(8,128)(2,1)S(1)} %collective-permute-done.4.refs_2_), channel_id=1, source_target_pairs={{0,8},{1,9},{2,10},{3,11},{4,12},{5,13},{6,14},{7,15},{8,0},{9,1},... | collective-permute-start | bytes 393224 | tf_op jit(solution)/shard_map/ppermute | solution.py:234
  18.8 1.3 %collective-permute-start.7 = (bf16[128,512]{1,0:T(8,128)(2,1)S(1)}, bf16[128,512]{1,0:T(8,128)(2,1)S(1)}, u32[]{:S(2)}, u32[]{:S(2)}) collective-permute-start(bf16[128,512]{1,0:T(8,128)(2,1)S(1)} %collective-permute-done.3.refs_1_), channel_id=1, source_target_pairs={{0,8},{1,9},{2,10},{3,11},{4,12},{5,13},{6,14},{7,15},{8,0},{9,1},... | collective-permute-start | bytes 393224 | tf_op jit(solution)/shard_map/ppermute | solution.py:234
  20.7 4.9 %collective-permute-start.12 = (bf16[32,512]{1,0:T(8,128)(2,1)S(1)}, bf16[32,512]{1,0:T(8,128)(2,1)S(1)}, u32[]{:S(2)}, u32[]{:S(2)}) collective-permute-start(bf16[32,512]{1,0:T(8,128)(2,1)S(1)} %get-tuple-element.31.refs_0_), channel_id=1, source_target_pairs={{0,4},{1,5},{2,6},{3,7},{4,0},{5,1},{6,2},{7,3},{8,25},{9,24},{10,... | collective-permute-start | bytes 98312 | tf_op jit(solution)/shard_map/ppermute | solution.py:229
  22.0 5.7 %collective-permute-start.11 = (bf16[32,512]{1,0:T(8,128)(2,1)S(1)}, bf16[32,512]{1,0:T(8,128)(2,1)S(1)}, u32[]{:S(2)}, u32[]{:S(2)}) collective-permute-start(bf16[32,512]{1,0:T(8,128)(2,1)S(1)} %get-tuple-element.31.refs_0_), channel_id=1, source_target_pairs={{0,6},{1,7},{2,4},{3,5},{4,2},{5,3},{6,0},{7,1},{8,24},{9,25},{10,... | collective-permute-start | bytes 98312 | tf_op jit(solution)/shard_map/ppermute | solution.py:229
  23.0 4.7 %collective-permute-start.10 = (bf16[32,512]{1,0:T(8,128)(2,1)S(1)}, bf16[32,512]{1,0:T(8,128)(2,1)S(1)}, u32[]{:S(2)}, u32[]{:S(2)}) collective-permute-start(bf16[32,512]{1,0:T(8,128)(2,1)S(1)} %get-tuple-element.31.refs_0_), channel_id=1, source_target_pairs={{0,2},{1,3},{2,0},{3,1},{4,6},{5,7},{6,4},{7,5},{8,9},{9,8},{10,11... | collective-permute-start | bytes 98312 | tf_op jit(solution)/shard_map/ppermute | solution.py:229
  27.7 5.9 %collective-permute-start.15 = (bf16[128,512]{1,0:T(8,128)(2,1)S(1)}, bf16[128,512]{1,0:T(8,128)(2,1)S(1)}, u32[]{:S(2)}, u32[]{:S(2)}) collective-permute-start(bf16[128,512]{1,0:T(8,128)(2,1)S(1)} %shard_map.79.blocks_ref), channel_id=1, source_target_pairs={{0,17},{1,16},{2,19},{3,18},{4,21},{5,20},{6,23},{7,22},{8,12},{9,... | collective-permute-start | bytes 393224 | tf_op jit(solution)/shard_map/ppermute | solution.py:229
  29.5 5.0 %collective-permute-start.14 = (bf16[128,512]{1,0:T(8,128)(2,1)S(1)}, bf16[128,512]{1,0:T(8,128)(2,1)S(1)}, u32[]{:S(2)}, u32[]{:S(2)}) collective-permute-start(bf16[128,512]{1,0:T(8,128)(2,1)S(1)} %shard_map.79.blocks_ref), channel_id=1, source_target_pairs={{0,16},{1,17},{2,18},{3,19},{4,20},{5,21},{6,22},{7,23},{8,14},{9,... | collective-permute-start | bytes 393224 | tf_op jit(solution)/shard_map/ppermute | solution.py:229
  30.1 5.0 %collective-permute-start.13 = (bf16[128,512]{1,0:T(8,128)(2,1)S(1)}, bf16[128,512]{1,0:T(8,128)(2,1)S(1)}, u32[]{:S(2)}, u32[]{:S(2)}) collective-permute-start(bf16[128,512]{1,0:T(8,128)(2,1)S(1)} %shard_map.79.blocks_ref), channel_id=1, source_target_pairs={{0,1},{1,0},{2,3},{3,2},{4,5},{5,4},{6,7},{7,6},{8,10},{9,11},{10,... | collective-permute-start | bytes 393224 | tf_op jit(solution)/shard_map/ppermute | solution.py:229
  32.0 3.1 %collective-permute-start.16 = (bf16[128,512]{1,0:T(8,128)(2,1)S(1)}, bf16[128,512]{1,0:T(8,128)(2,1)S(1)}, u32[]{:S(2)}, u32[]{:S(2)}) collective-permute-start(bf16[128,512]{1,0:T(8,128)(2,1)S(1)} %get-tuple-element.33.refs_0_), channel_id=1, source_target_pairs={{0,8},{1,9},{2,10},{3,11},{4,12},{5,13},{6,14},{7,15},{8,0},{9,1},... | collective-permute-start | bytes 393224 | tf_op jit(solution)/shard_map/ppermute | solution.py:234
  33.6 2.3 %collective-permute-start.19 = (bf16[128,512]{1,0:T(8,128)(2,1)S(1)}, bf16[128,512]{1,0:T(8,128)(2,1)S(1)}, u32[]{:S(2)}, u32[]{:S(2)}) collective-permute-start(bf16[128,512]{1,0:T(8,128)(2,1)S(1)} %collective-permute-done.15.refs_3_), channel_id=1, source_target_pairs={{0,8},{1,9},{2,10},{3,11},{4,12},{5,13},{6,14},{7,15},{8,0},{9,1},... | collective-permute-start | bytes 393224 | tf_op jit(solution)/shard_map/ppermute | solution.py:234
  34.5 1.4 %collective-permute-start.18 = (bf16[128,512]{1,0:T(8,128)(2,1)S(1)}, bf16[128,512]{1,0:T(8,128)(2,1)S(1)}, u32[]{:S(2)}, u32[]{:S(2)}) collective-permute-start(bf16[128,512]{1,0:T(8,128)(2,1)S(1)} %collective-permute-done.14.refs_2_), channel_id=1, source_target_pairs={{0,8},{1,9},{2,10},{3,11},{4,12},{5,13},{6,14},{7,15},{8,0},{9,1},... | collective-permute-start | bytes 393224 | tf_op jit(solution)/shard_map/ppermute | solution.py:234
  35.0 1.3 %collective-permute-start.17 = (bf16[128,512]{1,0:T(8,128)(2,1)S(1)}, bf16[128,512]{1,0:T(8,128)(2,1)S(1)}, u32[]{:S(2)}, u32[]{:S(2)}) collective-permute-start(bf16[128,512]{1,0:T(8,128)(2,1)S(1)} %collective-permute-done.13.refs_1_), channel_id=1, source_target_pairs={{0,8},{1,9},{2,10},{3,11},{4,12},{5,13},{6,14},{7,15},{8,0},{9,1},... | collective-permute-start | bytes 393224 | tf_op jit(solution)/shard_map/ppermute | solution.py:234

commit v8 on v7

--- a/solution.py
+++ b/solution.py
@@ -112,24 +112,36 @@
     return count
 
 
-def column_kernel(parts, p_dev, pop, counts_ref, *refs):
+def round_kernel(p_dev, x_ref, counts_ref, out_ref, wide_ref, count_ref, sems):
+    half = x_ref.shape[0] // 2
+    parts = [pl.ds(n * half, half) for n in range(2)]
+    moves = [
+        pltpu.make_async_copy(x_ref.at[at], wide_ref.at[at], sems.at[n])
+        for n, at in enumerate(parts)
+    ]
+    small = pltpu.make_async_copy(counts_ref, count_ref, sems.at[2])
+    small.start()
+    for move in moves:
+        move.start()
+    small.wait()
+    count = count_of(count_ref, lax.axis_index("area"))
+    first = lax.axis_index("local") * p_dev
+    pop = x_ref.shape[1] // p_dev
+    for move, at in zip(moves, parts):
+        move.wait()
+        for s in range(p_dev):
+            here = slice(s * pop, (s + 1) * pop)
+            x = wide_ref[at, here]
+            out_ref[at, here] = jnp.where(
+                first + s < count, x, jnp.zeros_like(x)
+            ).astype(out_ref.dtype)
+
+
+def column_kernel(*refs):
     out_ref = refs[-1]
     cond = refs[0].shape[0]
-    area, local = lax.axis_index("area"), lax.axis_index("local")
-    for (d, far), block in zip(parts, refs[:-1]):
-        if far is None:
-            out_ref[d * cond : (d + 1) * cond, :] = block[...]
-            continue
-        (x0, l0), (x1, l1) = far
-        odd = area & 1
-        count = count_of(counts_ref, area ^ (jnp.where(odd == 1, x1, x0) * CORES))
-        first = (local ^ jnp.where(odd == 1, l1, l0)) * p_dev
-        for s in range(p_dev):
-            at = slice(s * pop, (s + 1) * pop)
-            x = block[:, at]
-            out_ref[d * cond : (d + 1) * cond, at] = jnp.where(
-                first + s < count, x, jnp.zeros_like(x)
-            )
+    for d, block in enumerate(refs[:-1]):
+        out_ref[d * cond : (d + 1) * cond, :] = block[...]
 
 
 def lay(arrays, table, start, cond):
@@ -233,8 +245,19 @@
     def across(x):
         return lax.ppermute(x, AXES, [(i, i ^ locs) for i in range(devices)])
 
-    mine = rates_init.astype(jnp.bfloat16)
     shape = jax.ShapeDtypeStruct
+    mine = call(
+        functools.partial(round_kernel, p_dev),
+        pltpu.VMEM(rates_init.shape, jnp.bfloat16),
+        [in_hbm(rates_init), in_hbm(counts)],
+        [HBM] * 2,
+        0,
+        scratch=[
+            pltpu.VMEM(rates_init.shape, rates_init.dtype),
+            pltpu.VMEM(counts.shape, counts.dtype),
+            pltpu.SemaphoreType.DMA((3,)),
+        ],
+    )
     within_w, kept = call(
         within_kernel,
         [pltpu.VMEM(x.shape, x.dtype) for x in (within_w, mine)],
@@ -246,15 +269,10 @@
     )
     for step in range(STEPS):
         column = call(
-            functools.partial(
-                column_kernel,
-                [(d, None if step else by) for d, by in enumerate(first)],
-                p_dev,
-                pop,
-            ),
+            column_kernel,
             shape((len(first) * cond, width), mine.dtype),
-            [counts, kept] + [swap(mine, by) for by in first[1:]],
-            [VMEM] * (1 + len(first)),
+            [kept] + [swap(mine, by) for by in first[1:]],
+            [VMEM] * len(first),
             0,
         )
         whole = column

time: 37.7 us -> 37.7 us (level)
  other arithmetic: 0.86 us -> 0 us
  Pallas kernels: 9.15 us -> 9.84 us
    convert_element_type x1 -> x0, other arithmetic: 0.86 us -> none  [body(): mine = rates_init.astype(jnp.bfloat16)]
    pallas_call x10 -> x11, Pallas kernels: 9.15 us -> 9.84 us  [call(): pl.pallas_call(kernel, out_shape=out, in_specs=in_specs, out_specs=out_sp...]
where the time goes in v8:
time: 37.7 us; the launch traced here: 37.4 us
  starting transfers between devices  16.9 us (45%)
  waiting for transfers between devices  10.6 us (28%)
  Pallas kernels  9.84 us (26%)
    ppermute x12, starting transfers between devices, swap(): lax.ppermute(x, AXES, [(i, i ^ far[i // locs % CORES]) for i in range(dev...  16.3 us
    pallas_call x11, Pallas kernels, call(): pl.pallas_call(kernel, out_shape=out, in_specs=in_specs, out_specs=out_sp...  9.84 us
    ppermute x12, waiting for transfers between devices, swap(): lax.ppermute(x, AXES, [(i, i ^ far[i // locs % CORES]) for i in range(dev...  9.57 us
    ppermute x8, waiting for transfers between devices, across(): return lax.ppermute(x, AXES, [(i, i ^ locs) for i in range(devices)])  1.01 us
  transfers between devices with their start and end apart: 20, of which 10 were waited for; matrix products, arithmetic and copies ran while one was open for 0% of the time, Pallas kernels for 20%

profile of v8, /device:TPU:0, one launch (start us, length us, event | category | flops | bytes accessed | tf_op | source)
XLA Modules:
  0.0 37.4 jit_solution(4522716579985088328)
XLA Ops:
  0.0 0.8 %shard_map.73.x_ref = bf16[32,512]{1,0:T(8,128)(2,1)S(1)} custom-call(f32[32,512]{1,0:T(8,128)} %x_ref.1, s32[4]{0:T(128)} %refs_0_.3), custom_call_target="tpu_custom_call" | custom-call | bytes 65552 | tf_op jit(solution)/shard_map/pallas_call | solution.py:23
  0.8 4.1 %collective-permute-start.2 = (bf16[32,512]{1,0:T(8,128)(2,1)S(1)}, bf16[32,512]{1,0:T(8,128)(2,1)S(1)}, u32[]{:S(2)}, u32[]{:S(2)}) collective-permute-start(bf16[32,512]{1,0:T(8,128)(2,1)S(1)} %shard_map.73.x_ref), channel_id=1, source_target_pairs={{0,4},{1,5},{2,6},{3,7},{4,0},{5,1},{6,2},{7,3},{8,25},{9,24},{10,... | collective-permute-start | bytes 98312 | tf_op jit(solution)/shard_map/ppermute | solution.py:241
  4.9 1.3 %collective-permute-start.1 = (bf16[32,512]{1,0:T(8,128)(2,1)S(1)}, bf16[32,512]{1,0:T(8,128)(2,1)S(1)}, u32[]{:S(2)}, u32[]{:S(2)}) collective-permute-start(bf16[32,512]{1,0:T(8,128)(2,1)S(1)} %shard_map.73.x_ref), channel_id=1, source_target_pairs={{0,6},{1,7},{2,4},{3,5},{4,2},{5,3},{6,0},{7,1},{8,24},{9,25},{10,... | collective-permute-start | bytes 98312 | tf_op jit(solution)/shard_map/ppermute | solution.py:241
  6.3 0.2 collective-permute-start
  6.5 2.2 %shard_map.74 = (bf16[512,4096]{1,0:T(8,128)(2,1)S(1)}, bf16[32,512]{1,0:T(8,128)(2,1)S(1)}) custom-call(bf16[32,512]{1,0:T(8,128)(2,1)S(1)} %shard_map.73.x_ref, bf16[512,4096]{1,0:T(8,128)(2,1)} %w_ref.1), custom_call_target="tpu_custom_call" | custom-call | bytes 4227072 | tf_op jit(solution)/shard_map/pallas_call | solution.py:23
  8.7 0.0 collective-permute-done.2.refs_3_
  8.7 1.9 %collective-permute-done.1.refs_2_ = bf16[32,512]{1,0:T(8,128)(2,1)S(1)} collective-permute-done((bf16[32,512]{1,0:T(8,128)(2,1)S(1)}, bf16[32,512]{1,0:T(8,128)(2,1)S(1)}, u32[]{:S(2)}, u32[]{:S(2)}) %collective-permute-start.1) | collective-permute-done | bytes 32800 | tf_op jit(solution)/shard_map/ppermute | solution.py:241
  10.6 0.0 collective-permute-done.refs_1_
  10.7 2.5 %collective-permute-start.5 = (bf16[128,512]{1,0:T(8,128)(2,1)S(1)}, bf16[128,512]{1,0:T(8,128)(2,1)S(1)}, u32[]{:S(2)}, u32[]{:S(2)}) collective-permute-start(bf16[128,512]{1,0:T(8,128)(2,1)S(1)} %shard_map.75.refs_0_), channel_id=1, source_target_pairs={{0,17},{1,16},{2,19},{3,18},{4,21},{5,20},{6,23},{7,22},{8,12},{9,... | collective-permute-start | bytes 393224 | tf_op jit(solution)/shard_map/ppermute | solution.py:241
  13.2 0.5 %collective-permute-start.4 = (bf16[128,512]{1,0:T(8,128)(2,1)S(1)}, bf16[128,512]{1,0:T(8,128)(2,1)S(1)}, u32[]{:S(2)}, u32[]{:S(2)}) collective-permute-start(bf16[128,512]{1,0:T(8,128)(2,1)S(1)} %shard_map.75.refs_0_), channel_id=1, source_target_pairs={{0,16},{1,17},{2,18},{3,19},{4,20},{5,21},{6,22},{7,23},{8,14},{9,... | collective-permute-start | bytes 393224 | tf_op jit(solution)/shard_map/ppermute | solution.py:241
  13.7 0.5 %collective-permute-start.3 = (bf16[128,512]{1,0:T(8,128)(2,1)S(1)}, bf16[128,512]{1,0:T(8,128)(2,1)S(1)}, u32[]{:S(2)}, u32[]{:S(2)}) collective-permute-start(bf16[128,512]{1,0:T(8,128)(2,1)S(1)} %shard_map.75.refs_0_), channel_id=1, source_target_pairs={{0,1},{1,0},{2,3},{3,2},{4,5},{5,4},{6,7},{7,6},{8,10},{9,11},{10,... | collective-permute-start | bytes 393224 | tf_op jit(solution)/shard_map/ppermute | solution.py:241
  14.2 2.0 %shard_map.76 = (bf16[4,16,128,128]{3,2,1,0:T(8,128)(2,1)S(1)}, f32[32,512]{1,0:T(8,128)S(1)}, s32[4,16]{1,0:T(4,128)S(1)}, bf16[128,512]{1,0:T(8,128)(2,1)S(1)}) custom-call(bf16[128,512]{1,0:T(8,128)(2,1)S(1)} %shard_map.75.refs_0_, s32[4,16]{1,0:T(4,128)} %refs_1_.1, s32[4]{0:T(128)} %refs_2_.1, bf16[4,16,128,128]{3,2,1,0:T(8,128)(2,1)} %refs_3_.1, ...), custom_call_target="tpu_custom_call" | custom-call | bytes 2294032 | tf_op jit(solution)/shard_map/pallas_call | solution.py:23
  16.2 0.0 copy-start
  16.2 0.7 %shard_map.77 = (f32[32,512]{1,0:T(8,128)S(1)}, bf16[128,512]{1,0:T(8,128)(2,1)S(1)}) custom-call(bf16[128,512]{1,0:T(8,128)(2,1)S(1)} %get-tuple-element.25.blocks_ref, bf16[512,4096]{1,0:T(8,128)(2,1)S(1)} %get-tuple-element.24.w_ref), custom_call_target="tpu_custom_call" | custom-call | flops 67108864 | bytes 4325376 | tf_op jit(solution)/shard_map/pallas_call | solution.py:23
  17.0 0.0 collective-permute-start.6
  17.0 0.0 collective-permute-done.5.refs_3_
  17.0 0.5 %collective-permute-start.9 = (bf16[128,512]{1,0:T(8,128)(2,1)S(1)}, bf16[128,512]{1,0:T(8,128)(2,1)S(1)}, u32[]{:S(2)}, u32[]{:S(2)}) collective-permute-start(bf16[128,512]{1,0:T(8,128)(2,1)S(1)} %collective-permute-done.5.refs_3_), channel_id=1, source_target_pairs={{0,8},{1,9},{2,10},{3,11},{4,12},{5,13},{6,14},{7,15},{8,0},{9,1},... | collective-permute-start | bytes 393224 | tf_op jit(solution)/shard_map/ppermute | solution.py:246
  17.5 0.6 %collective-permute-done.4.refs_2_ = bf16[128,512]{1,0:T(8,128)(2,1)S(1)} collective-permute-done((bf16[128,512]{1,0:T(8,128)(2,1)S(1)}, bf16[128,512]{1,0:T(8,128)(2,1)S(1)}, u32[]{:S(2)}, u32[]{:S(2)}) %collective-permute-start.4) | collective-permute-done | bytes 131104 | tf_op jit(solution)/shard_map/ppermute | solution.py:241
  18.1 0.0 collective-permute-start.8
  18.1 0.5 %collective-permute-done.3.refs_1_ = bf16[128,512]{1,0:T(8,128)(2,1)S(1)} collective-permute-done((bf16[128,512]{1,0:T(8,128)(2,1)S(1)}, bf16[128,512]{1,0:T(8,128)(2,1)S(1)}, u32[]{:S(2)}, u32[]{:S(2)}) %collective-permute-start.3) | collective-permute-done | bytes 131104 | tf_op jit(solution)/shard_map/ppermute | solution.py:241
  18.7 0.0 collective-permute-start.7
  18.7 0.0 collective-permute-done.6.refs_4_
  18.7 0.8 %shard_map.78 = (f32[32,512]{1,0:T(8,128)S(1)}, bf16[128,32,128]{2,1,0:T(8,128)(2,1)S(1)}) custom-call(bf16[512,4096]{1,0:T(8,128)(2,1)S(1)} %get-tuple-element.24.w_ref, f32[32,512]{1,0:T(8,128)S(1)} %get-tuple-element.26.start_ref, bf16[128,512]{1,0:T(8,128)(2,1)S(1)} %get-tuple-element.27.refs_0_, bf16[128,512]{1,0:T(8,128)(2,1)S(1)} %collective-permute-done.3.refs_1_, ...), custom_call_target="tpu_custom_call" | custom-call | flops 67108864 | bytes 4915200 | tf_op jit(solution)/shard_map/pallas_call | solution.py:23
  19.5 0.0 collective-permute-done.9.refs_7_
  19.5 0.0 collective-permute-done.8.refs_6_
  19.5 0.5 %collective-permute-done.7.refs_5_ = bf16[128,512]{1,0:T(8,128)(2,1)S(1)} collective-permute-done((bf16[128,512]{1,0:T(8,128)(2,1)S(1)}, bf16[128,512]{1,0:T(8,128)(2,1)S(1)}, u32[]{:S(2)}, u32[]{:S(2)}) %collective-permute-start.7) | collective-permute-done | bytes 131104 | tf_op jit(solution)/shard_map/ppermute | solution.py:246
  20.0 0.0 copy-done
  20.0 0.5 %shard_map.79 = (bf16[32,512]{1,0:T(8,128)(2,1)S(1)}, bf16[128,32,128]{2,1,0:T(8,128)(2,1)S(1)}) custom-call(s32[4]{0:T(128)S(1)} %copy-done, s32[4,16]{1,0:T(4,128)S(1)} %get-tuple-element.22.refs_1_, bf16[4,16,128,128]{3,2,1,0:T(8,128)(2,1)S(1)} %get-tuple-element.23.refs_2_, ...), custom_call_target="tpu_custom_call", output_to_operand_aliasing={{1}: (8, {})} | custom-call | flops 67108864 | bytes 3670288 | tf_op jit(solution)/shard_map/pallas_call | solution.py:23
  20.6 1.3 %collective-permute-start.12 = (bf16[32,512]{1,0:T(8,128)(2,1)S(1)}, bf16[32,512]{1,0:T(8,128)(2,1)S(1)}, u32[]{:S(2)}, u32[]{:S(2)}) collective-permute-start(bf16[32,512]{1,0:T(8,128)(2,1)S(1)} %get-tuple-element.31.refs_0_), channel_id=1, source_target_pairs={{0,4},{1,5},{2,6},{3,7},{4,0},{5,1},{6,2},{7,3},{8,25},{9,24},{10,... | collective-permute-start | bytes 98312 | tf_op jit(solution)/shard_map/ppermute | solution.py:241
  21.9 1.0 %collective-permute-start.11 = (bf16[32,512]{1,0:T(8,128)(2,1)S(1)}, bf16[32,512]{1,0:T(8,128)(2,1)S(1)}, u32[]{:S(2)}, u32[]{:S(2)}) collective-permute-start(bf16[32,512]{1,0:T(8,128)(2,1)S(1)} %get-tuple-element.31.refs_0_), channel_id=1, source_target_pairs={{0,6},{1,7},{2,4},{3,5},{4,2},{5,3},{6,0},{7,1},{8,24},{9,25},{10,... | collective-permute-start | bytes 98312 | tf_op jit(solution)/shard_map/ppermute | solution.py:241
  22.9 1.2 %collective-permute-start.10 = (bf16[32,512]{1,0:T(8,128)(2,1)S(1)}, bf16[32,512]{1,0:T(8,128)(2,1)S(1)}, u32[]{:S(2)}, u32[]{:S(2)}) collective-permute-start(bf16[32,512]{1,0:T(8,128)(2,1)S(1)} %get-tuple-element.31.refs_0_), channel_id=1, source_target_pairs={{0,2},{1,3},{2,0},{3,1},{4,6},{5,7},{6,4},{7,5},{8,9},{9,8},{10,11... | collective-permute-start | bytes 98312 | tf_op jit(solution)/shard_map/ppermute | solution.py:241
  24.1 1.3 %collective-permute-done.12.refs_3_ = bf16[32,512]{1,0:T(8,128)(2,1)S(1)} collective-permute-done((bf16[32,512]{1,0:T(8,128)(2,1)S(1)}, bf16[32,512]{1,0:T(8,128)(2,1)S(1)}, u32[]{:S(2)}, u32[]{:S(2)}) %collective-permute-start.12) | collective-permute-done | bytes 32800 | tf_op jit(solution)/shard_map/ppermute | solution.py:241
  25.4 2.1 %collective-permute-done.11.refs_2_ = bf16[32,512]{1,0:T(8,128)(2,1)S(1)} collective-permute-done((bf16[32,512]{1,0:T(8,128)(2,1)S(1)}, bf16[32,512]{1,0:T(8,128)(2,1)S(1)}, u32[]{:S(2)}, u32[]{:S(2)}) %collective-permute-start.11) | collective-permute-done | bytes 32800 | tf_op jit(solution)/shard_map/ppermute | solution.py:241
  27.6 0.0 collective-permute-done.10.refs_1_
  27.6 1.8 %collective-permute-start.15 = (bf16[128,512]{1,0:T(8,128)(2,1)S(1)}, bf16[128,512]{1,0:T(8,128)(2,1)S(1)}, u32[]{:S(2)}, u32[]{:S(2)}) collective-permute-start(bf16[128,512]{1,0:T(8,128)(2,1)S(1)} %shard_map.80.blocks_ref), channel_id=1, source_target_pairs={{0,17},{1,16},{2,19},{3,18},{4,21},{5,20},{6,23},{7,22},{8,12},{9,... | collective-permute-start | bytes 393224 | tf_op jit(solution)/shard_map/ppermute | solution.py:241
  29.4 0.5 %collective-permute-start.14 = (bf16[128,512]{1,0:T(8,128)(2,1)S(1)}, bf16[128,512]{1,0:T(8,128)(2,1)S(1)}, u32[]{:S(2)}, u32[]{:S(2)}) collective-permute-start(bf16[128,512]{1,0:T(8,128)(2,1)S(1)} %shard_map.80.blocks_ref), channel_id=1, source_target_pairs={{0,16},{1,17},{2,18},{3,19},{4,20},{5,21},{6,22},{7,23},{8,14},{9,... | collective-permute-start | bytes 393224 | tf_op jit(solution)/shard_map/ppermute | solution.py:241
  30.0 1.2 %collective-permute-start.13 = (bf16[128,512]{1,0:T(8,128)(2,1)S(1)}, bf16[128,512]{1,0:T(8,128)(2,1)S(1)}, u32[]{:S(2)}, u32[]{:S(2)}) collective-permute-start(bf16[128,512]{1,0:T(8,128)(2,1)S(1)} %shard_map.80.blocks_ref), channel_id=1, source_target_pairs={{0,1},{1,0},{2,3},{3,2},{4,5},{5,4},{6,7},{7,6},{8,10},{9,11},{10,... | collective-permute-start | bytes 393224 | tf_op jit(solution)/shard_map/ppermute | solution.py:241
  31.2 0.7 %shard_map.81 = (f32[32,512]{1,0:T(8,128)S(1)}, bf16[128,512]{1,0:T(8,128)(2,1)S(1)}) custom-call(bf16[128,512]{1,0:T(8,128)(2,1)S(1)} %shard_map.80.blocks_ref, bf16[512,4096]{1,0:T(8,128)(2,1)S(1)} %get-tuple-element.24.w_ref), custom_call_target="tpu_custom_call" | custom-call | flops 67108864 | bytes 4325376 | tf_op jit(solution)/shard_map/pallas_call | solution.py:23
  31.9 0.0 collective-permute-start.16
  31.9 1.6 %collective-permute-done.15.refs_3_ = bf16[128,512]{1,0:T(8,128)(2,1)S(1)} collective-permute-done((bf16[128,512]{1,0:T(8,128)(2,1)S(1)}, bf16[128,512]{1,0:T(8,128)(2,1)S(1)}, u32[]{:S(2)}, u32[]{:S(2)}) %collective-permute-start.15) | collective-permute-done | bytes 131104 | tf_op jit(solution)/shard_map/ppermute | solution.py:241
  33.5 0.0 collective-permute-start.19
  33.5 0.9 %collective-permute-done.14.refs_2_ = bf16[128,512]{1,0:T(8,128)(2,1)S(1)} collective-permute-done((bf16[128,512]{1,0:T(8,128)(2,1)S(1)}, bf16[128,512]{1,0:T(8,128)(2,1)S(1)}, u32[]{:S(2)}, u32[]{:S(2)}) %collective-permute-start.14) | collective-permute-done | bytes 131104 | tf_op jit(solution)/shard_map/ppermute | solution.py:241
  34.4 0.0 collective-permute-start.18
  34.4 0.5 %collective-permute-done.13.refs_1_ = bf16[128,512]{1,0:T(8,128)(2,1)S(1)} collective-permute-done((bf16[128,512]{1,0:T(8,128)(2,1)S(1)}, bf16[128,512]{1,0:T(8,128)(2,1)S(1)}, u32[]{:S(2)}, u32[]{:S(2)}) %collective-permute-start.13) | collective-permute-done | bytes 131104 | tf_op jit(solution)/shard_map/ppermute | solution.py:241
  34.9 0.0 collective-permute-start.17
  34.9 0.0 collective-permute-done.16.refs_4_
  34.9 0.8 %shard_map.82 = (f32[32,512]{1,0:T(8,128)S(1)}, bf16[128,32,128]{2,1,0:T(8,128)(2,1)S(1)}) custom-call(bf16[512,4096]{1,0:T(8,128)(2,1)S(1)} %get-tuple-element.24.w_ref, f32[32,512]{1,0:T(8,128)S(1)} %get-tuple-element.32.start_ref, bf16[128,512]{1,0:T(8,128)(2,1)S(1)} %get-tuple-element.33.refs_0_, bf16[128,512]{1,0:T(8,128)(2,1)S(1)} %collective-permute-done.13.refs_1_, ...), custom_call_target="tpu_custom_call" | custom-call | flops 67108864 | bytes 4915200 | tf_op jit(solution)/shard_map/pallas_call | solution.py:23
  35.8 0.0 collective-permute-done.19.refs_7_
  35.8 0.0 collective-permute-done.18.refs_6_
  35.8 0.5 %collective-permute-done.17.refs_5_ = bf16[128,512]{1,0:T(8,128)(2,1)S(1)} collective-permute-done((bf16[128,512]{1,0:T(8,128)(2,1)S(1)}, bf16[128,512]{1,0:T(8,128)(2,1)S(1)}, u32[]{:S(2)}, u32[]{:S(2)}) %collective-permute-start.17) | collective-permute-done | bytes 131104 | tf_op jit(solution)/shard_map/ppermute | solution.py:246
  36.3 1.2 %shard_map.83 = (f32[32,512]{1,0:T(8,128)}, bf16[128,32,128]{2,1,0:T(8,128)(2,1)S(1)}) custom-call(s32[4]{0:T(128)S(1)} %copy-done, s32[4,16]{1,0:T(4,128)S(1)} %get-tuple-element.22.refs_1_, bf16[4,16,128,128]{3,2,1,0:T(8,128)(2,1)S(1)} %get-tuple-element.23.refs_2_, f32[32,512]{1,0:T(8,128)S(1)} %get-tuple-element.34.refs_3_, ...), custom_call_target="tpu_custom_call", output_to_operand_aliasing={{1}: (8, {})} | custom-call | flops 67108864 | bytes 3670288 | tf_op jit(solution)/shard_map/pallas_call | solution.py:23
  (2 shorter events, 0.0 us)
Async XLA Ops:
  0.8 7.9 %collective-permute-start.2 = (bf16[32,512]{1,0:T(8,128)(2,1)S(1)}, bf16[32,512]{1,0:T(8,128)(2,1)S(1)}, u32[]{:S(2)}, u32[]{:S(2)}) collective-permute-start(bf16[32,512]{1,0:T(8,128)(2,1)S(1)} %shard_map.73.x_ref), channel_id=1, source_target_pairs={{0,4},{1,5},{2,6},{3,7},{4,0},{5,1},{6,2},{7,3},{8,25},{9,24},{10,... | collective-permute-start | bytes 98312 | tf_op jit(solution)/shard_map/ppermute | solution.py:241
  4.9 5.7 %collective-permute-start.1 = (bf16[32,512]{1,0:T(8,128)(2,1)S(1)}, bf16[32,512]{1,0:T(8,128)(2,1)S(1)}, u32[]{:S(2)}, u32[]{:S(2)}) collective-permute-start(bf16[32,512]{1,0:T(8,128)(2,1)S(1)} %shard_map.73.x_ref), channel_id=1, source_target_pairs={{0,6},{1,7},{2,4},{3,5},{4,2},{5,3},{6,0},{7,1},{8,24},{9,25},{10,... | collective-permute-start | bytes 98312 | tf_op jit(solution)/shard_map/ppermute | solution.py:241
  6.3 4.4 %collective-permute-start = (bf16[32,512]{1,0:T(8,128)(2,1)S(1)}, bf16[32,512]{1,0:T(8,128)(2,1)S(1)}, u32[]{:S(2)}, u32[]{:S(2)}) collective-permute-start(bf16[32,512]{1,0:T(8,128)(2,1)S(1)} %shard_map.73.x_ref), channel_id=1, source_target_pairs={{0,2},{1,3},{2,0},{3,1},{4,6},{5,7},{6,4},{7,5},{8,9},{9,8},{10,11... | collective-permute-start | bytes 98312 | tf_op jit(solution)/shard_map/ppermute | solution.py:241
  10.7 6.3 %collective-permute-start.5 = (bf16[128,512]{1,0:T(8,128)(2,1)S(1)}, bf16[128,512]{1,0:T(8,128)(2,1)S(1)}, u32[]{:S(2)}, u32[]{:S(2)}) collective-permute-start(bf16[128,512]{1,0:T(8,128)(2,1)S(1)} %shard_map.75.refs_0_), channel_id=1, source_target_pairs={{0,17},{1,16},{2,19},{3,18},{4,21},{5,20},{6,23},{7,22},{8,12},{9,... | collective-permute-start | bytes 393224 | tf_op jit(solution)/shard_map/ppermute | solution.py:241
  13.2 5.0 %collective-permute-start.4 = (bf16[128,512]{1,0:T(8,128)(2,1)S(1)}, bf16[128,512]{1,0:T(8,128)(2,1)S(1)}, u32[]{:S(2)}, u32[]{:S(2)}) collective-permute-start(bf16[128,512]{1,0:T(8,128)(2,1)S(1)} %shard_map.75.refs_0_), channel_id=1, source_target_pairs={{0,16},{1,17},{2,18},{3,19},{4,20},{5,21},{6,22},{7,23},{8,14},{9,... | collective-permute-start | bytes 393224 | tf_op jit(solution)/shard_map/ppermute | solution.py:241
  13.7 5.0 %collective-permute-start.3 = (bf16[128,512]{1,0:T(8,128)(2,1)S(1)}, bf16[128,512]{1,0:T(8,128)(2,1)S(1)}, u32[]{:S(2)}, u32[]{:S(2)}) collective-permute-start(bf16[128,512]{1,0:T(8,128)(2,1)S(1)} %shard_map.75.refs_0_), channel_id=1, source_target_pairs={{0,1},{1,0},{2,3},{3,2},{4,5},{5,4},{6,7},{7,6},{8,10},{9,11},{10,... | collective-permute-start | bytes 393224 | tf_op jit(solution)/shard_map/ppermute | solution.py:241
  16.2 3.8 %copy-start = (s32[4]{0:T(128)S(1)}, s32[4]{0:T(128)}, u32[]{:S(2)}) copy-start(s32[4]{0:T(128)} %refs_0_.3) | copy-start | bytes 52
  17.0 1.7 %collective-permute-start.6 = (bf16[128,512]{1,0:T(8,128)(2,1)S(1)}, bf16[128,512]{1,0:T(8,128)(2,1)S(1)}, u32[]{:S(2)}, u32[]{:S(2)}) collective-permute-start(bf16[128,512]{1,0:T(8,128)(2,1)S(1)} %get-tuple-element.27.refs_0_), channel_id=1, source_target_pairs={{0,8},{1,9},{2,10},{3,11},{4,12},{5,13},{6,14},{7,15},{8,0},{9,1},... | collective-permute-start | bytes 393224 | tf_op jit(solution)/shard_map/ppermute | solution.py:246
  17.0 2.5 %collective-permute-start.9 = (bf16[128,512]{1,0:T(8,128)(2,1)S(1)}, bf16[128,512]{1,0:T(8,128)(2,1)S(1)}, u32[]{:S(2)}, u32[]{:S(2)}) collective-permute-start(bf16[128,512]{1,0:T(8,128)(2,1)S(1)} %collective-permute-done.5.refs_3_), channel_id=1, source_target_pairs={{0,8},{1,9},{2,10},{3,11},{4,12},{5,13},{6,14},{7,15},{8,0},{9,1},... | collective-permute-start | bytes 393224 | tf_op jit(solution)/shard_map/ppermute | solution.py:246
  18.1 1.4 %collective-permute-start.8 = (bf16[128,512]{1,0:T(8,128)(2,1)S(1)}, bf16[128,512]{1,0:T(8,128)(2,1)S(1)}, u32[]{:S(2)}, u32[]{:S(2)}) collective-permute-start(bf16[128,512]{1,0:T(8,128)(2,1)S(1)} %collective-permute-done.4.refs_2_), channel_id=1, source_target_pairs={{0,8},{1,9},{2,10},{3,11},{4,12},{5,13},{6,14},{7,15},{8,0},{9,1},... | collective-permute-start | bytes 393224 | tf_op jit(solution)/shard_map/ppermute | solution.py:246
  18.7 1.3 %collective-permute-start.7 = (bf16[128,512]{1,0:T(8,128)(2,1)S(1)}, bf16[128,512]{1,0:T(8,128)(2,1)S(1)}, u32[]{:S(2)}, u32[]{:S(2)}) collective-permute-start(bf16[128,512]{1,0:T(8,128)(2,1)S(1)} %collective-permute-done.3.refs_1_), channel_id=1, source_target_pairs={{0,8},{1,9},{2,10},{3,11},{4,12},{5,13},{6,14},{7,15},{8,0},{9,1},... | collective-permute-start | bytes 393224 | tf_op jit(solution)/shard_map/ppermute | solution.py:246
  20.6 4.9 %collective-permute-start.12 = (bf16[32,512]{1,0:T(8,128)(2,1)S(1)}, bf16[32,512]{1,0:T(8,128)(2,1)S(1)}, u32[]{:S(2)}, u32[]{:S(2)}) collective-permute-start(bf16[32,512]{1,0:T(8,128)(2,1)S(1)} %get-tuple-element.31.refs_0_), channel_id=1, source_target_pairs={{0,4},{1,5},{2,6},{3,7},{4,0},{5,1},{6,2},{7,3},{8,25},{9,24},{10,... | collective-permute-start | bytes 98312 | tf_op jit(solution)/shard_map/ppermute | solution.py:241
  21.9 5.7 %collective-permute-start.11 = (bf16[32,512]{1,0:T(8,128)(2,1)S(1)}, bf16[32,512]{1,0:T(8,128)(2,1)S(1)}, u32[]{:S(2)}, u32[]{:S(2)}) collective-permute-start(bf16[32,512]{1,0:T(8,128)(2,1)S(1)} %get-tuple-element.31.refs_0_), channel_id=1, source_target_pairs={{0,6},{1,7},{2,4},{3,5},{4,2},{5,3},{6,0},{7,1},{8,24},{9,25},{10,... | collective-permute-start | bytes 98312 | tf_op jit(solution)/shard_map/ppermute | solution.py:241
  22.9 4.7 %collective-permute-start.10 = (bf16[32,512]{1,0:T(8,128)(2,1)S(1)}, bf16[32,512]{1,0:T(8,128)(2,1)S(1)}, u32[]{:S(2)}, u32[]{:S(2)}) collective-permute-start(bf16[32,512]{1,0:T(8,128)(2,1)S(1)} %get-tuple-element.31.refs_0_), channel_id=1, source_target_pairs={{0,2},{1,3},{2,0},{3,1},{4,6},{5,7},{6,4},{7,5},{8,9},{9,8},{10,11... | collective-permute-start | bytes 98312 | tf_op jit(solution)/shard_map/ppermute | solution.py:241
  27.6 5.9 %collective-permute-start.15 = (bf16[128,512]{1,0:T(8,128)(2,1)S(1)}, bf16[128,512]{1,0:T(8,128)(2,1)S(1)}, u32[]{:S(2)}, u32[]{:S(2)}) collective-permute-start(bf16[128,512]{1,0:T(8,128)(2,1)S(1)} %shard_map.80.blocks_ref), channel_id=1, source_target_pairs={{0,17},{1,16},{2,19},{3,18},{4,21},{5,20},{6,23},{7,22},{8,12},{9,... | collective-permute-start | bytes 393224 | tf_op jit(solution)/shard_map/ppermute | solution.py:241
  29.4 5.0 %collective-permute-start.14 = (bf16[128,512]{1,0:T(8,128)(2,1)S(1)}, bf16[128,512]{1,0:T(8,128)(2,1)S(1)}, u32[]{:S(2)}, u32[]{:S(2)}) collective-permute-start(bf16[128,512]{1,0:T(8,128)(2,1)S(1)} %shard_map.80.blocks_ref), channel_id=1, source_target_pairs={{0,16},{1,17},{2,18},{3,19},{4,20},{5,21},{6,22},{7,23},{8,14},{9,... | collective-permute-start | bytes 393224 | tf_op jit(solution)/shard_map/ppermute | solution.py:241
  30.0 5.0 %collective-permute-start.13 = (bf16[128,512]{1,0:T(8,128)(2,1)S(1)}, bf16[128,512]{1,0:T(8,128)(2,1)S(1)}, u32[]{:S(2)}, u32[]{:S(2)}) collective-permute-start(bf16[128,512]{1,0:T(8,128)(2,1)S(1)} %shard_map.80.blocks_ref), channel_id=1, source_target_pairs={{0,1},{1,0},{2,3},{3,2},{4,5},{5,4},{6,7},{7,6},{8,10},{9,11},{10,... | collective-permute-start | bytes 393224 | tf_op jit(solution)/shard_map/ppermute | solution.py:241
  31.9 3.1 %collective-permute-start.16 = (bf16[128,512]{1,0:T(8,128)(2,1)S(1)}, bf16[128,512]{1,0:T(8,128)(2,1)S(1)}, u32[]{:S(2)}, u32[]{:S(2)}) collective-permute-start(bf16[128,512]{1,0:T(8,128)(2,1)S(1)} %get-tuple-element.33.refs_0_), channel_id=1, source_target_pairs={{0,8},{1,9},{2,10},{3,11},{4,12},{5,13},{6,14},{7,15},{8,0},{9,1},... | collective-permute-start | bytes 393224 | tf_op jit(solution)/shard_map/ppermute | solution.py:246
  33.5 2.2 %collective-permute-start.19 = (bf16[128,512]{1,0:T(8,128)(2,1)S(1)}, bf16[128,512]{1,0:T(8,128)(2,1)S(1)}, u32[]{:S(2)}, u32[]{:S(2)}) collective-permute-start(bf16[128,512]{1,0:T(8,128)(2,1)S(1)} %collective-permute-done.15.refs_3_), channel_id=1, source_target_pairs={{0,8},{1,9},{2,10},{3,11},{4,12},{5,13},{6,14},{7,15},{8,0},{9,1},... | collective-permute-start | bytes 393224 | tf_op jit(solution)/shard_map/ppermute | solution.py:246
  34.4 1.4 %collective-permute-start.18 = (bf16[128,512]{1,0:T(8,128)(2,1)S(1)}, bf16[128,512]{1,0:T(8,128)(2,1)S(1)}, u32[]{:S(2)}, u32[]{:S(2)}) collective-permute-start(bf16[128,512]{1,0:T(8,128)(2,1)S(1)} %collective-permute-done.14.refs_2_), channel_id=1, source_target_pairs={{0,8},{1,9},{2,10},{3,11},{4,12},{5,13},{6,14},{7,15},{8,0},{9,1},... | collective-permute-start | bytes 393224 | tf_op jit(solution)/shard_map/ppermute | solution.py:246
  34.9 1.3 %collective-permute-start.17 = (bf16[128,512]{1,0:T(8,128)(2,1)S(1)}, bf16[128,512]{1,0:T(8,128)(2,1)S(1)}, u32[]{:S(2)}, u32[]{:S(2)}) collective-permute-start(bf16[128,512]{1,0:T(8,128)(2,1)S(1)} %collective-permute-done.13.refs_1_), channel_id=1, source_target_pairs={{0,8},{1,9},{2,10},{3,11},{4,12},{5,13},{6,14},{7,15},{8,0},{9,1},... | collective-permute-start | bytes 393224 | tf_op jit(solution)/shard_map/ppermute | solution.py:246
